TPU v7x, 512 devices: a whole 4x8x8 slice. The times are simulated.
512 devices in a mesh: gx: 64 (over y, z_lo, core), gy: 8 (over x, z_hi).
Axes of the slice: x: 4, y: 8, z: 8 (z_hi: 2, z_lo: 4; z = z_hi * 4 + z_lo), core: 2. Of those that a mesh axis runs over, the one named last changes fastest.
Arguments:
- populations: float32 [19, 768, 3072], P(None, 'gx', 'gy'), may hold values from 0.02 to 0.1
- phase_field: float32 [768, 3072], P('gx', 'gy'), may hold values from -1 to 1
- plane_shifts: int32 [4, 16], replicated, may hold values from 0 to 127
Outputs:
- populations_out: float32 [19, 768, 3072], P(None, 'gx', 'gy')
- phase_out: float32 [768, 3072], P('gx', 'gy')
All inputs are finite; a program needn't handle non-finite values.
Results may differ from a plain program's by a relative error of at most 0.0001.
Values sent between devices are 32-bit elements; how exact they have to be, the bound alone decides.
A program may use at most 64 MiB of HBM per device.

v0:
```python
import jax
import jax.numpy as jnp
from jax import lax
from jax.sharding import PartitionSpec as P

PLANES = 16
STEPS = 4
NZ = 24


lattice_vel = (
    (0, 0, 0),
    (1, 0, 0),
    (-1, 0, 0),
    (0, 1, 0),
    (0, -1, 0),
    (0, 0, 1),
    (0, 0, -1),
    (1, 1, 0),
    (-1, -1, 0),
    (1, -1, 0),
    (-1, 1, 0),
    (1, 0, 1),
    (-1, 0, -1),
    (1, 0, -1),
    (-1, 0, 1),
    (0, 1, 1),
    (0, -1, -1),
    (0, 1, -1),
    (0, -1, 1),
)
weights = (1.0 / 3.0,) + (1.0 / 18.0,) * 6 + (1.0 / 36.0,) * 12
all_slots = tuple(range(19))
relax_rate = 0.8
coupling = 0.01
bulk_coeff = 0.5
stiffness = 0.5
mobility = 0.02
far_weight = 0.25


def passed_along(value, axis, steps):
    count = lax.axis_size(axis)
    pairs = [(source, (source + steps) % count) for source in range(count)]
    return lax.ppermute(value, axis, pairs)


def extended_2(cells, sides, width):
    for axis, dim in sides:
        count = lax.axis_size(axis)
        head = lax.slice_in_dim(cells, 0, width, axis=dim)
        tail = lax.slice_in_dim(cells, cells.shape[dim] - width, cells.shape[dim], axis=dim)
        cells = jnp.concatenate(
            [
                lax.ppermute(tail, axis, [(i, (i + 1) % count) for i in range(count)]),
                cells,
                lax.ppermute(head, axis, [((i + 1) % count, i) for i in range(count)]),
            ],
            axis=dim,
        )
    return cells


def roll_cells(field, shift, depth):
    position = lax.broadcasted_iota(jnp.int32, (field.shape[-1],), 0) % depth
    if shift == 1:
        return jnp.where(position == 0, jnp.roll(field, 1 - depth, -1), jnp.roll(field, 1, -1))
    if shift == -1:
        return jnp.where(
            position == depth - 1, jnp.roll(field, depth - 1, -1), jnp.roll(field, -1, -1)
        )
    return field


def laplace(extended, depth):
    core = extended[1:-1, depth:-depth]
    total = extended[2:, depth:-depth] + extended[:-2, depth:-depth]
    total = total + extended[1:-1, 2 * depth :] + extended[1:-1, : -2 * depth]
    return total + roll_cells(core, 1, depth) + roll_cells(core, -1, depth) - 6.0 * core


def gradient(extended, depth):
    core = extended[1:-1, depth:-depth]
    along_x = 0.5 * (extended[2:, depth:-depth] - extended[:-2, depth:-depth])
    along_y = 0.5 * (extended[1:-1, 2 * depth :] - extended[1:-1, : -2 * depth])
    along_z = 0.5 * (roll_cells(core, -1, depth) - roll_cells(core, 1, depth))
    return (along_x, along_y, along_z)


def update_cells(current, phase_ext, depth):
    inner = phase_ext[1:-1, depth:-depth]
    chem_pot = bulk_coeff * (inner * inner * inner - inner) - stiffness * laplace(phase_ext, depth)
    phase_core = phase_ext[2:-2, 2 * depth : -2 * depth]
    push = gradient(chem_pot, depth)
    slope = gradient(inner, depth)
    density = jnp.sum(current, axis=0)
    flow = []
    for axis in range(3):
        total = jnp.zeros_like(density)
        for slot in range(19):
            if lattice_vel[slot][axis] != 0:
                total = total + lattice_vel[slot][axis] * current[slot]
        flow.append(total / density)
    drift = [
        flow[axis] - coupling * phase_core * push[axis] / (relax_rate * density)
        for axis in range(3)
    ]
    speed_sq = drift[0] * drift[0] + drift[1] * drift[1] + drift[2] * drift[2]
    post = []
    for slot in range(19):
        along = jnp.zeros_like(density)
        for axis in range(3):
            if lattice_vel[slot][axis] != 0:
                along = along + lattice_vel[slot][axis] * drift[axis]
        balance = (
            weights[slot] * density * (1.0 + 3.0 * along + 4.5 * along * along - 1.5 * speed_sq)
        )
        post.append(current[slot] + relax_rate * (balance - current[slot]))
    advect = flow[0] * slope[0] + flow[1] * slope[1] + flow[2] * slope[2]
    phase_next = phase_core - advect + mobility * laplace(chem_pot, depth)
    return (jnp.stack(post), phase_next)


def stream_cells(post, from_left, from_right, beside, depth):
    rows = post.shape[2] // depth
    outputs = []
    for slot in range(19):
        step_x, step_y, step_z = lattice_vel[slot]
        low = (1 - step_y) * depth
        high = (1 - step_y + rows) * depth
        if step_y == 0:
            middle = post[slot]
        else:
            middle = beside[slot][:, low:high]
        if step_x == 1:
            middle = jnp.concatenate([from_left[slot][:, low:high], middle[:-1]], 0)
        elif step_x == -1:
            middle = jnp.concatenate([middle[1:], from_right[slot][:, low:high]], 0)
        outputs.append(roll_cells(middle, step_z, depth))
    return jnp.stack(outputs)


def send_along(strip, shift):
    return passed_along(strip, "gx", shift)


def block_rim(field, width):
    return extended_2(field, (("gy", 2),), width)


def plane_windows(strips, lows, near, far, margin, depth):
    block_rows = strips.shape[3] // depth
    rows_total = lax.axis_size("gy") * block_rows
    width = (block_rows + 2 * margin + 1) * depth
    first_row = lax.axis_index("gy") * block_rows
    entry = lax.broadcasted_iota(jnp.int32, (2, width), 1)
    source_row = (first_row - margin - 1 - lows[:, None] + entry // depth) % rows_total
    source = source_row * depth + entry % depth
    whole = lax.all_gather(strips, "gy", axis=3, tiled=True)
    local = source - 0
    inside = (local >= 0) & (local < whole.shape[3])
    clipped = jnp.clip(local, 0, whole.shape[3] - 1)
    picked = jnp.stack([jnp.take(whole[side], clipped[side], axis=2) for side in range(2)])
    gathered = jnp.where(inside[:, None, None, :], picked, 0.0)
    return (
        near[:, None, None, None] * gathered[..., depth:]
        + far[:, None, None, None] * gathered[..., :-depth]
    )


def on_device(populations, phase_field, plane_shifts):
    depth = NZ
    per_segment = lax.axis_size("gx") // PLANES
    index = lax.axis_index("gx")
    left_plane = index % per_segment == 0
    right_plane = (index + 1) % per_segment == 0
    left_slot = (index // per_segment + PLANES - 1) % PLANES
    right_slot = jnp.clip((index + 1) // per_segment - 1, 0, PLANES - 1)
    near = jnp.stack(
        [
            jnp.where(left_plane, jnp.float32(1.0 - far_weight), jnp.float32(1.0)),
            jnp.where(right_plane, jnp.float32(far_weight), jnp.float32(1.0)),
        ]
    )
    far = jnp.stack(
        [
            jnp.where(left_plane, jnp.float32(far_weight), jnp.float32(0.0)),
            jnp.where(right_plane, jnp.float32(1.0 - far_weight), jnp.float32(0.0)),
        ]
    )
    toward, backward, sideways = (all_slots, all_slots, all_slots)
    current = populations
    phase = phase_field
    for step in range(STEPS):
        lows = jnp.stack(
            [
                jnp.where(left_plane, plane_shifts[step, left_slot], 0),
                jnp.where(right_plane, -plane_shifts[step, right_slot] - 1, 0),
            ]
        )
        strips = jnp.stack([send_along(phase[None, -2:], 1), send_along(phase[None, :2], -1)])
        windows = plane_windows(strips, lows, near, far, 2, depth)
        beside = block_rim(phase[None], 2 * depth)
        phase_ext = jnp.concatenate([windows[0, 0], beside[0], windows[1, 0]], 0)
        post, phase = update_cells(current, phase_ext, depth)
        upward = jnp.stack([post[slot, -1:] for slot in toward])
        downward = jnp.stack([post[slot, :1] for slot in backward])
        strips = jnp.stack([send_along(upward, 1), send_along(downward, -1)])
        windows = plane_windows(strips, lows, near, far, 1, depth)
        rims = block_rim(jnp.stack([post[slot] for slot in sideways]), depth)
        from_left = {slot: windows[0, place] for place, slot in enumerate(toward)}
        from_right = {slot: windows[1, place] for place, slot in enumerate(backward)}
        beside_rows = {slot: rims[place] for place, slot in enumerate(sideways)}
        current = stream_cells(post, from_left, from_right, beside_rows, depth)
    return (current, phase)


def solution(mesh):
    return jax.shard_map(
        on_device,
        mesh=mesh,
        in_specs=(P(None, "gx", "gy"), P("gx", "gy"), P()),
        out_specs=(P(None, "gx", "gy"), P("gx", "gy")),
        check_vma=False,
    )
```

profile of v0, /device:TPU:84, one launch (start us, length us, event | category | flops | bytes accessed | tf_op | source)
XLA Modules:
  0.0 1357.7 jit_solution(8118939983091516566)
XLA Ops:
  3.3 3.6 collective-permute-start.3
  7.8 10.0 collective-permute-start
  39.4 3.4 fusion.720
  52.7 126.7 %all_gather.24 = f32[2,1,2,3072]{2,3,1,0:T(8,128)S(1)} all-gather(f32[2,1,2,384]{2,3,1,0:T(8,128)S(1)} %copy.3094), channel_id=1, replica_groups=mesh['gx'=64,'gy'=8] {'gy'}, dimensions={3}, use_global_device_ids=true | all-gather | bytes 55296 | tf_op jit(solution)/shard_map/all_gather | solution.py:159
  196.4 3.6 collective-permute-start.5
  200.0 3.3 collective-permute-start.8
  203.3 7.4 collective-permute-start.9
  213.8 4.1 collective-permute-start.10
  222.8 7.8 collective-permute-start.7
  230.8 117.8 %all_gather.26 = f32[2,1,2,3072]{2,3,1,0:T(8,128)S(1)} all-gather(f32[2,1,2,384]{2,3,1,0:T(8,128)S(1)} %copy.3112), channel_id=1, replica_groups=mesh['gx'=64,'gy'=8] {'gy'}, dimensions={3}, use_global_device_ids=true | all-gather | bytes 55296 | tf_op jit(solution)/shard_map/all_gather | solution.py:159
  350.1 2.6 gather_fusion.4
  371.0 110.7 %all_gather.25 = f32[2,19,1,3072]{1,3,2,0:T(8,128)S(1)} all-gather(f32[2,19,1,384]{1,3,2,0:T(8,128)S(1)} %pad_maximum_fusion), channel_id=1, replica_groups=mesh['gx'=64,'gy'=8] {'gy'}, dimensions={3}, use_global_device_ids=true | all-gather | bytes 525312 | tf_op jit(solution)/shard_map/all_gather | solution.py:159
  506.3 25.2 %collective-permute-start.12 = (f32[19,1,384]{2,1,0:T(1,128)}, f32[19,1,384]{2,1,0:T(1,128)}, u32[]{:S(2)}, u32[]{:S(2)}) collective-permute-start(f32[19,1,384]{2,1,0:T(1,128)} %get-tuple-element.527), channel_id=1, source_target_pairs={{0,8},{8,16},{16,24},{24,32},{32,40},{40,48},{48,56},{56,64},{64,7... | collective-permute-start | bytes 87560 | tf_op jit(solution)/shard_map/ppermute | solution.py:45
  535.4 8.7 collective-permute-start.17
  546.8 5.9 collective-permute-start.18
  552.7 6.1 collective-permute-start.19
  561.7 6.1 collective-permute-start.15
  568.0 124.8 %all_gather.28 = f32[2,1,2,3072]{2,3,1,0:T(8,128)S(1)} all-gather(f32[2,1,2,384]{2,3,1,0:T(8,128)S(1)} %copy.3143), channel_id=1, replica_groups=mesh['gx'=64,'gy'=8] {'gy'}, dimensions={3}, use_global_device_ids=true | all-gather | bytes 55296 | tf_op jit(solution)/shard_map/all_gather | solution.py:159
  694.2 2.6 gather_fusion.8
  704.5 125.7 %all_gather.27 = f32[2,19,1,3072]{1,3,2,0:T(8,128)S(1)} all-gather(f32[2,19,1,384]{1,3,2,0:T(8,128)S(1)} %pad_maximum_fusion.1), channel_id=1, replica_groups=mesh['gx'=64,'gy'=8] {'gy'}, dimensions={3}, use_global_device_ids=true | all-gather | bytes 525312 | tf_op jit(solution)/shard_map/all_gather | solution.py:159
  854.9 3.6 collective-permute-start.21
  858.6 7.8 collective-permute-start.24
  866.4 3.3 collective-permute-start.25
  870.4 6.4 collective-permute-start.22
  878.8 3.6 collective-permute-start.27
  885.3 4.2 collective-permute-start.23
  889.8 130.1 %all_gather.30 = f32[2,1,2,3072]{2,3,1,0:T(8,128)S(1)} all-gather(f32[2,1,2,384]{2,3,1,0:T(8,128)S(1)} %copy.3174), channel_id=1, replica_groups=mesh['gx'=64,'gy'=8] {'gy'}, dimensions={3}, use_global_device_ids=true | all-gather | bytes 55296 | tf_op jit(solution)/shard_map/all_gather | solution.py:159
  1021.3 2.6 gather_fusion.12
  1035.8 123.8 %all_gather.29 = f32[2,19,1,3072]{1,3,2,0:T(8,128)S(1)} all-gather(f32[2,19,1,384]{1,3,2,0:T(8,128)S(1)} %pad_maximum_fusion.2), channel_id=1, replica_groups=mesh['gx'=64,'gy'=8] {'gy'}, dimensions={3}, use_global_device_ids=true | all-gather | bytes 525312 | tf_op jit(solution)/shard_map/all_gather | solution.py:159
  1175.5 8.7 collective-permute-start.31
  1190.5 5.3 collective-permute-done.31
  1212.4 132.9 %all_gather.31 = f32[2,19,1,3072]{1,3,2,0:T(8,128)S(1)} all-gather(f32[2,19,1,384]{1,3,2,0:T(8,128)S(1)} %pad_maximum_fusion.3), channel_id=1, replica_groups=mesh['gx'=64,'gy'=8] {'gy'}, dimensions={3}, use_global_device_ids=true | all-gather | bytes 525312 | tf_op jit(solution)/shard_map/all_gather | solution.py:159
  (1108 shorter events, 208.3 us)
Async XLA Ops:
  1.4 51.1 %collective-permute-start.2 = (f32[1,2,384]{2,1,0:T(2,128)S(1)}, f32[1,2,384]{2,1,0:T(2,128)S(1)}, u32[]{:S(2)}, u32[]{:S(2)}) collective-permute-start(f32[1,2,384]{2,1,0:T(2,128)S(1)} %get-tuple-element.611), channel_id=1, source_target_pairs={{0,8},{8,16},{16,24},{24,32},{32,40},{40,48},{48,56},{56,64},{64,7... | collective-permute-start | bytes 9224 | tf_op jit(solution)/shard_map/ppermute | solution.py:45
  3.3 49.2 %collective-permute-start.3 = (f32[1,2,384]{2,1,0:T(2,128)S(1)}, f32[1,2,384]{2,1,0:T(2,128)S(1)}, u32[]{:S(2)}, u32[]{:S(2)}) collective-permute-start(f32[1,2,384]{2,1,0:T(2,128)S(1)} %get-tuple-element.612), channel_id=1, source_target_pairs={{0,504},{8,0},{16,8},{24,16},{32,24},{40,32},{48,40},{56,48},{64,5... | collective-permute-start | bytes 9224 | tf_op jit(solution)/shard_map/ppermute | solution.py:45
  7.8 41.7 %collective-permute-start = (f32[1,12,48]{2,0,1:T(1,128)S(1)}, f32[1,12,48]{2,0,1:T(1,128)S(1)}, u32[]{:S(2)}, u32[]{:S(2)}) collective-permute-start(f32[1,12,48]{2,0,1:T(1,128)S(1)} %get-tuple-element.613), channel_id=1, source_target_pairs={{0,1},{1,2},{2,3},{3,4},{4,5},{5,6},{6,7},{7,0},{8,9},{9,10},{10,1... | collective-permute-start | bytes 6920 | tf_op jit(solution)/shard_map/ppermute | solution.py:55
  17.8 31.7 %collective-permute-start.1 = (f32[1,12,48]{2,0,1:T(1,128)S(1)}, f32[1,12,48]{2,0,1:T(1,128)S(1)}, u32[]{:S(2)}, u32[]{:S(2)}) collective-permute-start(f32[1,12,48]{2,0,1:T(1,128)S(1)} %get-tuple-element.614), channel_id=1, source_target_pairs={{1,0},{2,1},{3,2},{4,3},{5,4},{6,5},{7,6},{0,7},{9,8},{10,9},{11,1... | collective-permute-start | bytes 6920 | tf_op jit(solution)/shard_map/ppermute | solution.py:57
  193.6 176.4 %collective-permute-start.4 = (f32[19,1,384]{0,2,1:T(8,128)S(1)}, f32[19,1,384]{0,2,1:T(8,128)}, u32[]{:S(2)}, u32[]{:S(2)}) collective-permute-start(f32[19,1,384]{0,2,1:T(8,128)S(1)} %copy.3105), channel_id=1, source_target_pairs={{0,8},{8,16},{16,24},{24,32},{32,40},{40,48},{48,56},{56,64},{64,7... | collective-permute-start | bytes 87560 | tf_op jit(solution)/shard_map/ppermute | solution.py:45
  196.4 173.6 %collective-permute-start.5 = (f32[19,1,384]{0,2,1:T(8,128)}, f32[19,1,384]{0,2,1:T(8,128)}, u32[]{:S(2)}, u32[]{:S(2)}) collective-permute-start(f32[19,1,384]{0,2,1:T(8,128)} %copy.3106), channel_id=1, source_target_pairs={{0,504},{8,0},{16,8},{24,16},{32,24},{40,32},{48,40},{56,48},{64,5... | collective-permute-start | bytes 87560 | tf_op jit(solution)/shard_map/ppermute | solution.py:45
  200.0 13.8 %collective-permute-start.8 = (f32[1,12,48]{2,1,0:T(8,128)S(1)}, f32[1,12,48]{2,1,0:T(8,128)S(1)}, u32[]{:S(2)}, u32[]{:S(2)}) collective-permute-start(f32[1,12,48]{2,1,0:T(8,128)S(1)} %get-tuple-element.607), channel_id=1, source_target_pairs={{0,1},{1,2},{2,3},{3,4},{4,5},{5,6},{6,7},{7,0},{8,9},{9,10},{10,1... | collective-permute-start | bytes 6920 | tf_op jit(solution)/shard_map/ppermute | solution.py:55
  203.3 14.7 %collective-permute-start.9 = (f32[1,12,48]{2,1,0:T(8,128)S(1)}, f32[1,12,48]{2,1,0:T(8,128)S(1)}, u32[]{:S(2)}, u32[]{:S(2)}) collective-permute-start(f32[1,12,48]{2,1,0:T(8,128)S(1)} %get-tuple-element.608), channel_id=1, source_target_pairs={{1,0},{2,1},{3,2},{4,3},{5,4},{6,5},{7,6},{0,7},{9,8},{10,9},{11,1... | collective-permute-start | bytes 6920 | tf_op jit(solution)/shard_map/ppermute | solution.py:57
  211.5 145.1 %collective-permute-start.6 = (f32[19,12,24]{2,1,0:T(8,128)}, f32[19,12,24]{2,1,0:T(8,128)S(1)}, u32[]{:S(2)}, u32[]{:S(2)}) collective-permute-start(f32[19,12,24]{2,1,0:T(8,128)} %get-tuple-element.218), channel_id=1, source_target_pairs={{0,1},{1,2},{2,3},{3,4},{4,5},{5,6},{6,7},{7,0},{8,9},{9,10},{10,1... | collective-permute-start | bytes 65672 | tf_op jit(solution)/shard_map/ppermute | solution.py:55
  213.8 9.0 collective-permute-start.10
  218.0 12.7 collective-permute-start.11
  222.8 133.8 %collective-permute-start.7 = (f32[19,12,24]{2,1,0:T(8,128)}, f32[19,12,24]{2,1,0:T(8,128)S(1)}, u32[]{:S(2)}, u32[]{:S(2)}) collective-permute-start(f32[19,12,24]{2,1,0:T(8,128)} %get-tuple-element.219), channel_id=1, source_target_pairs={{1,0},{2,1},{3,2},{4,3},{5,4},{6,5},{7,6},{0,7},{9,8},{10,9},{11,1... | collective-permute-start | bytes 65672 | tf_op jit(solution)/shard_map/ppermute | solution.py:57
  506.3 196.4 %collective-permute-start.12 = (f32[19,1,384]{2,1,0:T(1,128)}, f32[19,1,384]{2,1,0:T(1,128)}, u32[]{:S(2)}, u32[]{:S(2)}) collective-permute-start(f32[19,1,384]{2,1,0:T(1,128)} %get-tuple-element.527), channel_id=1, source_target_pairs={{0,8},{8,16},{16,24},{24,32},{32,40},{40,48},{48,56},{56,64},{64,7... | collective-permute-start | bytes 87560 | tf_op jit(solution)/shard_map/ppermute | solution.py:45
  531.6 172.0 %collective-permute-start.13 = (f32[19,1,384]{2,1,0:T(1,128)}, f32[19,1,384]{2,1,0:T(1,128)}, u32[]{:S(2)}, u32[]{:S(2)}) collective-permute-start(f32[19,1,384]{2,1,0:T(1,128)} %get-tuple-element.528), channel_id=1, source_target_pairs={{0,504},{8,0},{16,8},{24,16},{32,24},{40,32},{48,40},{56,48},{64,5... | collective-permute-start | bytes 87560 | tf_op jit(solution)/shard_map/ppermute | solution.py:45
  533.5 13.3 collective-permute-start.16
  535.4 17.3 %collective-permute-start.17 = (f32[1,12,48]{2,1,0:T(8,128)S(1)}, f32[1,12,48]{2,1,0:T(8,128)S(1)}, u32[]{:S(2)}, u32[]{:S(2)}) collective-permute-start(f32[1,12,48]{2,1,0:T(8,128)S(1)} %get-tuple-element.566), channel_id=1, source_target_pairs={{1,0},{2,1},{3,2},{4,3},{5,4},{6,5},{7,6},{0,7},{9,8},{10,9},{11,1... | collective-permute-start | bytes 6920 | tf_op jit(solution)/shard_map/ppermute | solution.py:57
  544.9 155.9 %collective-permute-start.14 = (f32[19,12,24]{2,0,1:T(8,128)S(1)}, f32[19,12,24]{2,0,1:T(8,128)S(1)}, u32[]{:S(2)}, u32[]{:S(2)}) collective-permute-start(f32[19,12,24]{2,0,1:T(8,128)S(1)} %get-tuple-element.224), channel_id=1, source_target_pairs={{0,1},{1,2},{2,3},{3,4},{4,5},{5,6},{6,7},{7,0},{8,9},{9,10},{10,1... | collective-permute-start | bytes 65672 | tf_op jit(solution)/shard_map/ppermute | solution.py:55
  546.8 14.9 %collective-permute-start.18 = (f32[1,2,384]{2,1,0:T(2,128)S(1)}, f32[1,2,384]{2,1,0:T(2,128)S(1)}, u32[]{:S(2)}, u32[]{:S(2)}) collective-permute-start(f32[1,2,384]{2,1,0:T(2,128)S(1)} %get-tuple-element.567), channel_id=1, source_target_pairs={{0,8},{8,16},{16,24},{24,32},{32,40},{40,48},{48,56},{56,64},{64,7... | collective-permute-start | bytes 9224 | tf_op jit(solution)/shard_map/ppermute | solution.py:45
  552.7 15.1 %collective-permute-start.19 = (f32[1,2,384]{2,1,0:T(2,128)S(1)}, f32[1,2,384]{2,1,0:T(2,128)S(1)}, u32[]{:S(2)}, u32[]{:S(2)}) collective-permute-start(f32[1,2,384]{2,1,0:T(2,128)S(1)} %get-tuple-element.568), channel_id=1, source_target_pairs={{0,504},{8,0},{16,8},{24,16},{32,24},{40,32},{48,40},{56,48},{64,5... | collective-permute-start | bytes 9224 | tf_op jit(solution)/shard_map/ppermute | solution.py:45
  561.7 139.0 %collective-permute-start.15 = (f32[19,12,24]{2,0,1:T(8,128)S(1)}, f32[19,12,24]{2,0,1:T(8,128)S(1)}, u32[]{:S(2)}, u32[]{:S(2)}) collective-permute-start(f32[19,12,24]{2,0,1:T(8,128)S(1)} %get-tuple-element.225), channel_id=1, source_target_pairs={{1,0},{2,1},{3,2},{4,3},{5,4},{6,5},{7,6},{0,7},{9,8},{10,9},{11,1... | collective-permute-start | bytes 65672 | tf_op jit(solution)/shard_map/ppermute | solution.py:57
  853.0 180.9 %collective-permute-start.20 = (f32[19,1,384]{2,1,0:T(1,128)}, f32[19,1,384]{2,1,0:T(1,128)}, u32[]{:S(2)}, u32[]{:S(2)}) collective-permute-start(f32[19,1,384]{2,1,0:T(1,128)} %get-tuple-element.485), channel_id=1, source_target_pairs={{0,8},{8,16},{16,24},{24,32},{32,40},{40,48},{48,56},{56,64},{64,7... | collective-permute-start | bytes 87560 | tf_op jit(solution)/shard_map/ppermute | solution.py:45
  854.9 179.9 %collective-permute-start.21 = (f32[19,1,384]{2,1,0:T(1,128)}, f32[19,1,384]{2,1,0:T(1,128)}, u32[]{:S(2)}, u32[]{:S(2)}) collective-permute-start(f32[19,1,384]{2,1,0:T(1,128)} %get-tuple-element.486), channel_id=1, source_target_pairs={{0,504},{8,0},{16,8},{24,16},{32,24},{40,32},{48,40},{56,48},{64,5... | collective-permute-start | bytes 87560 | tf_op jit(solution)/shard_map/ppermute | solution.py:45
  858.6 18.2 %collective-permute-start.24 = (f32[1,12,48]{2,1,0:T(8,128)S(1)}, f32[1,12,48]{2,1,0:T(8,128)S(1)}, u32[]{:S(2)}, u32[]{:S(2)}) collective-permute-start(f32[1,12,48]{2,1,0:T(8,128)S(1)} %get-tuple-element.523), channel_id=1, source_target_pairs={{0,1},{1,2},{2,3},{3,4},{4,5},{5,6},{6,7},{7,0},{8,9},{9,10},{10,1... | collective-permute-start | bytes 6920 | tf_op jit(solution)/shard_map/ppermute | solution.py:55
  866.4 12.4 collective-permute-start.25
  870.4 156.8 %collective-permute-start.22 = (f32[19,12,24]{2,0,1:T(8,128)S(1)}, f32[19,12,24]{2,0,1:T(8,128)S(1)}, u32[]{:S(2)}, u32[]{:S(2)}) collective-permute-start(f32[19,12,24]{2,0,1:T(8,128)S(1)} %get-tuple-element.222), channel_id=1, source_target_pairs={{0,1},{1,2},{2,3},{3,4},{4,5},{5,6},{6,7},{7,0},{8,9},{9,10},{10,1... | collective-permute-start | bytes 65672 | tf_op jit(solution)/shard_map/ppermute | solution.py:55
  876.8 8.5 collective-permute-start.26
  878.8 10.8 collective-permute-start.27
  885.3 141.9 %collective-permute-start.23 = (f32[19,12,24]{2,0,1:T(8,128)S(1)}, f32[19,12,24]{2,0,1:T(8,128)S(1)}, u32[]{:S(2)}, u32[]{:S(2)}) collective-permute-start(f32[19,12,24]{2,0,1:T(8,128)S(1)} %get-tuple-element.223), channel_id=1, source_target_pairs={{1,0},{2,1},{3,2},{4,3},{5,4},{6,5},{7,6},{0,7},{9,8},{10,9},{11,1... | collective-permute-start | bytes 65672 | tf_op jit(solution)/shard_map/ppermute | solution.py:57
  1170.7 41.5 %collective-permute-start.29 = (f32[19,1,384]{2,1,0:T(1,128)S(1)}, f32[19,1,384]{2,1,0:T(1,128)S(1)}, u32[]{:S(2)}, u32[]{:S(2)}) collective-permute-start(f32[19,1,384]{2,1,0:T(1,128)S(1)} %get-tuple-element.448), channel_id=1, source_target_pairs={{0,504},{8,0},{16,8},{24,16},{32,24},{40,32},{48,40},{56,48},{64,5... | collective-permute-start | bytes 87560 | tf_op jit(solution)/shard_map/ppermute | solution.py:45
  1173.6 16.9 %collective-permute-start.30 = (f32[19,12,24]{2,0,1:T(8,128)S(1)}, f32[19,12,24]{2,0,1:T(8,128)S(1)}, u32[]{:S(2)}, u32[]{:S(2)}) collective-permute-start(f32[19,12,24]{2,0,1:T(8,128)S(1)} %get-tuple-element.220), channel_id=1, source_target_pairs={{0,1},{1,2},{2,3},{3,4},{4,5},{5,6},{6,7},{7,0},{8,9},{9,10},{10,1... | collective-permute-start | bytes 65672 | tf_op jit(solution)/shard_map/ppermute | solution.py:55
  1175.5 20.3 %collective-permute-start.31 = (f32[19,12,24]{2,0,1:T(8,128)S(1)}, f32[19,12,24]{2,0,1:T(8,128)S(1)}, u32[]{:S(2)}, u32[]{:S(2)}) collective-permute-start(f32[19,12,24]{2,0,1:T(8,128)S(1)} %get-tuple-element.221), channel_id=1, source_target_pairs={{1,0},{2,1},{3,2},{4,3},{5,4},{6,5},{7,6},{0,7},{9,8},{10,9},{11,1... | collective-permute-start | bytes 65672 | tf_op jit(solution)/shard_map/ppermute | solution.py:57
  1186.1 26.0 %collective-permute-start.28 = (f32[19,1,384]{2,1,0:T(1,128)S(1)}, f32[19,1,384]{2,1,0:T(1,128)S(1)}, u32[]{:S(2)}, u32[]{:S(2)}) collective-permute-start(f32[19,1,384]{2,1,0:T(1,128)S(1)} %get-tuple-element.447), channel_id=1, source_target_pairs={{0,8},{8,16},{16,24},{24,32},{32,40},{40,48},{48,56},{56,64},{64,7... | collective-permute-start | bytes 87560 | tf_op jit(solution)/shard_map/ppermute | solution.py:45
  (161 other events, 1469.4 us)
where the time goes:
time: 1360 us
  blocking collectives  992 us (73%)
  starting transfers between devices  155 us (11%)
  local copies, waits for them, and re-layouts  143 us (11%)
  other arithmetic  47.9 us (4%)
    all_gather x8, blocking collectives, plane_windows(): whole = lax.all_gather(strips, 'gy', axis=3, tiled=True)  992 us
    ppermute x16, starting transfers between devices, passed_along(): return lax.ppermute(value, axis, pairs)  71.5 us
    ppermute x8, starting transfers between devices, extended_2(): lax.ppermute(head, axis, [((i + 1) % count, i) for i in range(count)])  48.2 us
    ppermute x8, starting transfers between devices, extended_2(): lax.ppermute(tail, axis, [(i, (i + 1) % count) for i in range(count)])  35.6 us
    gather x16, local copies, waits for them, and re-layouts, plane_windows(): jnp.take(whole[side], clipped[side], axis=2)  27.4 us
  transfers between devices with their start and end apart: 32, of which 2 were waited for; matrix products, arithmetic and copies ran while one was open for 8% of the time, Pallas kernels for 0%

commit v1 on v0

v1 whole, which is shorter than its diff:
```python
import functools

import jax
import jax.numpy as jnp
from jax import lax
from jax.experimental import pallas as pl
from jax.experimental.pallas import tpu as pltpu
from jax.sharding import PartitionSpec as P

STEPS = 4
NZ = 24
ROWS = 12
WIDE = 384
SPAN = 4
MESH = pl.DeviceIdType.MESH

lattice_vel = (
    (0, 0, 0),
    (1, 0, 0),
    (-1, 0, 0),
    (0, 1, 0),
    (0, -1, 0),
    (0, 0, 1),
    (0, 0, -1),
    (1, 1, 0),
    (-1, -1, 0),
    (1, -1, 0),
    (-1, 1, 0),
    (1, 0, 1),
    (-1, 0, -1),
    (1, 0, -1),
    (-1, 0, 1),
    (0, 1, 1),
    (0, -1, -1),
    (0, 1, -1),
    (0, -1, 1),
)
relax_rate = 0.8
coupling = 0.01
mobility = 0.02

up_slots = (1, 11, 13, 7, 9)
down_slots = (2, 12, 14, 10, 8)
plus_y = (3, 7, 10, 15, 17)
minus_y = (4, 8, 9, 16, 18)


def rolled(value, shift, axis):
    size = value.shape[axis]
    shift = shift % size
    return value if shift == 0 else pltpu.roll(value, shift, axis)


def moved_yz(value, step_y, step_z, place):
    if step_z == 0:
        return rolled(value, step_y * NZ, 1)
    edge = 0 if step_z == 1 else NZ - 1
    inner = rolled(value, step_y * NZ + step_z, 1)
    wrap = rolled(value, step_y * NZ + step_z - step_z * NZ, 1)
    return jnp.where(place == edge, wrap, inner)


def kernel(
    shifts, f_in, p_in, f_out, p_out,
    f, ext, from_x, from_y, from_corner, to_x, to_y, to_corner, ring, send_sem, recv_sem,
):
    count_x, count_y = lax.axis_size("gx"), lax.axis_size("gy")
    gx, gy = lax.axis_index("gx"), lax.axis_index("gy")
    above, below = lax.rem(gx + 1, count_x), lax.rem(gx + count_x - 1, count_x)
    front, back = lax.rem(gy + 1, count_y), lax.rem(gy + count_y - 1, count_y)
    planes = count_x // SPAN
    left_plane = lax.rem(gx, SPAN) == 0
    right_plane = lax.rem(gx, SPAN) == SPAN - 1
    left_slot = lax.rem(gx // SPAN + planes - 1, planes)
    right_slot = gx // SPAN
    blocks = 3 * count_y

    def signal(x, y):
        pl.semaphore_signal(barrier, inc=1, device_id=(x, y), device_id_type=MESH)

    barrier = pltpu.get_barrier_semaphore()
    signal(gx, front)
    signal(gx, back)
    for is_plane, side in ((left_plane, below), (right_plane, above)):
        @pl.when(is_plane)
        def _(side=side):
            for y in range(count_y):
                signal(side, y)

        @pl.when(jnp.logical_not(is_plane))
        def _(side=side):
            signal(side, gy)
            signal(side, front)
            signal(side, back)

    lane = lax.broadcasted_iota(jnp.int32, (16, WIDE), 1)
    place = lax.rem(lane, NZ)
    lane4 = lax.broadcasted_iota(jnp.int32, (16, 512), 1)
    place4 = lax.rem(jnp.where(lane4 < 448, lane4, lane4 - 464), NZ)
    lane1 = lax.broadcasted_iota(jnp.int32, (16, 128), 1)

    def pack_phase(r):
        for b in range(3):
            cut = slice(b * 128, b * 128 + 128)
            to_x[r, 0, b, 5:7, :] = ext[10:12, cut]
            to_x[r, 1, b, 5:7, :] = ext[0:2, cut]
        to_y[r, 0, 12:24, :] = ext[0:12, 256:384]
        to_y[r, 1, 12:24, :] = ext[0:12, 0:128]
        to_corner[r, 0, 1:2, :] = ext[11:12, 256:384]
        to_corner[r, 1, 1:2, :] = ext[11:12, 0:128]
        to_corner[r, 2, 1:2, :] = ext[0:1, 256:384]
        to_corner[r, 3, 1:2, :] = ext[0:1, 0:128]

    def remote(src, dst, r, kind, x, y):
        return pltpu.make_async_remote_copy(
            src_ref=src, dst_ref=dst, send_sem=send_sem.at[r, kind], recv_sem=recv_sem.at[r, kind],
            device_id=(x, y), device_id_type=MESH,
        )

    def send(r):
        for kind, is_plane, side in ((0, right_plane, above), (1, left_plane, below)):
            @pl.when(is_plane)
            def _(kind=kind, side=side):
                for y in range(count_y):
                    remote(to_x.at[r, kind], from_x.at[r, kind, pl.ds(gy * 3, 3)], r, kind, side, y).start()

            @pl.when(jnp.logical_not(is_plane))
            def _(kind=kind, side=side):
                for k, y in ((2 * kind, front), (2 * kind + 1, back)):
                    remote(to_corner.at[r, k], from_corner.at[r, k], r, 4 + k, side, y).start()
                remote(to_x.at[r, kind], from_x.at[r, kind, pl.ds(0, 3)], r, kind, side, gy).start()
        remote(to_y.at[r, 0], from_y.at[r, 0], r, 2, gx, front).start()
        remote(to_y.at[r, 1], from_y.at[r, 1], r, 3, gx, back).start()

    def wait_for(ref, sem):
        pltpu.make_async_copy(ref, ref, sem).wait()

    def wait_sent(r):
        for kind, is_plane in ((0, right_plane), (1, left_plane)):
            @pl.when(is_plane)
            def _(kind=kind):
                wait_for(from_x.at[r, kind], send_sem.at[r, kind])

            @pl.when(jnp.logical_not(is_plane))
            def _(kind=kind):
                for k in (2 * kind, 2 * kind + 1):
                    wait_for(to_corner.at[r, k], send_sem.at[r, 4 + k])
                wait_for(to_x.at[r, kind], send_sem.at[r, kind])
        for k in (0, 1):
            wait_for(to_y.at[r, k], send_sem.at[r, 2 + k])

    def close_ring(r, kind):
        for b in range(blocks + 4):
            ring[b] = from_x[r, kind, b % blocks]

    def view(kind, shift):
        low = shift if kind == 0 else -shift - 1
        near, far = (0.75, 0.25) if kind == 0 else (0.25, 0.75)
        start = ((gy * 16 - low - 3) & (16 * count_y - 1)) * NZ
        first, offset = start >> 7, start & 127
        window = jnp.concatenate([ring[first + i] for i in range(5)], axis=1)
        window = pltpu.roll(window, 640 - 3 * NZ - offset, 1)
        return near * window + far * rolled(window, NZ, 1)

    def receive(r, step):
        slots_of = (up_slots, down_slots)
        edges = (0, ROWS - 1)
        for k in (0, 1):
            wait_for(from_y.at[r, k], recv_sem.at[r, 2 + k])
        for k, slots in ((0, plus_y), (1, minus_y)):
            packed = from_y[r, k, 0:16]
            cut = slice(0, 128) if k == 0 else slice(256, 384)
            keep = lane1 < NZ if k == 0 else lane1 >= 128 - NZ
            for i, slot in enumerate(slots):
                part = rolled(packed, -i * NZ if k == 0 else i * NZ, 1)
                f[slot, :, cut] = jnp.where(keep, part, f[slot, :, cut])
        ext[0:12, 384:512] = jnp.where(lane1[:12] < 64, from_y[r, 1, 12:24], from_y[r, 0, 12:24])
        row = lax.broadcasted_iota(jnp.int32, (8, WIDE), 0)
        lane8 = lax.broadcasted_iota(jnp.int32, (8, WIDE), 1)
        for kind, is_plane, place_of in ((0, left_plane, left_slot), (1, right_plane, right_slot)):
            outer = 14 - 2 * kind
            near_row = 15 - 3 * kind

            @pl.when(is_plane)
            def _(kind=kind, place_of=place_of, outer=outer):
                wait_for(from_x.at[r, kind], recv_sem.at[r, kind])
                close_ring(r, kind)
                rows = lax.broadcasted_iota(jnp.int32, (8, 640), 0)
                strip = view(kind, shifts[step, place_of])
                strip = jnp.where(
                    rows == 3, rolled(strip, NZ, 1), jnp.where(rows == 4, rolled(strip, -NZ, 1), strip)
                )
                for i, slot in enumerate(slots_of[kind]):
                    f[slot, edges[kind]:edges[kind] + 1, :] = strip[i:i + 1, :WIDE]
                phase = view(kind, shifts[jnp.minimum(step + 1, STEPS - 1), place_of])
                ext[outer:outer + 2, 0:WIDE] = phase[5:7, 0:WIDE]
                ext[outer:outer + 2, WIDE:512] = jnp.where(
                    lane1[:2] < 64, phase[5:7, 384:512], phase[5:7, 512:640]
                )

            @pl.when(jnp.logical_not(is_plane))
            def _(kind=kind, outer=outer, near_row=near_row):
                for k in (2 * kind, 2 * kind + 1):
                    wait_for(from_corner.at[r, k], recv_sem.at[r, 4 + k])
                wait_for(from_x.at[r, kind, pl.ds(0, 3)], recv_sem.at[r, kind])
                strip = jnp.concatenate([from_x[r, kind, b] for b in range(3)], axis=1)
                first, last = from_corner[r, 2 * kind], from_corner[r, 2 * kind + 1]
                plus = rolled(strip, NZ, 1)
                minus = rolled(strip, -NZ, 1)
                for i in range(3):
                    slot = slots_of[kind][i]
                    f[slot, edges[kind]:edges[kind] + 1, :] = strip[i:i + 1]
                head = jnp.where(lane1[:1] < NZ, first[0:1], plus[3:4, 0:128])
                tail = jnp.where(lane1[:1] >= 128 - NZ, last[0:1], minus[4:5, 256:384])
                e = edges[kind]
                f[slots_of[kind][3], e:e + 1, 0:128] = head
                f[slots_of[kind][3], e:e + 1, 128:384] = plus[3:4, 128:384]
                f[slots_of[kind][4], e:e + 1, 0:256] = minus[4:5, 0:256]
                f[slots_of[kind][4], e:e + 1, 256:384] = tail
                ext[outer:outer + 2, 0:WIDE] = strip[5:7]
                ext[near_row:near_row + 1, WIDE:512] = jnp.where(lane1[:1] < 64, last[1:2], first[1:2])

    def advance(r):
        p = ext[...]
        px, mx = rolled(p, -1, 0), rolled(p, 1, 0)
        py, my = rolled(p, -NZ, 1), rolled(p, NZ, 1)
        pz, mz = moved_yz(p, 0, -1, place4), moved_yz(p, 0, 1, place4)
        chem = 0.5 * (p * p * p - p) - 0.5 * (px + mx + py + my + pz + mz - 6.0 * p)
        slope = [0.5 * (a - b)[:, :WIDE] for a, b in ((px, mx), (py, my), (pz, mz))]
        px, mx = rolled(chem, -1, 0)[:, :WIDE], rolled(chem, 1, 0)[:, :WIDE]
        py, my = rolled(chem, -NZ, 1)[:, :WIDE], rolled(chem, NZ, 1)[:, :WIDE]
        pz, mz = moved_yz(chem, 0, -1, place4)[:, :WIDE], moved_yz(chem, 0, 1, place4)[:, :WIDE]
        bend = px + mx + py + my + pz + mz - 6.0 * chem[:, :WIDE]
        own = p[:, :WIDE]
        density = f[0]
        for slot in range(1, 19):
            density = density + f[slot]
        inverse = 1.0 / density
        scaled = (-0.5 * coupling / relax_rate) * own
        next_phase = own + mobility * bend
        drift = []
        for axis, push in enumerate((px - mx, py - my, pz - mz)):
            total = None
            for slot in range(1, 19, 2):
                sign = lattice_vel[slot][axis]
                if sign != 0:
                    pair = f[slot] - f[slot + 1]
                    if total is None:
                        total = pair
                    else:
                        total = total + pair if sign == 1 else total - pair
            next_phase = next_phase - total * inverse * slope[axis]
            drift.append((total + scaled * push) * inverse)
        ext[0:12, 0:WIDE] = next_phase[:12]
        base = 1.0 - 1.5 * (drift[0] * drift[0] + drift[1] * drift[1] + drift[2] * drift[2])
        weight = relax_rate / 36.0 * density
        keep = 1.0 - relax_rate
        packs = {}

        def put(slot, post):
            step_x, step_y, step_z = lattice_vel[slot]
            value = rolled(post, step_x, 0)
            moved = moved_yz(value, step_y, step_z, place)
            f[slot] = moved
            if step_x != 0:
                kind = 0 if step_x == 1 else 1
                i = (up_slots, down_slots)[kind].index(slot)
                line = 12 if step_x == 1 else 15
                shown = value if step_y != 0 else moved
                for b in range(3):
                    to_x[r, kind, b, i:i + 1, :] = shown[line:line + 1, b * 128:b * 128 + 128]
                if step_y != 0:
                    k = 2 * kind + (0 if step_y == 1 else 1)
                    cut = slice(0, 128) if step_y == 1 else slice(256, 384)
                    to_corner[r, k, 0:1, :] = moved[line:line + 1, cut]
            if step_y == 1:
                i = plus_y.index(slot)
                part = rolled(moved[:, 0:128], i * NZ, 1)
                packs[0] = part if i == 0 else jnp.where(lane1 >= i * NZ, part, packs[0])
            if step_y == -1:
                i = minus_y.index(slot)
                part = rolled(moved[:, 256:384], -i * NZ, 1)
                packs[1] = part if i == 0 else jnp.where(lane1 < 128 - i * NZ, part, packs[1])

        put(0, keep * f[0] + 12.0 * weight * base)
        for slot in range(1, 19, 2):
            along = None
            for axis in range(3):
                sign = lattice_vel[slot][axis]
                if sign != 0:
                    if along is None:
                        along = drift[axis]
                    else:
                        along = along + drift[axis] if sign == 1 else along - drift[axis]
            scale = 2.0 * weight if slot < 7 else weight
            even = scale * (base + 4.5 * along * along)
            odd = scale * (3.0 * along)
            here, there = f[slot], f[slot + 1]
            put(slot, keep * here + (even + odd))
            put(slot + 1, keep * there + (even - odd))
        to_y[r, 0, 0:12, :] = packs[0][:12]
        to_y[r, 1, 0:12, :] = packs[1][:12]
        pack_phase(r)

    for slot in range(19):
        f[slot, 0:12, :] = f_in[slot]
        f[slot, 12:16, :] = jnp.ones((4, WIDE), jnp.float32)
    ext[...] = jnp.zeros_like(ext)
    ext[0:12, 0:WIDE] = p_in[...]
    pack_phase(0)
    pl.semaphore_wait(barrier, jnp.where(left_plane | right_plane, 5 + count_y, 8))
    send(0)
    for k in (0, 1):
        wait_for(from_y.at[0, k], recv_sem.at[0, 2 + k])
    ext[0:12, 384:512] = jnp.where(lane1[:12] < 64, from_y[0, 1, 12:24], from_y[0, 0, 12:24])
    for kind, is_plane, place_of in ((0, left_plane, left_slot), (1, right_plane, right_slot)):
        outer = 14 - 2 * kind
        near_row = 15 - 3 * kind

        @pl.when(is_plane)
        def _(kind=kind, place_of=place_of, outer=outer):
            wait_for(from_x.at[0, kind], recv_sem.at[0, kind])
            close_ring(0, kind)
            phase = view(kind, shifts[0, place_of])
            ext[outer:outer + 2, 0:WIDE] = phase[5:7, 0:WIDE]
            ext[outer:outer + 2, WIDE:512] = jnp.where(
                lane1[:2] < 64, phase[5:7, 384:512], phase[5:7, 512:640]
            )

        @pl.when(jnp.logical_not(is_plane))
        def _(kind=kind, outer=outer, near_row=near_row):
            for k in (2 * kind, 2 * kind + 1):
                wait_for(from_corner.at[0, k], recv_sem.at[0, 4 + k])
            wait_for(from_x.at[0, kind, pl.ds(0, 3)], recv_sem.at[0, kind])
            first, last = from_corner[0, 2 * kind], from_corner[0, 2 * kind + 1]
            for b in range(3):
                ext[outer:outer + 2, b * 128:b * 128 + 128] = from_x[0, kind, b, 5:7, :]
            ext[near_row:near_row + 1, WIDE:512] = jnp.where(lane1[:1] < 64, last[1:2], first[1:2])

    def body(step, carry):
        advance(step + 1)
        send(step + 1)
        wait_sent(step)
        receive(step + 1, step)
        return carry

    lax.fori_loop(0, STEPS, body, 0)
    for slot in range(19):
        f_out[slot] = f[slot, 0:12, :]
    p_out[...] = ext[0:12, 0:WIDE]
    wait_sent(STEPS)


def on_device(populations, phase_field, plane_shifts):
    blocks = 3 * lax.axis_size("gy")
    rounds = STEPS + 1
    vmem = pl.BlockSpec(memory_space=pltpu.VMEM)
    return pl.pallas_call(
        kernel,
        out_shape=(
            jax.ShapeDtypeStruct(populations.shape, jnp.float32),
            jax.ShapeDtypeStruct(phase_field.shape, jnp.float32),
        ),
        in_specs=[pl.BlockSpec(memory_space=pltpu.SMEM), vmem, vmem],
        out_specs=(vmem, vmem),
        scratch_shapes=[
            pltpu.VMEM((19, 16, WIDE), jnp.float32),
            pltpu.VMEM((16, 512), jnp.float32),
            pltpu.VMEM((rounds, 2, blocks, 8, 128), jnp.float32),
            pltpu.VMEM((rounds, 2, 24, 128), jnp.float32),
            pltpu.VMEM((rounds, 4, 8, 128), jnp.float32),
            pltpu.VMEM((rounds, 2, 3, 8, 128), jnp.float32),
            pltpu.VMEM((rounds, 2, 24, 128), jnp.float32),
            pltpu.VMEM((rounds, 4, 8, 128), jnp.float32),
            pltpu.VMEM((blocks + 4, 8, 128), jnp.float32),
            pltpu.SemaphoreType.DMA((rounds, 8)),
            pltpu.SemaphoreType.DMA((rounds, 8)),
        ],
        compiler_params=pltpu.CompilerParams(
            collective_id=0, has_side_effects=True, vmem_limit_bytes=32 * 1024 * 1024
        ),
    )(plane_shifts, populations, phase_field)


def solution(mesh):
    return jax.shard_map(
        on_device,
        mesh=mesh,
        in_specs=(P(None, "gx", "gy"), P("gx", "gy"), P()),
        out_specs=(P(None, "gx", "gy"), P("gx", "gy")),
        check_vma=False,
    )
```

time: 1360 us -> 54.3 us (0.04)
  the two profiles are of different devices: /device:TPU:84 before, /device:TPU:1 now
where the time goes in v1:
time: 54.3 us; the launch traced here: 54.2 us
  Pallas kernels  50.9 us (94%)
  local copies, waits for them, and re-layouts  2.6 us (5%)
  between operations  0.67 us (1%)
    pallas_call x1, Pallas kernels, on_device(): pl.pallas_call(kernel, out_shape=(jax.ShapeDtypeStruct(populations.shape,...  50.9 us
    unnamed x6, local copies, waits for them, and re-layouts  1.71 us

profile of v1, /device:TPU:1, one launch (start us, length us, event | category | flops | bytes accessed | tf_op | source)
XLA Modules:
  0.0 54.2 jit_solution(6170228759184543831)
XLA Ops:
  0.6 0.0 copy-start.1
  0.6 0.0 copy-start
  0.6 1.1 %copy.5.f_in = f32[19,12,384]{2,1,0:T(8,128)S(1)} copy(f32[19,12,384]{2,0,1:T(8,128)} %param.3) | data formatting | bytes 700416 | tf_op args[0]
  1.8 0.0 copy-done.1
  1.8 0.0 copy-done
  1.8 50.9 %shard_map.50 = (f32[19,12,384]{2,1,0:T(8,128)S(1)}, f32[12,384]{1,0:T(8,128)S(1)}) custom-call(s32[4,16]{1,0:T(4,128)S(1)} %copy-done.1, f32[19,12,384]{2,1,0:T(8,128)S(1)} %copy.5.f_in, f32[12,384]{1,0:T(8,128)S(1)} %copy-done), custom_call_target="tpu_custom_call" | custom-call | tf_op jit(solution)/shard_map/pallas_call | solution.py:358
  52.7 0.9 %copy.6 = f32[19,12,384]{2,0,1:T(8,128)} copy(f32[19,12,384]{2,1,0:T(8,128)S(1)} %get-tuple-element.2) | data formatting | bytes 700416 | tf_op jit(solution)/shard_map/pallas_call | solution.py:358
  53.6 0.6 %copy.8 = f32[12,384]{1,0:T(8,128)} copy(f32[12,384]{1,0:T(8,128)S(1)} %get-tuple-element.7) | data formatting | bytes 36864
Async XLA Ops:
  0.6 1.1 %copy-start.1 = (s32[4,16]{1,0:T(4,128)S(1)}, s32[4,16]{1,0:T(4,128)}, u32[]{:S(2)}) copy-start(s32[4,16]{1,0:T(4,128)} %shifts.1) | copy-start | bytes 772
  0.6 1.1 %copy-start = (f32[12,384]{1,0:T(8,128)S(1)}, f32[12,384]{1,0:T(8,128)}, u32[]{:S(2)}) copy-start(f32[12,384]{1,0:T(8,128)} %p_in.1) | copy-start | bytes 55300

commit v2 on v1

--- a/solution.py
+++ b/solution.py
@@ -60,9 +60,91 @@
     return jnp.where(place == edge, wrap, inner)
 
 
+def differences(value, place):
+    return (
+        (rolled(value, -1, 0), rolled(value, 1, 0)),
+        (rolled(value, -NZ, 1), rolled(value, NZ, 1)),
+        (moved_yz(value, 0, -1, place), moved_yz(value, 0, 1, place)),
+    )
+
+
+def bulk(p, around):
+    total = around[0][0] + around[0][1] + around[1][0] + around[1][1] + around[2][0] + around[2][1]
+    return 0.5 * (p * p * p - p) - 0.5 * (total - 6.0 * p)
+
+
+def bent(chem, around):
+    total = around[0][0] + around[0][1] + around[1][0] + around[1][1] + around[2][0] + around[2][1]
+    return total - 6.0 * chem
+
+
+def relaxed(here, weight, along, drift):
+    square = drift[0] * drift[0] + drift[1] * drift[1] + drift[2] * drift[2]
+    return (1.0 - relax_rate) * here + weight * (
+        1.0 - 1.5 * square + 3.0 * along + 4.5 * along * along
+    )
+
+
+def strip_post(kind, here, density, drift, place):
+    sign = 1.0 - 2.0 * kind
+    row = lax.broadcasted_iota(jnp.int32, here.shape, 0)
+    full = [jnp.broadcast_to(d, here.shape) for d in drift]
+    along = sign * full[0]
+    along = along + jnp.where(row == 3, full[1], jnp.where(row == 4, -full[1], 0.0))
+    along = along + jnp.where(row == 1, sign * full[2], jnp.where(row == 2, -sign * full[2], 0.0))
+    weight = jnp.where(row == 0, 2.0, 1.0) * (relax_rate / 36.0) * density
+    post = relaxed(here, weight, along, full)
+    first, second = (1, -1) if kind == 0 else (-1, 1)
+    return jnp.where(
+        row == 1, moved_yz(post, 0, first, place), jnp.where(row == 2, moved_yz(post, 0, second, place), post)
+    )
+
+
+def strip_moved(strip):
+    row = lax.broadcasted_iota(jnp.int32, strip.shape, 0)
+    return jnp.where(row == 3, rolled(strip, NZ, 1), jnp.where(row == 4, rolled(strip, -NZ, 1), strip))
+
+
+def packed_post(k, here, density, drift, lane1):
+    def spread(value):
+        out = rolled(value, NZ if k == 0 else 104, 1)
+        first = out
+        for i in range(1, 5):
+            if k == 0:
+                out = jnp.where(lane1 >= i * NZ, rolled(first, i * NZ, 1), out)
+            else:
+                out = jnp.where(lane1 < 128 - i * NZ, rolled(first, -i * NZ, 1), out)
+        return out
+
+    slots = plus_y if k == 0 else minus_y
+    group = lane1 // NZ if k == 0 else (127 - lane1) // NZ
+    density, drift = spread(density), [spread(d) for d in drift]
+
+    def chosen(axis, value):
+        out = jnp.zeros_like(value)
+        for i, slot in enumerate(slots):
+            if lattice_vel[slot][axis] != 0:
+                out = jnp.where(group == i, lattice_vel[slot][axis] * value, out)
+        return out
+
+    along = chosen(0, drift[0]) + chosen(1, drift[1]) + chosen(2, drift[2])
+    weight = jnp.where(group == 0, 2.0, 1.0) * (relax_rate / 36.0) * density
+    post = relaxed(here, weight, along, drift)
+    place = lax.rem(lane1, NZ) if k == 0 else lax.rem(lane1 + 16, NZ)
+    out = post
+    for i, slot in enumerate(slots):
+        step_x, _, step_z = lattice_vel[slot]
+        if step_x != 0 or step_z != 0:
+            out = jnp.where(group == i, moved_yz(rolled(post, step_x, 0), 0, step_z, place), out)
+    return out
+
+
 def kernel(
     shifts, f_in, p_in, f_out, p_out,
-    f, ext, from_x, from_y, from_corner, to_x, to_y, to_corner, ring, send_sem, recv_sem,
+    f, ext, from_x, from_y, from_corner, to_x, to_y, to_corner, ring,
+    e_p, e_r, e_u, ring_b, ring_a,
+    wide_x, wide_y, wide_corner, wide_a, out_x, out_y, out_corner, out_a,
+    send_sem, recv_sem,
 ):
     count_x, count_y = lax.axis_size("gx"), lax.axis_size("gy")
     gx, gy = lax.axis_index("gx"), lax.axis_index("gy")
@@ -79,8 +161,15 @@
         pl.semaphore_signal(barrier, inc=1, device_id=(x, y), device_id_type=MESH)
 
     barrier = pltpu.get_barrier_semaphore()
+    any_plane = left_plane | right_plane
     signal(gx, front)
     signal(gx, back)
+
+    @pl.when(any_plane)
+    def _():
+        for j in range(2, count_y - 1):
+            signal(gx, lax.rem(gy + j, count_y))
+
     for is_plane, side in ((left_plane, below), (right_plane, above)):
         @pl.when(is_plane)
         def _(side=side):
@@ -98,6 +187,9 @@
     lane4 = lax.broadcasted_iota(jnp.int32, (16, 512), 1)
     place4 = lax.rem(jnp.where(lane4 < 448, lane4, lane4 - 464), NZ)
     lane1 = lax.broadcasted_iota(jnp.int32, (16, 128), 1)
+    lane5 = lax.broadcasted_iota(jnp.int32, (24, 640), 1)
+    place5 = lax.rem(jnp.where(lane5 < 512, lane5, lane5 + 8), NZ)
+    place6 = lax.rem(lax.broadcasted_iota(jnp.int32, (8, 768), 1), NZ)
 
     def pack_phase(r):
         for b in range(3):
@@ -149,6 +241,15 @@
         for k in (0, 1):
             wait_for(to_y.at[r, k], send_sem.at[r, 2 + k])
 
+    def window_of(held, turn):
+        start = ((gy * 16 - turn - 4) & (16 * count_y - 1)) * NZ
+        first, offset = start >> 7, start & 127
+        window = jnp.concatenate([held[first + i] for i in range(6)], axis=1)
+        return pltpu.roll(window, 768 - 4 * NZ - offset, 1)
+
+    def view_b(kind, shift):
+        return window_of(ring_b, shift if kind == 0 else -shift - 1)
+
     def close_ring(r, kind):
         for b in range(blocks + 4):
             ring[b] = from_x[r, kind, b % blocks]
@@ -162,21 +263,26 @@
         window = pltpu.roll(window, 640 - 3 * NZ - offset, 1)
         return near * window + far * rolled(window, NZ, 1)
 
+    def patch_y(k, packed):
+        cut = slice(0, 128) if k == 0 else slice(256, 384)
+        keep = lane1 < NZ if k == 0 else lane1 >= 128 - NZ
+        for i, slot in enumerate(plus_y if k == 0 else minus_y):
+            part = rolled(packed, -i * NZ if k == 0 else i * NZ, 1)
+            f[slot, :, cut] = jnp.where(keep, part, f[slot, :, cut])
+
+    def patch_x(kind, strip):
+        edge = 0 if kind == 0 else ROWS - 1
+        for i, slot in enumerate(up_slots if kind == 0 else down_slots):
+            f[slot, edge:edge + 1, :] = strip[i:i + 1, :WIDE]
+
     def receive(r, step):
         slots_of = (up_slots, down_slots)
         edges = (0, ROWS - 1)
         for k in (0, 1):
             wait_for(from_y.at[r, k], recv_sem.at[r, 2 + k])
-        for k, slots in ((0, plus_y), (1, minus_y)):
-            packed = from_y[r, k, 0:16]
-            cut = slice(0, 128) if k == 0 else slice(256, 384)
-            keep = lane1 < NZ if k == 0 else lane1 >= 128 - NZ
-            for i, slot in enumerate(slots):
-                part = rolled(packed, -i * NZ if k == 0 else i * NZ, 1)
-                f[slot, :, cut] = jnp.where(keep, part, f[slot, :, cut])
+        for k in (0, 1):
+            patch_y(k, from_y[r, k, 0:16])
         ext[0:12, 384:512] = jnp.where(lane1[:12] < 64, from_y[r, 1, 12:24], from_y[r, 0, 12:24])
-        row = lax.broadcasted_iota(jnp.int32, (8, WIDE), 0)
-        lane8 = lax.broadcasted_iota(jnp.int32, (8, WIDE), 1)
         for kind, is_plane, place_of in ((0, left_plane, left_slot), (1, right_plane, right_slot)):
             outer = 14 - 2 * kind
             near_row = 15 - 3 * kind
@@ -185,13 +291,7 @@
             def _(kind=kind, place_of=place_of, outer=outer):
                 wait_for(from_x.at[r, kind], recv_sem.at[r, kind])
                 close_ring(r, kind)
-                rows = lax.broadcasted_iota(jnp.int32, (8, 640), 0)
-                strip = view(kind, shifts[step, place_of])
-                strip = jnp.where(
-                    rows == 3, rolled(strip, NZ, 1), jnp.where(rows == 4, rolled(strip, -NZ, 1), strip)
-                )
-                for i, slot in enumerate(slots_of[kind]):
-                    f[slot, edges[kind]:edges[kind] + 1, :] = strip[i:i + 1, :WIDE]
+                patch_x(kind, strip_moved(view(kind, shifts[step, place_of])))
                 phase = view(kind, shifts[jnp.minimum(step + 1, STEPS - 1), place_of])
                 ext[outer:outer + 2, 0:WIDE] = phase[5:7, 0:WIDE]
                 ext[outer:outer + 2, WIDE:512] = jnp.where(
@@ -220,26 +320,12 @@
                 ext[outer:outer + 2, 0:WIDE] = strip[5:7]
                 ext[near_row:near_row + 1, WIDE:512] = jnp.where(lane1[:1] < 64, last[1:2], first[1:2])
 
-    def advance(r):
-        p = ext[...]
-        px, mx = rolled(p, -1, 0), rolled(p, 1, 0)
-        py, my = rolled(p, -NZ, 1), rolled(p, NZ, 1)
-        pz, mz = moved_yz(p, 0, -1, place4), moved_yz(p, 0, 1, place4)
-        chem = 0.5 * (p * p * p - p) - 0.5 * (px + mx + py + my + pz + mz - 6.0 * p)
-        slope = [0.5 * (a - b)[:, :WIDE] for a, b in ((px, mx), (py, my), (pz, mz))]
-        px, mx = rolled(chem, -1, 0)[:, :WIDE], rolled(chem, 1, 0)[:, :WIDE]
-        py, my = rolled(chem, -NZ, 1)[:, :WIDE], rolled(chem, NZ, 1)[:, :WIDE]
-        pz, mz = moved_yz(chem, 0, -1, place4)[:, :WIDE], moved_yz(chem, 0, 1, place4)[:, :WIDE]
-        bend = px + mx + py + my + pz + mz - 6.0 * chem[:, :WIDE]
-        own = p[:, :WIDE]
+    def momentum():
         density = f[0]
         for slot in range(1, 19):
             density = density + f[slot]
-        inverse = 1.0 / density
-        scaled = (-0.5 * coupling / relax_rate) * own
-        next_phase = own + mobility * bend
-        drift = []
-        for axis, push in enumerate((px - mx, py - my, pz - mz)):
+        totals = []
+        for axis in range(3):
             total = None
             for slot in range(1, 19, 2):
                 sign = lattice_vel[slot][axis]
@@ -249,9 +335,30 @@
                         total = pair
                     else:
                         total = total + pair if sign == 1 else total - pair
-            next_phase = next_phase - total * inverse * slope[axis]
-            drift.append((total + scaled * push) * inverse)
+            totals.append(total)
+        return density, totals
+
+    def advance(r):
+        p = ext[...]
+        around = differences(p, place4)
+        chem = bulk(p, around)
+        slope = [0.5 * (a - b)[:, :WIDE] for a, b in around]
+        around = [(a[:, :WIDE], b[:, :WIDE]) for a, b in differences(chem, place4)]
+        bend = bent(chem[:, :WIDE], around)
+        own = p[:, :WIDE]
+        density, totals = momentum()
+        inverse = 1.0 / density
+        scaled = (-0.5 * coupling / relax_rate) * own
+        next_phase = own + mobility * bend
+        drift = []
+        for axis in range(3):
+            next_phase = next_phase - totals[axis] * inverse * slope[axis]
+            drift.append((totals[axis] + scaled * (around[axis][0] - around[axis][1])) * inverse)
         ext[0:12, 0:WIDE] = next_phase[:12]
+        collide(density, drift, r)
+        pack_phase(r)
+
+    def collide(density, drift, r):
         base = 1.0 - 1.5 * (drift[0] * drift[0] + drift[1] * drift[1] + drift[2] * drift[2])
         weight = relax_rate / 36.0 * density
         keep = 1.0 - relax_rate
@@ -262,6 +369,8 @@
             value = rolled(post, step_x, 0)
             moved = moved_yz(value, step_y, step_z, place)
             f[slot] = moved
+            if r is None:
+                return
             if step_x != 0:
                 kind = 0 if step_x == 1 else 1
                 i = (up_slots, down_slots)[kind].index(slot)
@@ -298,62 +407,252 @@
             here, there = f[slot], f[slot + 1]
             put(slot, keep * here + (even + odd))
             put(slot + 1, keep * there + (even - odd))
-        to_y[r, 0, 0:12, :] = packs[0][:12]
-        to_y[r, 1, 0:12, :] = packs[1][:12]
-        pack_phase(r)
+        if r is not None:
+            to_y[r, 0, 0:12, :] = packs[0][:12]
+            to_y[r, 1, 0:12, :] = packs[1][:12]
 
     for slot in range(19):
         f[slot, 0:12, :] = f_in[slot]
         f[slot, 12:16, :] = jnp.ones((4, WIDE), jnp.float32)
     ext[...] = jnp.zeros_like(ext)
-    ext[0:12, 0:WIDE] = p_in[...]
-    pack_phase(0)
-    pl.semaphore_wait(barrier, jnp.where(left_plane | right_plane, 5 + count_y, 8))
-    send(0)
+    sides = ((0, left_plane, left_slot), (1, right_plane, right_slot))
+    e_p[...] = jnp.zeros_like(e_p)
+    e_r[...] = jnp.ones_like(e_r)
+    e_u[...] = jnp.zeros_like(e_u)
+    e_p[0:12, 0:WIDE] = p_in[...]
+    density, totals = momentum()
+    e_r[0:12, 0:WIDE] = density[:12]
+    for axis in range(3):
+        e_u[axis, 0:12, 0:WIDE] = (totals[axis] / density)[:12]
+
+    for kind in (0, 1):
+        edge, second, low = ((11, 10, 8), (0, 1, 0))[kind]
+        for b in range(3):
+            cut = slice(b * 128, b * 128 + 128)
+            out_x[kind, b, 0:4, :] = e_p[low:low + 4, cut]
+            out_x[kind, b, 4:5, :] = e_r[edge:edge + 1, cut]
+            for axis in range(3):
+                out_x[kind, b, 5 + axis:6 + axis, :] = e_u[axis, edge:edge + 1, cut]
+                out_x[kind, b, 13 + axis:14 + axis, :] = e_u[axis, second:second + 1, cut]
+            for i, slot in enumerate(up_slots if kind == 0 else down_slots):
+                out_x[kind, b, 8 + i:9 + i, :] = f[slot, edge:edge + 1, cut]
+        third = (9, 0)[kind]
+        for k in (2 * kind, 2 * kind + 1):
+            cut = slice(256, 384) if k % 2 == 0 else slice(0, 128)
+            out_corner[k, 0:3, :] = e_p[third:third + 3, cut]
+            out_corner[k, 3:4, :] = e_r[edge:edge + 1, cut]
+            for axis in range(3):
+                out_corner[k, 4 + axis:5 + axis, :] = e_u[axis, edge:edge + 1, cut]
+            slot = (up_slots if kind == 0 else down_slots)[3 + k % 2]
+            out_corner[k, 7:8, :] = f[slot, edge:edge + 1, cut]
     for k in (0, 1):
-        wait_for(from_y.at[0, k], recv_sem.at[0, 2 + k])
-    ext[0:12, 384:512] = jnp.where(lane1[:12] < 64, from_y[0, 1, 12:24], from_y[0, 0, 12:24])
-    for kind, is_plane, place_of in ((0, left_plane, left_slot), (1, right_plane, right_slot)):
-        outer = 14 - 2 * kind
-        near_row = 15 - 3 * kind
-
+        cut = slice(256, 384) if k == 0 else slice(0, 128)
+        low = lane1[:12] < 64
+        if k == 0:
+            pair = lambda a, b: jnp.where(low, pltpu.roll(b, 64, 1), a)
+        else:
+            pair = lambda a, b: jnp.where(low, a, pltpu.roll(b, 64, 1))
+        packed = None
+        for i, slot in enumerate(plus_y if k == 0 else minus_y):
+            block = f[slot, :, cut]
+            part = rolled(block, NZ + i * NZ if k == 0 else -NZ - i * NZ, 1)
+            if i == 0:
+                packed = part
+            else:
+                packed = jnp.where(lane1 >= i * NZ if k == 0 else lane1 < 128 - i * NZ, part, packed)
+        out_y[k, 0:12, :] = packed[:12]
+        out_y[k, 12:24, :] = e_p[0:12, cut]
+        out_y[k, 24:36, :] = pair(e_r[0:12, cut], e_u[0, 0:12, cut])
+        out_y[k, 36:48, :] = pair(e_u[1, 0:12, cut], e_u[2, 0:12, cut])
+
+    @pl.when(left_plane)
+    def _():
+        for b in range(3):
+            out_a[2 * b:2 * b + 2, :] = e_p[0:2, b * 128:b * 128 + 128]
+
+    @pl.when(right_plane)
+    def _():
+        for b in range(3):
+            out_a[2 * b:2 * b + 2, :] = e_p[10:12, b * 128:b * 128 + 128]
+
+    pl.semaphore_wait(barrier, jnp.where(any_plane, 5 + count_y + max(count_y - 3, 0), 8))
+
+    for kind, is_plane, side in ((0, right_plane, above), (1, left_plane, below)):
         @pl.when(is_plane)
-        def _(kind=kind, place_of=place_of, outer=outer):
-            wait_for(from_x.at[0, kind], recv_sem.at[0, kind])
-            close_ring(0, kind)
-            phase = view(kind, shifts[0, place_of])
-            ext[outer:outer + 2, 0:WIDE] = phase[5:7, 0:WIDE]
-            ext[outer:outer + 2, WIDE:512] = jnp.where(
-                lane1[:2] < 64, phase[5:7, 384:512], phase[5:7, 512:640]
+        def _(kind=kind, side=side):
+            for y in range(count_y):
+                remote(out_x.at[kind], wide_x.at[kind, pl.ds(gy * 3, 3)], 0, kind, side, y).start()
+
+        @pl.when(jnp.logical_not(is_plane))
+        def _(kind=kind, side=side):
+            for k, y in ((2 * kind, front), (2 * kind + 1, back)):
+                remote(out_corner.at[k], wide_corner.at[k], 0, 4 + k, side, y).start()
+            remote(out_x.at[kind], wide_x.at[kind, pl.ds(0, 3)], 0, kind, side, gy).start()
+
+    @pl.when(any_plane)
+    def _():
+        for j in range(1, count_y):
+            remote(out_a, wide_a.at[j - 1], 0, 8, gx, lax.rem(gy + j, count_y)).start()
+
+    remote(out_y.at[0], wide_y.at[0], 0, 2, gx, front).start()
+    remote(out_y.at[1], wide_y.at[1], 0, 3, gx, back).start()
+
+    for k in (0, 1):
+        wait_for(wide_y.at[k], recv_sem.at[0, 2 + k])
+        cut = slice(512, 640) if k == 0 else slice(384, 512)
+        e_p[0:12, cut] = wide_y[k, 12:24]
+        e_r[0:12, cut] = wide_y[k, 24:36]
+        e_u[0, 0:12, cut] = pltpu.roll(wide_y[k, 24:36], 64, 1)
+        e_u[1, 0:12, cut] = wide_y[k, 36:48]
+        e_u[2, 0:12, cut] = pltpu.roll(wide_y[k, 36:48], 64, 1)
+    for kind, is_plane, place_of in sides:
+        low = (20, 12)[kind]
+        edge, second, third = ((23, 22, 21), (12, 13, 12))[kind]
+
+        @pl.when(is_plane)
+        def _(kind=kind, place_of=place_of):
+            wait_for(wide_x.at[kind], recv_sem.at[0, kind])
+            wait_for(wide_a.at[pl.ds(0, count_y - 1)], recv_sem.at[0, 8])
+            for b in range(blocks + 5):
+                ring_b[b] = wide_x[kind, b % blocks]
+            a_row = (4, 6)[kind]
+            for j in range(count_y):
+                source = lax.rem(gy + count_y - j, count_y)
+                for b in range(3):
+                    piece = out_a[2 * b:2 * b + 2, :] if j == 0 else wide_a[j - 1, 2 * b:2 * b + 2, :]
+                    ring_a[source * 3 + b, a_row:a_row + 2, :] = piece
+            for b in range(5):
+                ring_a[blocks + b] = ring_a[b]
+            shift = shifts[0, place_of]
+            near = view_b(kind, shift)[0:8]
+            phase = (near * 0.75 + rolled(near, NZ, 1) * 0.25) if kind == 0 else (
+                near * 0.25 + rolled(near, NZ, 1) * 0.75)
+            row, at = ((22, 2), (12, 0))[kind]
+            e_p[row:row + 2, 0:512] = phase[at:at + 2, 0:512]
+            e_p[row:row + 2, 512:640] = phase[at:at + 2, 640:768]
+
+        @pl.when(jnp.logical_not(is_plane))
+        def _(kind=kind, low=low, edge=edge, second=second, third=third):
+            for k in (2 * kind, 2 * kind + 1):
+                wait_for(wide_corner.at[k], recv_sem.at[0, 4 + k])
+                cut = slice(512, 640) if k % 2 == 0 else slice(384, 512)
+                e_p[third:third + 3, cut] = wide_corner[k, 0:3]
+                e_r[edge:edge + 1, cut] = wide_corner[k, 3:4]
+                for axis in range(3):
+                    e_u[axis, edge:edge + 1, cut] = wide_corner[k, 4 + axis:5 + axis]
+            wait_for(wide_x.at[kind, pl.ds(0, 3)], recv_sem.at[0, kind])
+            for b in range(3):
+                cut = slice(b * 128, b * 128 + 128)
+                e_p[low:low + 4, cut] = wide_x[kind, b, 0:4]
+                e_r[edge:edge + 1, cut] = wide_x[kind, b, 4:5]
+                for axis in range(3):
+                    e_u[axis, edge:edge + 1, cut] = wide_x[kind, b, 5 + axis:6 + axis]
+                    e_u[axis, second:second + 1, cut] = wide_x[kind, b, 13 + axis:14 + axis]
+
+    p = e_p[...]
+    around = differences(p, place5)
+    chem = bulk(p, around)
+    slope = [0.5 * (a - b) for a, b in around]
+    around = differences(chem, place5)
+    next_phase = p + mobility * bent(chem, around)
+    scaled = (-0.5 * coupling / relax_rate) * p / e_r[...]
+    drift = []
+    for axis in range(3):
+        flow = e_u[axis]
+        next_phase = next_phase - flow * slope[axis]
+        drift.append(flow + scaled * (around[axis][0] - around[axis][1]))
+    for top, at, size in ((0, 0, 12), (12, 12, 2), (14, 22, 2)):
+        ext[top:top + size, 0:WIDE] = next_phase[at:at + size, 0:WIDE]
+        ext[top:top + size, WIDE:512] = jnp.where(
+            lane1[:size] < 64, next_phase[at:at + size, 384:512], next_phase[at:at + size, 512:640]
+        )
+    collide(e_r[0:16, 0:WIDE], [d[0:16, 0:WIDE] for d in drift], None)
+    for k in (0, 1):
+        cut = slice(512, 640) if k == 0 else slice(384, 512)
+        patch_y(k, packed_post(k, wide_y[k, 0:16], e_r[0:16, cut], [d[0:16, cut] for d in drift], lane1))
+    for kind, is_plane, place_of in sides:
+        @pl.when(is_plane)
+        def _(kind=kind, place_of=place_of):
+            first = shifts[0, place_of]
+            row = lax.broadcasted_iota(jnp.int32, (8, 768), 0)
+            edge, at, outer = ((3, 2, 14), (0, 0, 12))[kind]
+            weights_of = ((0.75, 0.25), (0.25, 0.75))[kind]
+            for step in (0, 1):
+                shift = shifts[step, place_of]
+                both = view_b(kind, shift)
+                turn = shift - first if kind == 0 else first - shift - 1
+                own = window_of(ring_a, turn)
+                own = 0.75 * own + 0.25 * rolled(own, -NZ if kind == 0 else NZ, 1)
+                far_p = jnp.where(row < 4, both[0:8], own)
+                around = differences(far_p, place6)
+                chem = bulk(far_p, around)
+                slope = [0.5 * (a - b) for a, b in around]
+                around = differences(chem, place6)
+                if step == 0:
+                    density = both[4:5]
+                    scaled = (-0.5 * coupling / relax_rate) * far_p[edge:edge + 1] / density
+                    drift = [
+                        both[5 + axis:6 + axis]
+                        + scaled * (around[axis][0] - around[axis][1])[edge:edge + 1]
+                        for axis in range(3)
+                    ]
+                    strip = strip_post(kind, both[8:16], density, drift, place6)
+                    strip = weights_of[0] * strip + weights_of[1] * rolled(strip, NZ, 1)
+                    patch_x(kind, strip_moved(strip))
+                else:
+                    after = far_p + mobility * bent(chem, around)
+                    for axis in range(3):
+                        flow = jnp.where(row == edge, both[5 + axis:6 + axis], both[13 + axis:14 + axis])
+                        after = after - flow * slope[axis]
+                    after = weights_of[0] * after + weights_of[1] * rolled(after, NZ, 1)
+                    ext[outer:outer + 2, 0:WIDE] = after[at:at + 2, 0:WIDE]
+                    ext[outer:outer + 2, WIDE:512] = jnp.where(
+                        lane1[:2] < 64, after[at:at + 2, 384:512], after[at:at + 2, 640:768]
+                    )
+
+        @pl.when(jnp.logical_not(is_plane))
+        def _(kind=kind):
+            edge = (23, 12)[kind]
+            strip = jnp.concatenate(
+                [wide_x[kind, b, 8:16] for b in range(3)]
+                + [jnp.broadcast_to(wide_corner[2 * kind + i, 7:8], (8, 128)) for i in (1, 0)],
+                axis=1,
             )
+            strip = strip_post(
+                kind, strip, e_r[edge:edge + 1, :], [d[edge:edge + 1] for d in drift], place5[:8]
+            )
+            patch_x(kind, strip_moved(strip))
+
+    for kind, is_plane in ((0, right_plane), (1, left_plane)):
+        @pl.when(is_plane)
+        def _(kind=kind):
+            wait_for(wide_x.at[kind], send_sem.at[0, kind])
+            wait_for(wide_a.at[pl.ds(0, count_y - 1)], send_sem.at[0, 8])
 
         @pl.when(jnp.logical_not(is_plane))
-        def _(kind=kind, outer=outer, near_row=near_row):
+        def _(kind=kind):
             for k in (2 * kind, 2 * kind + 1):
-                wait_for(from_corner.at[0, k], recv_sem.at[0, 4 + k])
-            wait_for(from_x.at[0, kind, pl.ds(0, 3)], recv_sem.at[0, kind])
-            first, last = from_corner[0, 2 * kind], from_corner[0, 2 * kind + 1]
-            for b in range(3):
-                ext[outer:outer + 2, b * 128:b * 128 + 128] = from_x[0, kind, b, 5:7, :]
-            ext[near_row:near_row + 1, WIDE:512] = jnp.where(lane1[:1] < 64, last[1:2], first[1:2])
+                wait_for(out_corner.at[k], send_sem.at[0, 4 + k])
+            wait_for(out_x.at[kind], send_sem.at[0, kind])
+    for k in (0, 1):
+        wait_for(out_y.at[k], send_sem.at[0, 2 + k])
 
     def body(step, carry):
-        advance(step + 1)
-        send(step + 1)
+        advance(step)
+        send(step)
+        receive(step, step)
         wait_sent(step)
-        receive(step + 1, step)
         return carry
 
-    lax.fori_loop(0, STEPS, body, 0)
+    lax.fori_loop(1, STEPS, body, 0)
     for slot in range(19):
         f_out[slot] = f[slot, 0:12, :]
     p_out[...] = ext[0:12, 0:WIDE]
-    wait_sent(STEPS)
 
 
 def on_device(populations, phase_field, plane_shifts):
     blocks = 3 * lax.axis_size("gy")
-    rounds = STEPS + 1
+    rounds = STEPS
     vmem = pl.BlockSpec(memory_space=pltpu.VMEM)
     return pl.pallas_call(
         kernel,
@@ -373,8 +672,21 @@
             pltpu.VMEM((rounds, 2, 24, 128), jnp.float32),
             pltpu.VMEM((rounds, 4, 8, 128), jnp.float32),
             pltpu.VMEM((blocks + 4, 8, 128), jnp.float32),
-            pltpu.SemaphoreType.DMA((rounds, 8)),
-            pltpu.SemaphoreType.DMA((rounds, 8)),
+            pltpu.VMEM((24, 640), jnp.float32),
+            pltpu.VMEM((24, 640), jnp.float32),
+            pltpu.VMEM((3, 24, 640), jnp.float32),
+            pltpu.VMEM((blocks + 5, 16, 128), jnp.float32),
+            pltpu.VMEM((blocks + 5, 8, 128), jnp.float32),
+            pltpu.VMEM((2, blocks, 16, 128), jnp.float32),
+            pltpu.VMEM((2, 48, 128), jnp.float32),
+            pltpu.VMEM((4, 8, 128), jnp.float32),
+            pltpu.VMEM((lax.axis_size("gy") - 1, 8, 128), jnp.float32),
+            pltpu.VMEM((2, 3, 16, 128), jnp.float32),
+            pltpu.VMEM((2, 48, 128), jnp.float32),
+            pltpu.VMEM((4, 8, 128), jnp.float32),
+            pltpu.VMEM((8, 128), jnp.float32),
+            pltpu.SemaphoreType.DMA((rounds, 9)),
+            pltpu.SemaphoreType.DMA((rounds, 9)),
         ],
         compiler_params=pltpu.CompilerParams(
             collective_id=0, has_side_effects=True, vmem_limit_bytes=32 * 1024 * 1024

time: 54.3 us -> 51.8 us (0.954)
  the two profiles are of different devices: /device:TPU:1 before, /device:TPU:48 now
where the time goes in v2:
time: 51.8 us; the launch traced here: 51.6 us
  Pallas kernels  48.4 us (93%)
  local copies, waits for them, and re-layouts  2.6 us (5%)
  between operations  0.67 us (1%)
    pallas_call x1, Pallas kernels, on_device(): pl.pallas_call(kernel, out_shape=(jax.ShapeDtypeStruct(populations.shape,...  48.4 us
    unnamed x6, local copies, waits for them, and re-layouts  1.71 us

profile of v2, /device:TPU:48, one launch (start us, length us, event | category | flops | bytes accessed | tf_op | source)
XLA Modules:
  0.0 51.6 jit_solution(14031519492805070735)
XLA Ops:
  0.6 0.0 copy-start.1
  0.6 0.0 copy-start
  0.6 1.1 %copy.5.f_in = f32[19,12,384]{2,1,0:T(8,128)S(1)} copy(f32[19,12,384]{2,0,1:T(8,128)} %param.3) | data formatting | bytes 700416 | tf_op args[0]
  1.8 0.0 copy-done.1
  1.8 0.0 copy-done
  1.8 48.4 %shard_map.50 = (f32[19,12,384]{2,1,0:T(8,128)S(1)}, f32[12,384]{1,0:T(8,128)S(1)}) custom-call(s32[4,16]{1,0:T(4,128)S(1)} %copy-done.1, f32[19,12,384]{2,1,0:T(8,128)S(1)} %copy.5.f_in, f32[12,384]{1,0:T(8,128)S(1)} %copy-done), custom_call_target="tpu_custom_call" | custom-call | tf_op jit(solution)/shard_map/pallas_call | solution.py:657
  50.2 0.9 %copy.6 = f32[19,12,384]{2,0,1:T(8,128)} copy(f32[19,12,384]{2,1,0:T(8,128)S(1)} %get-tuple-element.2) | data formatting | bytes 700416 | tf_op jit(solution)/shard_map/pallas_call | solution.py:657
  51.0 0.6 %copy.8 = f32[12,384]{1,0:T(8,128)} copy(f32[12,384]{1,0:T(8,128)S(1)} %get-tuple-element.7) | data formatting | bytes 36864
Async XLA Ops:
  0.6 1.1 %copy-start.1 = (s32[4,16]{1,0:T(4,128)S(1)}, s32[4,16]{1,0:T(4,128)}, u32[]{:S(2)}) copy-start(s32[4,16]{1,0:T(4,128)} %shifts.1) | copy-start | bytes 772
  0.6 1.1 %copy-start = (f32[12,384]{1,0:T(8,128)S(1)}, f32[12,384]{1,0:T(8,128)}, u32[]{:S(2)}) copy-start(f32[12,384]{1,0:T(8,128)} %p_in.1) | copy-start | bytes 55300

commit v3 on v2

--- a/solution.py
+++ b/solution.py
@@ -139,12 +139,67 @@
     return out
 
 
+def lanes_of_y(k):
+    groups = [NZ * i if k == 0 else 104 - NZ * i for i in range(5)]
+    return groups, (120 if k == 0 else 0), ((104, 80) if k == 0 else (0, 24))
+
+
+def with_phase(k, packed, phase):
+    groups, spare, (first, second) = lanes_of_y(k)
+    lane = lax.broadcasted_iota(jnp.int32, (8, 128), 1)
+    upper = lax.broadcasted_iota(jnp.int32, (8, 128), 0) >= 4
+    in_spare = (lane >= spare) & (lane < spare + 8)
+    top, low = phase[0:8], phase[8:16]
+    top_down, low_down = rolled(top, 4, 0), rolled(low, 4, 0)
+    head, tail = packed[0:8], packed[8:16]
+    pieces = ((top_down, first), (top, first), (low_down, first), (top_down, second), (top, second))
+    for start, (piece, at) in zip(groups, pieces):
+        here = upper & (lane >= start) & (lane < start + NZ)
+        tail = jnp.where(here, rolled(piece, start - at, 1), tail)
+    parts = [
+        rolled(low, spare - second, 1),
+        rolled(low_down, spare - second - 8, 1),
+        rolled(low, spare - second - 16, 1),
+    ]
+    head = jnp.where(in_spare, jnp.where(upper, parts[1], parts[0]), head)
+    tail = jnp.where(in_spare & jnp.logical_not(upper), parts[2], tail)
+    return jnp.concatenate([head, tail], axis=0)
+
+
+def phase_part(k, message):
+    groups, spare, (first, second) = lanes_of_y(k)
+    lane = lax.broadcasted_iota(jnp.int32, (8, 128), 1)
+    upper = lax.broadcasted_iota(jnp.int32, (8, 128), 0) >= 4
+    in_first = (lane >= first) & (lane < first + NZ)
+    head, tail = message[0:8], message[8:16]
+    head_up, tail_up = rolled(head, 4, 0), rolled(tail, 4, 0)
+
+    def picked(near, far):
+        return jnp.where(in_first, rolled(near[0], first - near[1], 1), rolled(far[0], second - far[1], 1))
+
+    top = jnp.where(
+        upper,
+        picked((tail, groups[1]), (tail, groups[4])),
+        picked((tail_up, groups[0]), (tail_up, groups[3])),
+    )
+    far = jnp.where(
+        lane < second + 8,
+        rolled(head, second - spare, 1),
+        jnp.where(
+            lane < second + 16,
+            rolled(head_up, second + 8 - spare, 1),
+            rolled(tail, second + 16 - spare, 1),
+        ),
+    )
+    low = jnp.where(in_first, rolled(tail_up, first - groups[2], 1), far)
+    return jnp.concatenate([top, low], axis=0)
+
+
 def kernel(
     shifts, f_in, p_in, f_out, p_out,
-    f, ext, from_x, from_y, from_corner, to_x, to_y, to_corner, ring,
-    e_p, e_r, e_u, ring_b, ring_a,
-    wide_x, wide_y, wide_corner, wide_a, out_x, out_y, out_corner, out_a,
-    send_sem, recv_sem,
+    f, ext, got, got_corner, to_x, to_y, to_corner, ring,
+    e_p, e_r, e_u, ring_b, ring_a, wide, out_x, out_y, out_corner, out_a,
+    send_sem, near_sem, plane_sem, corner_sem, corner_send,
 ):
     count_x, count_y = lax.axis_size("gx"), lax.axis_size("gy")
     gx, gy = lax.axis_index("gx"), lax.axis_index("gy")
@@ -155,32 +210,38 @@
     right_plane = lax.rem(gx, SPAN) == SPAN - 1
     left_slot = lax.rem(gx // SPAN + planes - 1, planes)
     right_slot = gx // SPAN
+    any_plane = left_plane | right_plane
     blocks = 3 * count_y
+    sides = ((0, left_plane, left_slot), (1, right_plane, right_slot))
 
     def signal(x, y):
         pl.semaphore_signal(barrier, inc=1, device_id=(x, y), device_id_type=MESH)
 
     barrier = pltpu.get_barrier_semaphore()
     any_plane = left_plane | right_plane
-    signal(gx, front)
-    signal(gx, back)
-
-    @pl.when(any_plane)
-    def _():
-        for j in range(2, count_y - 1):
-            signal(gx, lax.rem(gy + j, count_y))
+    def far_first():
+        half = count_y // 2
+        order = [(half // 2, 1), (half // 2, 0)]
+        for dx in range(half // 2 - 1, -1, -1):
+            order += [(d, z) for z in (1, 0) for d in sorted({dx, (half - dx) % half})]
+        return [2 * lax.rem(gy // 2 + dx, half) + lax.rem(gy + dz, 2) for dx, dz in dict.fromkeys(order)]
 
     for is_plane, side in ((left_plane, below), (right_plane, above)):
         @pl.when(is_plane)
         def _(side=side):
-            for y in range(count_y):
+            for y in far_first():
                 signal(side, y)
-
+            for j in range(2, count_y - 1):
+                signal(gx, lax.rem(gy + j, count_y))
+
+    signal(gx, front)
+    signal(gx, back)
+    for is_plane, side in ((left_plane, below), (right_plane, above)):
         @pl.when(jnp.logical_not(is_plane))
         def _(side=side):
-            signal(side, gy)
             signal(side, front)
             signal(side, back)
+            signal(side, gy)
 
     lane = lax.broadcasted_iota(jnp.int32, (16, WIDE), 1)
     place = lax.rem(lane, NZ)
@@ -194,52 +255,106 @@
     def pack_phase(r):
         for b in range(3):
             cut = slice(b * 128, b * 128 + 128)
-            to_x[r, 0, b, 5:7, :] = ext[10:12, cut]
-            to_x[r, 1, b, 5:7, :] = ext[0:2, cut]
-        to_y[r, 0, 12:24, :] = ext[0:12, 256:384]
-        to_y[r, 1, 12:24, :] = ext[0:12, 0:128]
-        to_corner[r, 0, 1:2, :] = ext[11:12, 256:384]
-        to_corner[r, 1, 1:2, :] = ext[11:12, 0:128]
-        to_corner[r, 2, 1:2, :] = ext[0:1, 256:384]
-        to_corner[r, 3, 1:2, :] = ext[0:1, 0:128]
-
-    def remote(src, dst, r, kind, x, y):
-        return pltpu.make_async_remote_copy(
-            src_ref=src, dst_ref=dst, send_sem=send_sem.at[r, kind], recv_sem=recv_sem.at[r, kind],
+            to_x[r, 0, 8 * b + 5:8 * b + 7, :] = ext[10:12, cut]
+            to_x[r, 1, 8 * b + 5:8 * b + 7, :] = ext[0:2, cut]
+
+    def remote(src, dst, r, sem, x, y, sent=send_sem):
+        pltpu.make_async_remote_copy(
+            src_ref=src, dst_ref=dst, send_sem=sent.at[r], recv_sem=sem.at[r],
             device_id=(x, y), device_id_type=MESH,
-        )
-
-    def send(r):
+        ).start()
+
+    def rows_of(wide_round):
+        y_rows, strip, corners = (48, 48, 16) if wide_round else (16, 24, 0)
+        return y_rows, strip, 2 * y_rows, strip + corners
+
+    def side_start(kind, wide_round, on_left_plane):
+        _, _, first, size = rows_of(wide_round)
+        return first if kind == 0 else jnp.where(on_left_plane, first, first + size)
+
+    def land(buffer, start, size):
+        return buffer.at[pl.ds(start, size)]
+
+    def landing(r):
+        return wide if r is None else got.at[r]
+
+    def send_x(r, strips, corners):
+        buffer = landing(r)
+        _, strip, first, size = rows_of(r is None)
+        n = 0 if r is None else r
         for kind, is_plane, side in ((0, right_plane, above), (1, left_plane, below)):
             @pl.when(is_plane)
             def _(kind=kind, side=side):
-                for y in range(count_y):
-                    remote(to_x.at[r, kind], from_x.at[r, kind, pl.ds(gy * 3, 3)], r, kind, side, y).start()
+                place = pl.multiple_of(first + size + gy * strip, 8)
+                for y in far_first():
+                    remote(strips(kind), land(buffer, place, strip), n, plane_sem, side, y)
 
             @pl.when(jnp.logical_not(is_plane))
             def _(kind=kind, side=side):
-                for k, y in ((2 * kind, front), (2 * kind + 1, back)):
-                    remote(to_corner.at[r, k], from_corner.at[r, k], r, 4 + k, side, y).start()
-                remote(to_x.at[r, kind], from_x.at[r, kind, pl.ds(0, 3)], r, kind, side, gy).start()
-        remote(to_y.at[r, 0], from_y.at[r, 0], r, 2, gx, front).start()
-        remote(to_y.at[r, 1], from_y.at[r, 1], r, 3, gx, back).start()
+                place = side_start(kind, r is None, lax.rem(side, SPAN) == 0)
+                for k, y in ((0, front), (1, back)):
+                    if r is None:
+                        spot = land(buffer, pl.multiple_of(place + strip + 8 * k, 8), 8)
+                        remote(corners(2 * kind + k), spot, n, near_sem, side, y)
+                    else:
+                        spot = got_corner.at[r, 2 * kind + k]
+                        remote(corners(2 * kind + k), spot, n, corner_sem, side, y, corner_send)
+                remote(strips(kind), land(buffer, pl.multiple_of(place, 8), strip), n, near_sem, side, gy)
+
+    def send_y(r, messages):
+        size = rows_of(r is None)[0]
+        n = 0 if r is None else r
+        for k, y in ((0, front), (1, back)):
+            remote(messages(k), land(landing(r), k * size, size), n, near_sem, gx, y)
 
     def wait_for(ref, sem):
         pltpu.make_async_copy(ref, ref, sem).wait()
 
+    def run_of(r):
+        _, strip, first, size = rows_of(r is None)
+        return first + size, first + 2 * size, count_y * strip + (8 * (count_y - 1) if r is None else 0)
+
+    def wait_corners(r, sem):
+        for is_kind, start, size in (
+            (left_plane, 2, 2), (right_plane, 0, 2), (jnp.logical_not(any_plane), 0, 4)
+        ):
+            @pl.when(is_kind)
+            def _(start=start, size=size):
+                wait_for(got_corner.at[r, pl.ds(start, size)], sem.at[r])
+
     def wait_sent(r):
-        for kind, is_plane in ((0, right_plane), (1, left_plane)):
-            @pl.when(is_plane)
-            def _(kind=kind):
-                wait_for(from_x.at[r, kind], send_sem.at[r, kind])
-
-            @pl.when(jnp.logical_not(is_plane))
-            def _(kind=kind):
-                for k in (2 * kind, 2 * kind + 1):
-                    wait_for(to_corner.at[r, k], send_sem.at[r, 4 + k])
-                wait_for(to_x.at[r, kind], send_sem.at[r, kind])
-        for k in (0, 1):
-            wait_for(to_y.at[r, k], send_sem.at[r, 2 + k])
+        buffer, n = landing(r), 0 if r is None else r
+        short, near, crossing = run_of(r)
+
+        @pl.when(any_plane)
+        def _():
+            wait_for(land(buffer, 0, short + crossing), send_sem.at[n])
+
+        @pl.when(jnp.logical_not(any_plane))
+        def _():
+            wait_for(land(buffer, 0, near), send_sem.at[n])
+
+        if r is not None:
+            wait_corners(r, corner_send)
+
+    def wait_near(r):
+        buffer, n = landing(r), 0 if r is None else r
+        short, near, _ = run_of(r)
+
+        @pl.when(any_plane)
+        def _():
+            wait_for(land(buffer, 0, short), near_sem.at[n])
+
+        @pl.when(jnp.logical_not(any_plane))
+        def _():
+            wait_for(land(buffer, 0, near), near_sem.at[n])
+
+        if r is not None:
+            wait_corners(r, corner_sem)
+
+    def wait_plane(r):
+        short, _, crossing = run_of(r)
+        wait_for(land(landing(r), short, crossing), plane_sem.at[0 if r is None else r])
 
     def window_of(held, turn):
         start = ((gy * 16 - turn - 4) & (16 * count_y - 1)) * NZ
@@ -250,9 +365,11 @@
     def view_b(kind, shift):
         return window_of(ring_b, shift if kind == 0 else -shift - 1)
 
-    def close_ring(r, kind):
+    def close_ring(r):
+        first = run_of(r)[0]
         for b in range(blocks + 4):
-            ring[b] = from_x[r, kind, b % blocks]
+            row = first + 8 * (b % blocks)
+            ring[b] = got[r, row:row + 8]
 
     def view(kind, shift):
         low = shift if kind == 0 else -shift - 1
@@ -276,49 +393,47 @@
             f[slot, edge:edge + 1, :] = strip[i:i + 1, :WIDE]
 
     def receive(r, step):
-        slots_of = (up_slots, down_slots)
-        edges = (0, ROWS - 1)
+        wait_near(r)
         for k in (0, 1):
-            wait_for(from_y.at[r, k], recv_sem.at[r, 2 + k])
-        for k in (0, 1):
-            patch_y(k, from_y[r, k, 0:16])
-        ext[0:12, 384:512] = jnp.where(lane1[:12] < 64, from_y[r, 1, 12:24], from_y[r, 0, 12:24])
-        for kind, is_plane, place_of in ((0, left_plane, left_slot), (1, right_plane, right_slot)):
-            outer = 14 - 2 * kind
-            near_row = 15 - 3 * kind
-
+            patch_y(k, got[r, 16 * k:16 * k + 16])
+        ext[0:12, 384:512] = jnp.where(
+            lane1 < 64, phase_part(1, got[r, 16:32]), phase_part(0, got[r, 0:16])
+        )[:12]
+        for kind, is_plane, _ in sides:
+            @pl.when(jnp.logical_not(is_plane))
+            def _(kind=kind):
+                outer = 14 - 2 * kind
+                near_row = 15 - 3 * kind
+                e = (0, ROWS - 1)[kind]
+                place = pl.multiple_of(side_start(kind, False, left_plane), 8)
+                strip = jnp.concatenate([got[r, pl.ds(place + 8 * b, 8)] for b in range(3)], axis=1)
+                first, last = got_corner[r, 2 * kind], got_corner[r, 2 * kind + 1]
+                plus = rolled(strip, NZ, 1)
+                minus = rolled(strip, -NZ, 1)
+                slots = up_slots if kind == 0 else down_slots
+                for i in range(3):
+                    f[slots[i], e:e + 1, :] = strip[i:i + 1]
+                head = jnp.where(lane1[:1] < NZ, first, plus[3:4, 0:128])
+                tail = jnp.where(lane1[:1] >= 128 - NZ, last, minus[4:5, 256:384])
+                f[slots[3], e:e + 1, 0:128] = head
+                f[slots[3], e:e + 1, 128:384] = plus[3:4, 128:384]
+                f[slots[4], e:e + 1, 0:256] = minus[4:5, 0:256]
+                f[slots[4], e:e + 1, 256:384] = tail
+                ext[outer:outer + 2, 0:WIDE] = strip[5:7]
+                ext[near_row:near_row + 1, WIDE:512] = jnp.where(lane1[:1] < 64, last, first)
+
+        for kind, is_plane, place_of in sides:
             @pl.when(is_plane)
-            def _(kind=kind, place_of=place_of, outer=outer):
-                wait_for(from_x.at[r, kind], recv_sem.at[r, kind])
-                close_ring(r, kind)
+            def _(kind=kind, place_of=place_of):
+                outer = 14 - 2 * kind
+                wait_plane(r)
+                close_ring(r)
                 patch_x(kind, strip_moved(view(kind, shifts[step, place_of])))
                 phase = view(kind, shifts[jnp.minimum(step + 1, STEPS - 1), place_of])
                 ext[outer:outer + 2, 0:WIDE] = phase[5:7, 0:WIDE]
                 ext[outer:outer + 2, WIDE:512] = jnp.where(
                     lane1[:2] < 64, phase[5:7, 384:512], phase[5:7, 512:640]
                 )
-
-            @pl.when(jnp.logical_not(is_plane))
-            def _(kind=kind, outer=outer, near_row=near_row):
-                for k in (2 * kind, 2 * kind + 1):
-                    wait_for(from_corner.at[r, k], recv_sem.at[r, 4 + k])
-                wait_for(from_x.at[r, kind, pl.ds(0, 3)], recv_sem.at[r, kind])
-                strip = jnp.concatenate([from_x[r, kind, b] for b in range(3)], axis=1)
-                first, last = from_corner[r, 2 * kind], from_corner[r, 2 * kind + 1]
-                plus = rolled(strip, NZ, 1)
-                minus = rolled(strip, -NZ, 1)
-                for i in range(3):
-                    slot = slots_of[kind][i]
-                    f[slot, edges[kind]:edges[kind] + 1, :] = strip[i:i + 1]
-                head = jnp.where(lane1[:1] < NZ, first[0:1], plus[3:4, 0:128])
-                tail = jnp.where(lane1[:1] >= 128 - NZ, last[0:1], minus[4:5, 256:384])
-                e = edges[kind]
-                f[slots_of[kind][3], e:e + 1, 0:128] = head
-                f[slots_of[kind][3], e:e + 1, 128:384] = plus[3:4, 128:384]
-                f[slots_of[kind][4], e:e + 1, 0:256] = minus[4:5, 0:256]
-                f[slots_of[kind][4], e:e + 1, 256:384] = tail
-                ext[outer:outer + 2, 0:WIDE] = strip[5:7]
-                ext[near_row:near_row + 1, WIDE:512] = jnp.where(lane1[:1] < 64, last[1:2], first[1:2])
 
     def momentum():
         density = f[0]
@@ -355,8 +470,8 @@
             next_phase = next_phase - totals[axis] * inverse * slope[axis]
             drift.append((totals[axis] + scaled * (around[axis][0] - around[axis][1])) * inverse)
         ext[0:12, 0:WIDE] = next_phase[:12]
+        pack_phase(r)
         collide(density, drift, r)
-        pack_phase(r)
 
     def collide(density, drift, r):
         base = 1.0 - 1.5 * (drift[0] * drift[0] + drift[1] * drift[1] + drift[2] * drift[2])
@@ -377,22 +492,29 @@
                 line = 12 if step_x == 1 else 15
                 shown = value if step_y != 0 else moved
                 for b in range(3):
-                    to_x[r, kind, b, i:i + 1, :] = shown[line:line + 1, b * 128:b * 128 + 128]
+                    to_x[r, kind, 8 * b + i:8 * b + i + 1, :] = shown[line:line + 1, b * 128:b * 128 + 128]
                 if step_y != 0:
                     k = 2 * kind + (0 if step_y == 1 else 1)
                     cut = slice(0, 128) if step_y == 1 else slice(256, 384)
-                    to_corner[r, k, 0:1, :] = moved[line:line + 1, cut]
+                    edge = 11 if step_x == 1 else 0
+                    own = ext[edge:edge + 1, slice(256, 384) if step_y == 1 else slice(0, 128)]
+                    post_row = moved[line:line + 1, cut]
+                    low = lane1[:1] < 64
+                    to_corner[r, k] = (
+                        jnp.where(low, post_row, own) if step_y == 1 else jnp.where(low, own, post_row)
+                    )
             if step_y == 1:
                 i = plus_y.index(slot)
                 part = rolled(moved[:, 0:128], i * NZ, 1)
-                packs[0] = part if i == 0 else jnp.where(lane1 >= i * NZ, part, packs[0])
+                mine = (lane1 >= i * NZ) & (lane1 < i * NZ + NZ)
+                packs[0] = jnp.where(mine, part, packs[0]) if 0 in packs else part
             if step_y == -1:
                 i = minus_y.index(slot)
                 part = rolled(moved[:, 256:384], -i * NZ, 1)
-                packs[1] = part if i == 0 else jnp.where(lane1 < 128 - i * NZ, part, packs[1])
-
-        put(0, keep * f[0] + 12.0 * weight * base)
-        for slot in range(1, 19, 2):
+                mine = (lane1 < 128 - i * NZ) & (lane1 >= 128 - NZ - i * NZ)
+                packs[1] = jnp.where(mine, part, packs[1]) if 1 in packs else part
+
+        def put_pair(slot):
             along = None
             for axis in range(3):
                 sign = lattice_vel[slot][axis]
@@ -407,15 +529,24 @@
             here, there = f[slot], f[slot + 1]
             put(slot, keep * here + (even + odd))
             put(slot + 1, keep * there + (even - odd))
+
+        for slot in (1, 7, 9, 11, 13):
+            put_pair(slot)
         if r is not None:
-            to_y[r, 0, 0:12, :] = packs[0][:12]
-            to_y[r, 1, 0:12, :] = packs[1][:12]
+            send_x(r, lambda kind: to_x.at[r, kind], lambda k: to_corner.at[r, k])
+        for slot in (3, 15, 17):
+            put_pair(slot)
+        if r is not None:
+            for k in (0, 1):
+                to_y[r, k] = with_phase(k, packs[k], ext[0:16, 256:384] if k == 0 else ext[0:16, 0:128])
+            send_y(r, lambda k: to_y.at[r, k])
+        put_pair(5)
+        put(0, keep * f[0] + 12.0 * weight * base)
 
     for slot in range(19):
         f[slot, 0:12, :] = f_in[slot]
         f[slot, 12:16, :] = jnp.ones((4, WIDE), jnp.float32)
     ext[...] = jnp.zeros_like(ext)
-    sides = ((0, left_plane, left_slot), (1, right_plane, right_slot))
     e_p[...] = jnp.zeros_like(e_p)
     e_r[...] = jnp.ones_like(e_r)
     e_u[...] = jnp.zeros_like(e_u)
@@ -429,13 +560,13 @@
         edge, second, low = ((11, 10, 8), (0, 1, 0))[kind]
         for b in range(3):
             cut = slice(b * 128, b * 128 + 128)
-            out_x[kind, b, 0:4, :] = e_p[low:low + 4, cut]
-            out_x[kind, b, 4:5, :] = e_r[edge:edge + 1, cut]
+            out_x[kind, 16 * b:16 * b + 4, :] = e_p[low:low + 4, cut]
+            out_x[kind, 16 * b + 4:16 * b + 5, :] = e_r[edge:edge + 1, cut]
             for axis in range(3):
-                out_x[kind, b, 5 + axis:6 + axis, :] = e_u[axis, edge:edge + 1, cut]
-                out_x[kind, b, 13 + axis:14 + axis, :] = e_u[axis, second:second + 1, cut]
+                out_x[kind, 16 * b + 5 + axis:16 * b + 6 + axis, :] = e_u[axis, edge:edge + 1, cut]
+                out_x[kind, 16 * b + 13 + axis:16 * b + 14 + axis, :] = e_u[axis, second:second + 1, cut]
             for i, slot in enumerate(up_slots if kind == 0 else down_slots):
-                out_x[kind, b, 8 + i:9 + i, :] = f[slot, edge:edge + 1, cut]
+                out_x[kind, 16 * b + 8 + i:16 * b + 9 + i, :] = f[slot, edge:edge + 1, cut]
         third = (9, 0)[kind]
         for k in (2 * kind, 2 * kind + 1):
             cut = slice(256, 384) if k % 2 == 0 else slice(0, 128)
@@ -477,49 +608,63 @@
 
     pl.semaphore_wait(barrier, jnp.where(any_plane, 5 + count_y + max(count_y - 3, 0), 8))
 
-    for kind, is_plane, side in ((0, right_plane, above), (1, left_plane, below)):
-        @pl.when(is_plane)
-        def _(kind=kind, side=side):
-            for y in range(count_y):
-                remote(out_x.at[kind], wide_x.at[kind, pl.ds(gy * 3, 3)], 0, kind, side, y).start()
-
-        @pl.when(jnp.logical_not(is_plane))
-        def _(kind=kind, side=side):
-            for k, y in ((2 * kind, front), (2 * kind + 1, back)):
-                remote(out_corner.at[k], wide_corner.at[k], 0, 4 + k, side, y).start()
-            remote(out_x.at[kind], wide_x.at[kind, pl.ds(0, 3)], 0, kind, side, gy).start()
+    send_x(None, lambda kind: out_x.at[kind], lambda k: out_corner.at[k])
 
     @pl.when(any_plane)
     def _():
+        start = run_of(None)[0] + count_y * 48
         for j in range(1, count_y):
-            remote(out_a, wide_a.at[j - 1], 0, 8, gx, lax.rem(gy + j, count_y)).start()
-
-    remote(out_y.at[0], wide_y.at[0], 0, 2, gx, front).start()
-    remote(out_y.at[1], wide_y.at[1], 0, 3, gx, back).start()
-
+            remote(out_a, land(wide, start + 8 * (j - 1), 8), 0, plane_sem, gx, lax.rem(gy + j, count_y))
+
+    send_y(None, lambda k: out_y.at[k])
+
+    wait_near(None)
     for k in (0, 1):
-        wait_for(wide_y.at[k], recv_sem.at[0, 2 + k])
+        at = 48 * k
         cut = slice(512, 640) if k == 0 else slice(384, 512)
-        e_p[0:12, cut] = wide_y[k, 12:24]
-        e_r[0:12, cut] = wide_y[k, 24:36]
-        e_u[0, 0:12, cut] = pltpu.roll(wide_y[k, 24:36], 64, 1)
-        e_u[1, 0:12, cut] = wide_y[k, 36:48]
-        e_u[2, 0:12, cut] = pltpu.roll(wide_y[k, 36:48], 64, 1)
+        e_p[0:12, cut] = wide[at + 12:at + 24]
+        e_r[0:12, cut] = wide[at + 24:at + 36]
+        e_u[0, 0:12, cut] = pltpu.roll(wide[at + 24:at + 36], 64, 1)
+        e_u[1, 0:12, cut] = wide[at + 36:at + 48]
+        e_u[2, 0:12, cut] = pltpu.roll(wide[at + 36:at + 48], 64, 1)
     for kind, is_plane, place_of in sides:
         low = (20, 12)[kind]
         edge, second, third = ((23, 22, 21), (12, 13, 12))[kind]
 
+        @pl.when(jnp.logical_not(is_plane))
+        def _(kind=kind, low=low, edge=edge, second=second, third=third):
+            place = pl.multiple_of(side_start(kind, True, left_plane), 8)
+            for k in (0, 1):
+                corner = wide[pl.ds(place + 48 + 8 * k, 8)]
+                cut = slice(512, 640) if k == 0 else slice(384, 512)
+                e_p[third:third + 3, cut] = corner[0:3]
+                e_r[edge:edge + 1, cut] = corner[3:4]
+                for axis in range(3):
+                    e_u[axis, edge:edge + 1, cut] = corner[4 + axis:5 + axis]
+            for b in range(3):
+                cut = slice(b * 128, b * 128 + 128)
+                strip = wide[pl.ds(place + 16 * b, 16)]
+                e_p[low:low + 4, cut] = strip[0:4]
+                e_r[edge:edge + 1, cut] = strip[4:5]
+                for axis in range(3):
+                    e_u[axis, edge:edge + 1, cut] = strip[5 + axis:6 + axis]
+                    e_u[axis, second:second + 1, cut] = strip[13 + axis:14 + axis]
+
+    for kind, is_plane, place_of in sides:
         @pl.when(is_plane)
         def _(kind=kind, place_of=place_of):
-            wait_for(wide_x.at[kind], recv_sem.at[0, kind])
-            wait_for(wide_a.at[pl.ds(0, count_y - 1)], recv_sem.at[0, 8])
+            wait_plane(None)
+            start = run_of(None)[0]
             for b in range(blocks + 5):
-                ring_b[b] = wide_x[kind, b % blocks]
+                row = start + 16 * (b % blocks)
+                ring_b[b] = wide[row:row + 16]
+            start = start + 16 * blocks
             a_row = (4, 6)[kind]
             for j in range(count_y):
                 source = lax.rem(gy + count_y - j, count_y)
                 for b in range(3):
-                    piece = out_a[2 * b:2 * b + 2, :] if j == 0 else wide_a[j - 1, 2 * b:2 * b + 2, :]
+                    row = start + 8 * (j - 1) + 2 * b
+                    piece = out_a[2 * b:2 * b + 2, :] if j == 0 else wide[row:row + 2]
                     ring_a[source * 3 + b, a_row:a_row + 2, :] = piece
             for b in range(5):
                 ring_a[blocks + b] = ring_a[b]
@@ -530,24 +675,6 @@
             row, at = ((22, 2), (12, 0))[kind]
             e_p[row:row + 2, 0:512] = phase[at:at + 2, 0:512]
             e_p[row:row + 2, 512:640] = phase[at:at + 2, 640:768]
-
-        @pl.when(jnp.logical_not(is_plane))
-        def _(kind=kind, low=low, edge=edge, second=second, third=third):
-            for k in (2 * kind, 2 * kind + 1):
-                wait_for(wide_corner.at[k], recv_sem.at[0, 4 + k])
-                cut = slice(512, 640) if k % 2 == 0 else slice(384, 512)
-                e_p[third:third + 3, cut] = wide_corner[k, 0:3]
-                e_r[edge:edge + 1, cut] = wide_corner[k, 3:4]
-                for axis in range(3):
-                    e_u[axis, edge:edge + 1, cut] = wide_corner[k, 4 + axis:5 + axis]
-            wait_for(wide_x.at[kind, pl.ds(0, 3)], recv_sem.at[0, kind])
-            for b in range(3):
-                cut = slice(b * 128, b * 128 + 128)
-                e_p[low:low + 4, cut] = wide_x[kind, b, 0:4]
-                e_r[edge:edge + 1, cut] = wide_x[kind, b, 4:5]
-                for axis in range(3):
-                    e_u[axis, edge:edge + 1, cut] = wide_x[kind, b, 5 + axis:6 + axis]
-                    e_u[axis, second:second + 1, cut] = wide_x[kind, b, 13 + axis:14 + axis]
 
     p = e_p[...]
     around = differences(p, place5)
@@ -569,7 +696,7 @@
     collide(e_r[0:16, 0:WIDE], [d[0:16, 0:WIDE] for d in drift], None)
     for k in (0, 1):
         cut = slice(512, 640) if k == 0 else slice(384, 512)
-        patch_y(k, packed_post(k, wide_y[k, 0:16], e_r[0:16, cut], [d[0:16, cut] for d in drift], lane1))
+        patch_y(k, packed_post(k, wide[48 * k:48 * k + 16], e_r[0:16, cut], [d[0:16, cut] for d in drift], lane1))
     for kind, is_plane, place_of in sides:
         @pl.when(is_plane)
         def _(kind=kind, place_of=place_of):
@@ -613,9 +740,10 @@
         @pl.when(jnp.logical_not(is_plane))
         def _(kind=kind):
             edge = (23, 12)[kind]
+            place = pl.multiple_of(side_start(kind, True, left_plane), 8)
             strip = jnp.concatenate(
-                [wide_x[kind, b, 8:16] for b in range(3)]
-                + [jnp.broadcast_to(wide_corner[2 * kind + i, 7:8], (8, 128)) for i in (1, 0)],
+                [wide[pl.ds(place + 16 * b + 8, 8)] for b in range(3)]
+                + [jnp.broadcast_to(wide[pl.ds(place + 48 + 8 * i, 8)][7:8], (8, 128)) for i in (1, 0)],
                 axis=1,
             )
             strip = strip_post(
@@ -623,31 +751,25 @@
             )
             patch_x(kind, strip_moved(strip))
 
-    for kind, is_plane in ((0, right_plane), (1, left_plane)):
-        @pl.when(is_plane)
-        def _(kind=kind):
-            wait_for(wide_x.at[kind], send_sem.at[0, kind])
-            wait_for(wide_a.at[pl.ds(0, count_y - 1)], send_sem.at[0, 8])
-
-        @pl.when(jnp.logical_not(is_plane))
-        def _(kind=kind):
-            for k in (2 * kind, 2 * kind + 1):
-                wait_for(out_corner.at[k], send_sem.at[0, 4 + k])
-            wait_for(out_x.at[kind], send_sem.at[0, kind])
-    for k in (0, 1):
-        wait_for(out_y.at[k], send_sem.at[0, 2 + k])
-
     def body(step, carry):
         advance(step)
-        send(step)
+
+        @pl.when(step == 1)
+        def _():
+            wait_sent(None)
+
+        @pl.when(step > 1)
+        def _():
+            wait_sent(step - 1)
+
         receive(step, step)
-        wait_sent(step)
         return carry
 
     lax.fori_loop(1, STEPS, body, 0)
     for slot in range(19):
         f_out[slot] = f[slot, 0:12, :]
     p_out[...] = ext[0:12, 0:WIDE]
+    wait_sent(STEPS - 1)
 
 
 def on_device(populations, phase_field, plane_shifts):
@@ -665,28 +787,27 @@
         scratch_shapes=[
             pltpu.VMEM((19, 16, WIDE), jnp.float32),
             pltpu.VMEM((16, 512), jnp.float32),
-            pltpu.VMEM((rounds, 2, blocks, 8, 128), jnp.float32),
+            pltpu.VMEM((rounds, 56 + 8 * blocks, 128), jnp.float32),
+            pltpu.VMEM((rounds, 4, 1, 128), jnp.float32),
             pltpu.VMEM((rounds, 2, 24, 128), jnp.float32),
-            pltpu.VMEM((rounds, 4, 8, 128), jnp.float32),
-            pltpu.VMEM((rounds, 2, 3, 8, 128), jnp.float32),
-            pltpu.VMEM((rounds, 2, 24, 128), jnp.float32),
-            pltpu.VMEM((rounds, 4, 8, 128), jnp.float32),
+            pltpu.VMEM((rounds, 2, 16, 128), jnp.float32),
+            pltpu.VMEM((rounds, 4, 1, 128), jnp.float32),
             pltpu.VMEM((blocks + 4, 8, 128), jnp.float32),
             pltpu.VMEM((24, 640), jnp.float32),
             pltpu.VMEM((24, 640), jnp.float32),
             pltpu.VMEM((3, 24, 640), jnp.float32),
             pltpu.VMEM((blocks + 5, 16, 128), jnp.float32),
             pltpu.VMEM((blocks + 5, 8, 128), jnp.float32),
-            pltpu.VMEM((2, blocks, 16, 128), jnp.float32),
+            pltpu.VMEM((160 + 16 * blocks + 8 * (lax.axis_size("gy") - 1), 128), jnp.float32),
             pltpu.VMEM((2, 48, 128), jnp.float32),
-            pltpu.VMEM((4, 8, 128), jnp.float32),
-            pltpu.VMEM((lax.axis_size("gy") - 1, 8, 128), jnp.float32),
-            pltpu.VMEM((2, 3, 16, 128), jnp.float32),
             pltpu.VMEM((2, 48, 128), jnp.float32),
             pltpu.VMEM((4, 8, 128), jnp.float32),
             pltpu.VMEM((8, 128), jnp.float32),
-            pltpu.SemaphoreType.DMA((rounds, 9)),
-            pltpu.SemaphoreType.DMA((rounds, 9)),
+            pltpu.SemaphoreType.DMA((rounds,)),
+            pltpu.SemaphoreType.DMA((rounds,)),
+            pltpu.SemaphoreType.DMA((rounds,)),
+            pltpu.SemaphoreType.DMA((rounds,)),
+            pltpu.SemaphoreType.DMA((rounds,)),
         ],
         compiler_params=pltpu.CompilerParams(
             collective_id=0, has_side_effects=True, vmem_limit_bytes=32 * 1024 * 1024

time: 51.8 us -> 50.6 us (0.977)
  the two profiles are of different devices: /device:TPU:48 before, /device:TPU:40 now
where the time goes in v3:
time: 50.6 us; the launch traced here: 50.4 us
  Pallas kernels  47.1 us (93%)
  local copies, waits for them, and re-layouts  2.6 us (5%)
  between operations  0.67 us (1%)
    pallas_call x1, Pallas kernels, on_device(): pl.pallas_call(kernel, out_shape=(jax.ShapeDtypeStruct(populations.shape,...  47.1 us
    unnamed x6, local copies, waits for them, and re-layouts  1.71 us

profile of v3, /device:TPU:40, one launch (start us, length us, event | category | flops | bytes accessed | tf_op | source)
XLA Modules:
  0.0 50.4 jit_solution(12868878734146384569)
XLA Ops:
  0.6 0.0 copy-start.1
  0.6 0.0 copy-start
  0.6 1.1 %copy.5.f_in = f32[19,12,384]{2,1,0:T(8,128)S(1)} copy(f32[19,12,384]{2,0,1:T(8,128)} %param.3) | data formatting | bytes 700416 | tf_op args[0]
  1.8 0.0 copy-done.1
  1.8 0.0 copy-done
  1.8 47.1 %shard_map.50 = (f32[19,12,384]{2,1,0:T(8,128)S(1)}, f32[12,384]{1,0:T(8,128)S(1)}) custom-call(s32[4,16]{1,0:T(4,128)S(1)} %copy-done.1, f32[19,12,384]{2,1,0:T(8,128)S(1)} %copy.5.f_in, f32[12,384]{1,0:T(8,128)S(1)} %copy-done), custom_call_target="tpu_custom_call" | custom-call | tf_op jit(solution)/shard_map/pallas_call | solution.py:779
  48.9 0.9 %copy.6 = f32[19,12,384]{2,0,1:T(8,128)} copy(f32[19,12,384]{2,1,0:T(8,128)S(1)} %get-tuple-element.2) | data formatting | bytes 700416 | tf_op jit(solution)/shard_map/pallas_call | solution.py:779
  49.8 0.6 %copy.8 = f32[12,384]{1,0:T(8,128)} copy(f32[12,384]{1,0:T(8,128)S(1)} %get-tuple-element.7) | data formatting | bytes 36864
Async XLA Ops:
  0.6 1.1 %copy-start.1 = (s32[4,16]{1,0:T(4,128)S(1)}, s32[4,16]{1,0:T(4,128)}, u32[]{:S(2)}) copy-start(s32[4,16]{1,0:T(4,128)} %shifts.1) | copy-start | bytes 772
  0.6 1.1 %copy-start = (f32[12,384]{1,0:T(8,128)S(1)}, f32[12,384]{1,0:T(8,128)}, u32[]{:S(2)}) copy-start(f32[12,384]{1,0:T(8,128)} %p_in.1) | copy-start | bytes 55300

commit v4 on v3

--- a/solution.py
+++ b/solution.py
@@ -45,6 +45,34 @@
 minus_y = (4, 8, 9, 16, 18)
 
 
+zero_x = (0, 3, 4, 5, 6, 15, 16, 17, 18)
+near_x = (up_slots + zero_x, down_slots + zero_x)
+zero_y = tuple(slot for slot in range(19) if lattice_vel[slot][1] == 0)
+near_y = (plus_y + zero_y, minus_y + zero_y)
+y_units = tuple(
+    tuple((slot, 1) for slot in near_y[k]) + tuple((slot, 2) for slot in (plus_y, minus_y)[k])
+    + ((None, 1), (None, 2), (None, 3))
+    for k in (0, 1)
+)
+
+
+def corner_units(kind, k):
+    step = (1 - 2 * kind, 1 - 2 * k)
+    units = []
+    for deep in ((1, 1), (2, 1), (1, 2), (2, 2)):
+        for slot in range(19):
+            if all(
+                lattice_vel[slot][axis] == step[axis] or (deep[axis] == 1 and lattice_vel[slot][axis] == 0)
+                for axis in (0, 1)
+            ):
+                units.append((slot,) + deep)
+    return tuple(units) + tuple((None, x, y) for x in (1, 2, 3) for y in range(1, 5 - x))
+
+
+def lane_of(k, depth):
+    return 128 - NZ * depth if k == 0 else NZ * (depth - 1)
+
+
 def rolled(value, shift, axis):
     size = value.shape[axis]
     shift = shift % size
@@ -94,9 +122,14 @@
     along = along + jnp.where(row == 1, sign * full[2], jnp.where(row == 2, -sign * full[2], 0.0))
     weight = jnp.where(row == 0, 2.0, 1.0) * (relax_rate / 36.0) * density
     post = relaxed(here, weight, along, full)
+    return strip_along_z(kind, post, place)
+
+
+def strip_along_z(kind, strip, place):
+    row = lax.broadcasted_iota(jnp.int32, strip.shape, 0)
     first, second = (1, -1) if kind == 0 else (-1, 1)
     return jnp.where(
-        row == 1, moved_yz(post, 0, first, place), jnp.where(row == 2, moved_yz(post, 0, second, place), post)
+        row == 1, moved_yz(strip, 0, first, place), jnp.where(row == 2, moved_yz(strip, 0, second, place), strip)
     )
 
 
@@ -199,6 +232,7 @@
     shifts, f_in, p_in, f_out, p_out,
     f, ext, got, got_corner, to_x, to_y, to_corner, ring,
     e_p, e_r, e_u, ring_b, ring_a, wide, out_x, out_y, out_corner, out_a,
+    fx, chem_x, tile_a, ring_e, ring_o, last, last_x, last_y, last_corner, last_a,
     send_sem, near_sem, plane_sem, corner_sem, corner_send,
 ):
     count_x, count_y = lax.axis_size("gx"), lax.axis_size("gy")
@@ -255,8 +289,8 @@
     def pack_phase(r):
         for b in range(3):
             cut = slice(b * 128, b * 128 + 128)
-            to_x[r, 0, 8 * b + 5:8 * b + 7, :] = ext[10:12, cut]
-            to_x[r, 1, 8 * b + 5:8 * b + 7, :] = ext[0:2, cut]
+            to_x[0, 8 * b + 5:8 * b + 7, :] = ext[10:12, cut]
+            to_x[1, 8 * b + 5:8 * b + 7, :] = ext[0:2, cut]
 
     def remote(src, dst, r, sem, x, y, sent=send_sem):
         pltpu.make_async_remote_copy(
@@ -264,24 +298,24 @@
             device_id=(x, y), device_id_type=MESH,
         ).start()
 
-    def rows_of(wide_round):
-        y_rows, strip, corners = (48, 48, 16) if wide_round else (16, 24, 0)
+    def rows_of(r):
+        y_rows, strip, corners = {0: (48, 48, 16), 1: (16, 24, 0), 2: (64, 72, 16)}[r]
         return y_rows, strip, 2 * y_rows, strip + corners
 
-    def side_start(kind, wide_round, on_left_plane):
-        _, _, first, size = rows_of(wide_round)
+    def side_start(kind, r, on_left_plane):
+        _, _, first, size = rows_of(r)
         return first if kind == 0 else jnp.where(on_left_plane, first, first + size)
 
     def land(buffer, start, size):
         return buffer.at[pl.ds(start, size)]
 
     def landing(r):
-        return wide if r is None else got.at[r]
+        return {0: wide, 1: got, 2: last}[r]
 
     def send_x(r, strips, corners):
         buffer = landing(r)
-        _, strip, first, size = rows_of(r is None)
-        n = 0 if r is None else r
+        _, strip, first, size = rows_of(r)
+        n = r
         for kind, is_plane, side in ((0, right_plane, above), (1, left_plane, below)):
             @pl.when(is_plane)
             def _(kind=kind, side=side):
@@ -291,19 +325,19 @@
 
             @pl.when(jnp.logical_not(is_plane))
             def _(kind=kind, side=side):
-                place = side_start(kind, r is None, lax.rem(side, SPAN) == 0)
+                place = side_start(kind, r, lax.rem(side, SPAN) == 0)
                 for k, y in ((0, front), (1, back)):
-                    if r is None:
+                    if r != 1:
                         spot = land(buffer, pl.multiple_of(place + strip + 8 * k, 8), 8)
                         remote(corners(2 * kind + k), spot, n, near_sem, side, y)
                     else:
-                        spot = got_corner.at[r, 2 * kind + k]
+                        spot = got_corner.at[2 * kind + k]
                         remote(corners(2 * kind + k), spot, n, corner_sem, side, y, corner_send)
                 remote(strips(kind), land(buffer, pl.multiple_of(place, 8), strip), n, near_sem, side, gy)
 
     def send_y(r, messages):
-        size = rows_of(r is None)[0]
-        n = 0 if r is None else r
+        size = rows_of(r)[0]
+        n = r
         for k, y in ((0, front), (1, back)):
             remote(messages(k), land(landing(r), k * size, size), n, near_sem, gx, y)
 
@@ -311,8 +345,8 @@
         pltpu.make_async_copy(ref, ref, sem).wait()
 
     def run_of(r):
-        _, strip, first, size = rows_of(r is None)
-        return first + size, first + 2 * size, count_y * strip + (8 * (count_y - 1) if r is None else 0)
+        _, strip, first, size = rows_of(r)
+        return first + size, first + 2 * size, count_y * strip + (8, 0, 24)[r] * (count_y - 1)
 
     def wait_corners(r, sem):
         for is_kind, start, size in (
@@ -320,10 +354,10 @@
         ):
             @pl.when(is_kind)
             def _(start=start, size=size):
-                wait_for(got_corner.at[r, pl.ds(start, size)], sem.at[r])
+                wait_for(got_corner.at[pl.ds(start, size)], sem.at[r])
 
     def wait_sent(r):
-        buffer, n = landing(r), 0 if r is None else r
+        buffer, n = landing(r), r
         short, near, crossing = run_of(r)
 
         @pl.when(any_plane)
@@ -334,11 +368,11 @@
         def _():
             wait_for(land(buffer, 0, near), send_sem.at[n])
 
-        if r is not None:
+        if r == 1:
             wait_corners(r, corner_send)
 
     def wait_near(r):
-        buffer, n = landing(r), 0 if r is None else r
+        buffer, n = landing(r), r
         short, near, _ = run_of(r)
 
         @pl.when(any_plane)
@@ -349,12 +383,12 @@
         def _():
             wait_for(land(buffer, 0, near), near_sem.at[n])
 
-        if r is not None:
+        if r == 1:
             wait_corners(r, corner_sem)
 
     def wait_plane(r):
         short, _, crossing = run_of(r)
-        wait_for(land(landing(r), short, crossing), plane_sem.at[0 if r is None else r])
+        wait_for(land(landing(r), short, crossing), plane_sem.at[r])
 
     def window_of(held, turn):
         start = ((gy * 16 - turn - 4) & (16 * count_y - 1)) * NZ
@@ -369,7 +403,7 @@
         first = run_of(r)[0]
         for b in range(blocks + 4):
             row = first + 8 * (b % blocks)
-            ring[b] = got[r, row:row + 8]
+            ring[b] = got[row:row + 8]
 
     def view(kind, shift):
         low = shift if kind == 0 else -shift - 1
@@ -395,9 +429,9 @@
     def receive(r, step):
         wait_near(r)
         for k in (0, 1):
-            patch_y(k, got[r, 16 * k:16 * k + 16])
+            patch_y(k, got[16 * k:16 * k + 16])
         ext[0:12, 384:512] = jnp.where(
-            lane1 < 64, phase_part(1, got[r, 16:32]), phase_part(0, got[r, 0:16])
+            lane1 < 64, phase_part(1, got[16:32]), phase_part(0, got[0:16])
         )[:12]
         for kind, is_plane, _ in sides:
             @pl.when(jnp.logical_not(is_plane))
@@ -405,9 +439,9 @@
                 outer = 14 - 2 * kind
                 near_row = 15 - 3 * kind
                 e = (0, ROWS - 1)[kind]
-                place = pl.multiple_of(side_start(kind, False, left_plane), 8)
-                strip = jnp.concatenate([got[r, pl.ds(place + 8 * b, 8)] for b in range(3)], axis=1)
-                first, last = got_corner[r, 2 * kind], got_corner[r, 2 * kind + 1]
+                place = pl.multiple_of(side_start(kind, 1, left_plane), 8)
+                strip = jnp.concatenate([got[pl.ds(place + 8 * b, 8)] for b in range(3)], axis=1)
+                first, last = got_corner[2 * kind], got_corner[2 * kind + 1]
                 plus = rolled(strip, NZ, 1)
                 minus = rolled(strip, -NZ, 1)
                 slots = up_slots if kind == 0 else down_slots
@@ -435,7 +469,7 @@
                     lane1[:2] < 64, phase[5:7, 384:512], phase[5:7, 512:640]
                 )
 
-    def momentum():
+    def momentum(f):
         density = f[0]
         for slot in range(1, 19):
             density = density + f[slot]
@@ -461,7 +495,7 @@
         around = [(a[:, :WIDE], b[:, :WIDE]) for a, b in differences(chem, place4)]
         bend = bent(chem[:, :WIDE], around)
         own = p[:, :WIDE]
-        density, totals = momentum()
+        density, totals = momentum(f)
         inverse = 1.0 / density
         scaled = (-0.5 * coupling / relax_rate) * own
         next_phase = own + mobility * bend
@@ -470,10 +504,11 @@
             next_phase = next_phase - totals[axis] * inverse * slope[axis]
             drift.append((totals[axis] + scaled * (around[axis][0] - around[axis][1])) * inverse)
         ext[0:12, 0:WIDE] = next_phase[:12]
-        pack_phase(r)
-        collide(density, drift, r)
-
-    def collide(density, drift, r):
+        if r == 1:
+            pack_phase(r)
+        collide(density, drift, r, lambda slot: f[slot])
+
+    def collide(density, drift, r, source):
         base = 1.0 - 1.5 * (drift[0] * drift[0] + drift[1] * drift[1] + drift[2] * drift[2])
         weight = relax_rate / 36.0 * density
         keep = 1.0 - relax_rate
@@ -481,6 +516,9 @@
 
         def put(slot, post):
             step_x, step_y, step_z = lattice_vel[slot]
+            if r == 2:
+                fx[slot, :, 0:WIDE] = post
+                return
             value = rolled(post, step_x, 0)
             moved = moved_yz(value, step_y, step_z, place)
             f[slot] = moved
@@ -492,7 +530,7 @@
                 line = 12 if step_x == 1 else 15
                 shown = value if step_y != 0 else moved
                 for b in range(3):
-                    to_x[r, kind, 8 * b + i:8 * b + i + 1, :] = shown[line:line + 1, b * 128:b * 128 + 128]
+                    to_x[kind, 8 * b + i:8 * b + i + 1, :] = shown[line:line + 1, b * 128:b * 128 + 128]
                 if step_y != 0:
                     k = 2 * kind + (0 if step_y == 1 else 1)
                     cut = slice(0, 128) if step_y == 1 else slice(256, 384)
@@ -500,7 +538,7 @@
                     own = ext[edge:edge + 1, slice(256, 384) if step_y == 1 else slice(0, 128)]
                     post_row = moved[line:line + 1, cut]
                     low = lane1[:1] < 64
-                    to_corner[r, k] = (
+                    to_corner[k] = (
                         jnp.where(low, post_row, own) if step_y == 1 else jnp.where(low, own, post_row)
                     )
             if step_y == 1:
@@ -526,22 +564,22 @@
             scale = 2.0 * weight if slot < 7 else weight
             even = scale * (base + 4.5 * along * along)
             odd = scale * (3.0 * along)
-            here, there = f[slot], f[slot + 1]
+            here, there = source(slot), source(slot + 1)
             put(slot, keep * here + (even + odd))
             put(slot + 1, keep * there + (even - odd))
 
         for slot in (1, 7, 9, 11, 13):
             put_pair(slot)
-        if r is not None:
-            send_x(r, lambda kind: to_x.at[r, kind], lambda k: to_corner.at[r, k])
+        if r == 1:
+            send_x(r, lambda kind: to_x.at[kind], lambda k: to_corner.at[k])
         for slot in (3, 15, 17):
             put_pair(slot)
-        if r is not None:
+        if r == 1:
             for k in (0, 1):
-                to_y[r, k] = with_phase(k, packs[k], ext[0:16, 256:384] if k == 0 else ext[0:16, 0:128])
-            send_y(r, lambda k: to_y.at[r, k])
+                to_y[k] = with_phase(k, packs[k], ext[0:16, 256:384] if k == 0 else ext[0:16, 0:128])
+            send_y(r, lambda k: to_y.at[k])
         put_pair(5)
-        put(0, keep * f[0] + 12.0 * weight * base)
+        put(0, keep * source(0) + 12.0 * weight * base)
 
     for slot in range(19):
         f[slot, 0:12, :] = f_in[slot]
@@ -551,7 +589,7 @@
     e_r[...] = jnp.ones_like(e_r)
     e_u[...] = jnp.zeros_like(e_u)
     e_p[0:12, 0:WIDE] = p_in[...]
-    density, totals = momentum()
+    density, totals = momentum(f)
     e_r[0:12, 0:WIDE] = density[:12]
     for axis in range(3):
         e_u[axis, 0:12, 0:WIDE] = (totals[axis] / density)[:12]
@@ -608,17 +646,17 @@
 
     pl.semaphore_wait(barrier, jnp.where(any_plane, 5 + count_y + max(count_y - 3, 0), 8))
 
-    send_x(None, lambda kind: out_x.at[kind], lambda k: out_corner.at[k])
+    send_x(0, lambda kind: out_x.at[kind], lambda k: out_corner.at[k])
 
     @pl.when(any_plane)
     def _():
-        start = run_of(None)[0] + count_y * 48
+        start = run_of(0)[0] + count_y * 48
         for j in range(1, count_y):
             remote(out_a, land(wide, start + 8 * (j - 1), 8), 0, plane_sem, gx, lax.rem(gy + j, count_y))
 
-    send_y(None, lambda k: out_y.at[k])
-
-    wait_near(None)
+    send_y(0, lambda k: out_y.at[k])
+
+    wait_near(0)
     for k in (0, 1):
         at = 48 * k
         cut = slice(512, 640) if k == 0 else slice(384, 512)
@@ -633,7 +671,7 @@
 
         @pl.when(jnp.logical_not(is_plane))
         def _(kind=kind, low=low, edge=edge, second=second, third=third):
-            place = pl.multiple_of(side_start(kind, True, left_plane), 8)
+            place = pl.multiple_of(side_start(kind, 0, left_plane), 8)
             for k in (0, 1):
                 corner = wide[pl.ds(place + 48 + 8 * k, 8)]
                 cut = slice(512, 640) if k == 0 else slice(384, 512)
@@ -653,8 +691,8 @@
     for kind, is_plane, place_of in sides:
         @pl.when(is_plane)
         def _(kind=kind, place_of=place_of):
-            wait_plane(None)
-            start = run_of(None)[0]
+            wait_plane(0)
+            start = run_of(0)[0]
             for b in range(blocks + 5):
                 row = start + 16 * (b % blocks)
                 ring_b[b] = wide[row:row + 16]
@@ -693,7 +731,7 @@
         ext[top:top + size, WIDE:512] = jnp.where(
             lane1[:size] < 64, next_phase[at:at + size, 384:512], next_phase[at:at + size, 512:640]
         )
-    collide(e_r[0:16, 0:WIDE], [d[0:16, 0:WIDE] for d in drift], None)
+    collide(e_r[0:16, 0:WIDE], [d[0:16, 0:WIDE] for d in drift], None, lambda slot: f[slot])
     for k in (0, 1):
         cut = slice(512, 640) if k == 0 else slice(384, 512)
         patch_y(k, packed_post(k, wide[48 * k:48 * k + 16], e_r[0:16, cut], [d[0:16, cut] for d in drift], lane1))
@@ -740,7 +778,7 @@
         @pl.when(jnp.logical_not(is_plane))
         def _(kind=kind):
             edge = (23, 12)[kind]
-            place = pl.multiple_of(side_start(kind, True, left_plane), 8)
+            place = pl.multiple_of(side_start(kind, 0, left_plane), 8)
             strip = jnp.concatenate(
                 [wide[pl.ds(place + 16 * b + 8, 8)] for b in range(3)]
                 + [jnp.broadcast_to(wide[pl.ds(place + 48 + 8 * i, 8)][7:8], (8, 128)) for i in (1, 0)],
@@ -751,30 +789,256 @@
             )
             patch_x(kind, strip_moved(strip))
 
-    def body(step, carry):
-        advance(step)
-
-        @pl.when(step == 1)
-        def _():
-            wait_sent(None)
-
-        @pl.when(step > 1)
-        def _():
-            wait_sent(step - 1)
-
-        receive(step, step)
-        return carry
-
-    lax.fori_loop(1, STEPS, body, 0)
+    advance(1)
+    wait_sent(0)
+    receive(1, 1)
+
+    advance(2)
+    lane_low = lane1 < 64
+    y_cut = (slice(256, 384), slice(0, 128))
+    for kind in (0, 1):
+        edge, second, low = ((11, 10, 9), (0, 1, 0))[kind]
+        inward = (up_slots, down_slots)[kind]
+        for b in range(3):
+            cut = slice(b * 128, b * 128 + 128)
+            for i, slot in enumerate(near_x[kind]):
+                last_x[kind, 24 * b + i:24 * b + i + 1, :] = fx[slot, edge:edge + 1, cut]
+            for i, slot in enumerate(inward):
+                last_x[kind, 24 * b + 14 + i:24 * b + 15 + i, :] = fx[slot, second:second + 1, cut]
+            last_x[kind, 24 * b + 19:24 * b + 22, :] = ext[low:low + 3, cut]
+        for k in (0, 1):
+            units = corner_units(kind, k)
+            for i in range(0, len(units), 5):
+                line = None
+                for j, (slot, deep_x, deep_y) in enumerate(units[i:i + 5]):
+                    row = 12 - deep_x if kind == 0 else deep_x - 1
+                    part = ext[row:row + 1, y_cut[k]] if slot is None else fx[slot, row:row + 1, y_cut[k]]
+                    part = rolled(part, NZ * j - lane_of(k, deep_y), 1)
+                    line = part if j == 0 else jnp.where(lane1[:1] >= NZ * j, part, line)
+                last_corner[2 * kind + k, i // 5:i // 5 + 1, :] = line
+    for is_plane, edge, slots in ((left_plane, 0, down_slots), (right_plane, 11, up_slots)):
+        @pl.when(is_plane)
+        def _(edge=edge, slots=slots):
+            for b in range(3):
+                for i, slot in enumerate(slots):
+                    last_a[8 * b + i:8 * b + i + 1, :] = fx[slot, edge:edge + 1, b * 128:b * 128 + 128]
+
+    send_x(2, lambda kind: last_x.at[kind], lambda k: last_corner.at[k])
+
+    @pl.when(any_plane)
+    def _():
+        start = run_of(2)[0] + count_y * 72
+        for j in range(1, count_y):
+            remote(last_a, land(last, start + 24 * (j - 1), 24), 2, plane_sem, gx, lax.rem(gy + j, count_y))
+
+    for k in (0, 1):
+        for i in range(0, len(y_units[k]), 5):
+            line = None
+            for j, (slot, deep) in enumerate(y_units[k][i:i + 5]):
+                part = ext[0:16, y_cut[k]] if slot is None else fx[slot, :, y_cut[k]]
+                part = rolled(part, NZ * j - lane_of(k, deep), 1)
+                line = part if j == 0 else jnp.where(lane1 >= NZ * j, part, line)
+            last_y[k, 12 * (i // 5):12 * (i // 5) + 12, :] = line[:12]
+    send_y(2, lambda k: last_y.at[k])
+    e_p[0:12, 0:WIDE] = ext[0:12, 0:WIDE]
+    wait_sent(1)
+
+    wait_near(2)
+
+    def unit_of_y(k, slot, deep):
+        place = y_units[k].index((slot, deep))
+        row = 64 * k + 12 * (place // 5)
+        return rolled(last[row:row + 12], lane_of(k, deep) - NZ * (place % 5), 1)
+
+    lane12 = lane1[:12]
+    for slot in range(19):
+        step_y = lattice_vel[slot][1]
+        if step_y == 0:
+            rim = jnp.where(lane12 < 64, unit_of_y(1, slot, 1), unit_of_y(0, slot, 1))
+        elif step_y == 1:
+            rim = jnp.where(lane12 >= 104, unit_of_y(0, slot, 1), unit_of_y(0, slot, 2))
+        else:
+            rim = jnp.where(lane12 < NZ, unit_of_y(1, slot, 1), unit_of_y(1, slot, 2))
+        fx[slot, 0:12, 384:512] = rim
+    e_p[0:12, 384:512] = jnp.where(
+        lane12 < NZ, unit_of_y(1, None, 1),
+        jnp.where(lane12 < 2 * NZ, unit_of_y(1, None, 2), unit_of_y(1, None, 3)),
+    )
+    e_p[0:12, 512:640] = jnp.where(
+        lane12 >= 104, unit_of_y(0, None, 1),
+        jnp.where(lane12 >= 80, unit_of_y(0, None, 2), unit_of_y(0, None, 3)),
+    )
+    for kind, is_plane, place_of in sides:
+        @pl.when(jnp.logical_not(is_plane))
+        def _(kind=kind):
+            place = pl.multiple_of(side_start(kind, 2, left_plane), 8)
+            rows = ((15, 14), (12, 13))[kind]
+            low = (21, 12)[kind]
+            inward = (up_slots, down_slots)[kind]
+            for b in range(3):
+                cut = slice(b * 128, b * 128 + 128)
+                strip = last[pl.ds(place + 24 * b, 24)]
+                for i, slot in enumerate(near_x[kind]):
+                    fx[slot, rows[0]:rows[0] + 1, cut] = strip[i:i + 1]
+                for i, slot in enumerate(inward):
+                    fx[slot, rows[1]:rows[1] + 1, cut] = strip[14 + i:15 + i]
+                e_p[low:low + 3, cut] = strip[19:22]
+            found = {}
+            for k in (0, 1):
+                corner = last[pl.ds(place + 72 + 8 * k, 8)]
+                for i, (slot, deep_x, deep_y) in enumerate(corner_units(kind, k)):
+                    part = corner[i // 5:i // 5 + 1]
+                    part = rolled(part, lane_of(k, deep_y) - NZ * (i % 5), 1)
+                    found.setdefault((slot, deep_x), []).append((k, deep_y, part))
+            for (slot, deep_x), parts in found.items():
+                line = {}
+                for k, deep_y, part in parts:
+                    start = lane_of(k, deep_y)
+                    here = (lane1[:1] >= start) & (lane1[:1] < start + NZ)
+                    at = k if slot is None else 0
+                    line[at] = jnp.where(here, part, line[at]) if at in line else part
+                if slot is None:
+                    row = 24 - deep_x if kind == 0 else 11 + deep_x
+                    e_p[row:row + 1, 512:640] = line[0]
+                    e_p[row:row + 1, 384:512] = line[1]
+                else:
+                    row = rows[deep_x - 1]
+                    fx[slot, row:row + 1, 384:512] = line[0]
+
+    def mixed(kind, value):
+        near, far = ((0.75, 0.25), (0.25, 0.75))[kind]
+        return near * value + far * rolled(value, NZ, 1)
+
+    for kind, is_plane, place_of in sides:
+        @pl.when(is_plane)
+        def _(kind=kind, place_of=place_of):
+            wait_plane(2)
+            start = run_of(2)[0]
+            for b in range(blocks + 5):
+                row = start + 24 * (b % blocks)
+                ring_e[b] = last[row:row + 24]
+            start = start + 24 * blocks
+            for j in range(count_y):
+                source = lax.rem(gy + count_y - j, count_y)
+                for b in range(3):
+                    row = start + 24 * (j - 1) + 8 * b
+                    ring_o[source * 3 + b] = last_a[8 * b:8 * b + 8, :] if j == 0 else last[row:row + 8]
+            for b in range(5):
+                ring_o[blocks + b] = ring_o[b]
+            row = (15, 12)[kind]
+            shift = shifts[2, place_of]
+            strip = mixed(kind, window_of(ring_e, shift if kind == 0 else -shift - 1)[0:8])
+            for i, slot in enumerate((up_slots, down_slots)[kind]):
+                fx[slot, row:row + 1, 0:384] = strip[i:i + 1, 0:384]
+                fx[slot, row:row + 1, 384:512] = jnp.where(
+                    lane1[:1] < 64, strip[i:i + 1, 384:512], strip[i:i + 1, 640:768]
+                )
+            shift = shifts[3, place_of]
+            phase = mixed(kind, window_of(ring_e, shift if kind == 0 else -shift - 1)[16:24])
+            row, at = ((22, 4), (12, 3))[kind]
+            e_p[row:row + 2, 0:512] = phase[at:at + 2, 0:512]
+            e_p[row:row + 2, 512:640] = phase[at:at + 2, 640:768]
+
+    def narrowed(to, value):
+        for top, at, size in ((0, 0, 12), (12, 12, 2), (14, 22, 2)):
+            to[top:top + size, 0:WIDE] = value[at:at + size, 0:WIDE]
+            to[top:top + size, WIDE:512] = jnp.where(
+                lane1[:size] < 64, value[at:at + size, 384:512], value[at:at + size, 512:640]
+            )
+
+    for slot in range(19):
+        step_x, step_y, step_z = lattice_vel[slot]
+        fx[slot] = moved_yz(rolled(fx[slot], step_x, 0), step_y, step_z, place4)
+    p = e_p[...]
+    narrowed(ext, p)
+    narrowed(chem_x, bulk(p, differences(p, place5)))
+    density, totals = momentum(fx)
+    inverse = 1.0 / density
+    p, chem = ext[...], chem_x[...]
+    around = differences(p, place4)
+    slope = [0.5 * (a - b)[:, :WIDE] for a, b in around]
+    around = differences(chem, place4)
+    next_phase = (p + mobility * bent(chem, around))[:, :WIDE]
+    scaled = (-0.5 * coupling / relax_rate) * p
+    drift = []
+    for axis in range(3):
+        next_phase = next_phase - (totals[axis] * inverse)[:, :WIDE] * slope[axis]
+        drift.append((totals[axis] + scaled * (around[axis][0] - around[axis][1])) * inverse)
+    p_out[...] = next_phase[:12]
+    collide(density[:, :WIDE], [d[:, :WIDE] for d in drift], None, lambda slot: fx[slot, :, 0:WIDE])
+    for k in (0, 1):
+        here = None
+        for i, slot in enumerate((plus_y, minus_y)[k]):
+            part = rolled(fx[slot, :, 384:512], NZ + NZ * i if k == 0 else 104 - NZ * i, 1)
+            if i == 0:
+                here = part
+            else:
+                here = jnp.where(lane1 >= NZ * i if k == 0 else lane1 < 128 - NZ * i, part, here)
+        rim = [d[:, 384:512] for d in drift]
+        patch_y(k, packed_post(k, here, density[:, 384:512], rim, lane1))
+    for kind, is_plane, place_of in sides:
+        @pl.when(is_plane)
+        def _(kind=kind, place_of=place_of):
+            before, shift = shifts[2, place_of], shifts[3, place_of]
+            edge, top, a_row, own_row = ((3, -2, 4, 0), (0, -3, 6, 10))[kind]
+            far = window_of(ring_e, shift if kind == 0 else -shift - 1)
+            inner = strip_moved(strip_along_z(kind, far[14:22], place6))
+            turn = shift - before if kind == 0 else before - shift - 1
+            outer = window_of(ring_o, turn)
+            outer = 0.75 * outer + 0.25 * rolled(outer, -NZ if kind == 0 else NZ, 1)
+            outer = strip_moved(strip_along_z(1 - kind, outer, place6))
+            total = [None] * 4
+            sign = 1.0 - 2.0 * kind
+            for tile, way in ((inner, sign), (outer, -sign)):
+                r = [tile[i:i + 1] for i in range(5)]
+                whole = r[0] + r[1] + r[2] + r[3] + r[4]
+                found = (whole, way * whole, r[3] - r[4], way * (r[1] - r[2]))
+                total = [b if a is None else a + b for a, b in zip(total, found)]
+            for i, slot in enumerate(zero_x):
+                _, step_y, step_z = lattice_vel[slot]
+                line = moved_yz(far[5 + i:6 + i], step_y, step_z, place6[:1])
+                total[0] = total[0] + line
+                if step_y != 0:
+                    total[2] = total[2] + step_y * line
+                if step_z != 0:
+                    total[3] = total[3] + step_z * line
+            tile_a[...] = jnp.zeros_like(tile_a)
+            tile_a[a_row:a_row + 2, 0:512] = e_p[own_row:own_row + 2, 0:512]
+            tile_a[a_row:a_row + 2, 640:768] = e_p[own_row:own_row + 2, 512:640]
+            own = tile_a[...]
+            ahead = rolled(own, -NZ, 1)
+            own = 0.75 * own + 0.25 * ahead if kind == 0 else 0.25 * own + 0.75 * ahead
+            row = lax.broadcasted_iota(jnp.int32, (8, 768), 0)
+            far_p = jnp.where(row < 4, rolled(far[16:24], top, 0), own)
+            around = differences(bulk(far_p, differences(far_p, place6)), place6)
+            inverse = 1.0 / total[0]
+            scaled = (-0.5 * coupling / relax_rate) * far_p[edge:edge + 1]
+            drift = [
+                (total[1 + axis] + scaled * (around[axis][0] - around[axis][1])[edge:edge + 1]) * inverse
+                for axis in range(3)
+            ]
+            strip = mixed(kind, strip_post(kind, inner, total[0], drift, place6))
+            patch_x(kind, strip_moved(strip))
+
+        @pl.when(jnp.logical_not(is_plane))
+        def _(kind=kind):
+            row = (15, 12)[kind]
+            inward = (up_slots, down_slots)[kind]
+            lines = [fx[slot, row:row + 1, :] for slot in inward]
+            strip = jnp.concatenate(lines + lines[:1] * 3, axis=0)
+            strip = strip_post(
+                kind, strip, density[row:row + 1], [d[row:row + 1] for d in drift], place4[:8]
+            )
+            patch_x(kind, strip_moved(strip))
+
+    wait_sent(2)
     for slot in range(19):
         f_out[slot] = f[slot, 0:12, :]
-    p_out[...] = ext[0:12, 0:WIDE]
-    wait_sent(STEPS - 1)
 
 
 def on_device(populations, phase_field, plane_shifts):
     blocks = 3 * lax.axis_size("gy")
-    rounds = STEPS
+    rounds = 3
     vmem = pl.BlockSpec(memory_space=pltpu.VMEM)
     return pl.pallas_call(
         kernel,
@@ -787,11 +1051,11 @@
         scratch_shapes=[
             pltpu.VMEM((19, 16, WIDE), jnp.float32),
             pltpu.VMEM((16, 512), jnp.float32),
-            pltpu.VMEM((rounds, 56 + 8 * blocks, 128), jnp.float32),
-            pltpu.VMEM((rounds, 4, 1, 128), jnp.float32),
-            pltpu.VMEM((rounds, 2, 24, 128), jnp.float32),
-            pltpu.VMEM((rounds, 2, 16, 128), jnp.float32),
-            pltpu.VMEM((rounds, 4, 1, 128), jnp.float32),
+            pltpu.VMEM((56 + 8 * blocks, 128), jnp.float32),
+            pltpu.VMEM((4, 1, 128), jnp.float32),
+            pltpu.VMEM((2, 24, 128), jnp.float32),
+            pltpu.VMEM((2, 16, 128), jnp.float32),
+            pltpu.VMEM((4, 1, 128), jnp.float32),
             pltpu.VMEM((blocks + 4, 8, 128), jnp.float32),
             pltpu.VMEM((24, 640), jnp.float32),
             pltpu.VMEM((24, 640), jnp.float32),
@@ -803,6 +1067,16 @@
             pltpu.VMEM((2, 48, 128), jnp.float32),
             pltpu.VMEM((4, 8, 128), jnp.float32),
             pltpu.VMEM((8, 128), jnp.float32),
+            pltpu.VMEM((19, 16, 512), jnp.float32),
+            pltpu.VMEM((16, 512), jnp.float32),
+            pltpu.VMEM((8, 768), jnp.float32),
+            pltpu.VMEM((blocks + 5, 24, 128), jnp.float32),
+            pltpu.VMEM((blocks + 5, 8, 128), jnp.float32),
+            pltpu.VMEM((304 + 24 * blocks + 24 * (lax.axis_size("gy") - 1), 128), jnp.float32),
+            pltpu.VMEM((2, 72, 128), jnp.float32),
+            pltpu.VMEM((2, 64, 128), jnp.float32),
+            pltpu.VMEM((4, 8, 128), jnp.float32),
+            pltpu.VMEM((24, 128), jnp.float32),
             pltpu.SemaphoreType.DMA((rounds,)),
             pltpu.SemaphoreType.DMA((rounds,)),
             pltpu.SemaphoreType.DMA((rounds,)),

time: 50.6 us -> 47.8 us (0.945)
  the two profiles are of different devices: /device:TPU:40 before, /device:TPU:89 now
where the time goes in v4:
time: 47.8 us; the launch traced here: 47.7 us
  Pallas kernels  44.4 us (93%)
  local copies, waits for them, and re-layouts  2.6 us (5%)
  between operations  0.67 us (1%)
    pallas_call x1, Pallas kernels, on_device(): pl.pallas_call(kernel, out_shape=(jax.ShapeDtypeStruct(populations.shape,...  44.4 us
    unnamed x6, local copies, waits for them, and re-layouts  1.71 us

profile of v4, /device:TPU:89, one launch (start us, length us, event | category | flops | bytes accessed | tf_op | source)
XLA Modules:
  0.0 47.7 jit_solution(15148379989014368168)
XLA Ops:
  0.6 0.0 copy-start.1
  0.6 0.0 copy-start
  0.6 1.1 %copy.5.f_in = f32[19,12,384]{2,1,0:T(8,128)S(1)} copy(f32[19,12,384]{2,0,1:T(8,128)} %param.3) | data formatting | bytes 700416 | tf_op args[0]
  1.8 0.0 copy-done.1
  1.8 0.0 copy-done
  1.8 44.4 %shard_map.50 = (f32[19,12,384]{2,1,0:T(8,128)S(1)}, f32[12,384]{1,0:T(8,128)S(1)}) custom-call(s32[4,16]{1,0:T(4,128)S(1)} %copy-done.1, f32[19,12,384]{2,1,0:T(8,128)S(1)} %copy.5.f_in, f32[12,384]{1,0:T(8,128)S(1)} %copy-done), custom_call_target="tpu_custom_call" | custom-call | tf_op jit(solution)/shard_map/pallas_call | solution.py:1043
  46.2 0.9 %copy.6 = f32[19,12,384]{2,0,1:T(8,128)} copy(f32[19,12,384]{2,1,0:T(8,128)S(1)} %get-tuple-element.2) | data formatting | bytes 700416 | tf_op jit(solution)/shard_map/pallas_call | solution.py:1043
  47.1 0.6 %copy.8 = f32[12,384]{1,0:T(8,128)} copy(f32[12,384]{1,0:T(8,128)S(1)} %get-tuple-element.7) | data formatting | bytes 36864
Async XLA Ops:
  0.6 1.1 %copy-start.1 = (s32[4,16]{1,0:T(4,128)S(1)}, s32[4,16]{1,0:T(4,128)}, u32[]{:S(2)}) copy-start(s32[4,16]{1,0:T(4,128)} %shifts.1) | copy-start | bytes 772
  0.6 1.1 %copy-start = (f32[12,384]{1,0:T(8,128)S(1)}, f32[12,384]{1,0:T(8,128)}, u32[]{:S(2)}) copy-start(f32[12,384]{1,0:T(8,128)} %p_in.1) | copy-start | bytes 55300

commit v5 on v4

--- a/solution.py
+++ b/solution.py
@@ -45,10 +45,11 @@
 minus_y = (4, 8, 9, 16, 18)
 
 
-zero_x = (0, 3, 4, 5, 6, 15, 16, 17, 18)
-near_x = (up_slots + zero_x, down_slots + zero_x)
-zero_y = tuple(slot for slot in range(19) if lattice_vel[slot][1] == 0)
-near_y = (plus_y + zero_y, minus_y + zero_y)
+x_groups = ((0, 5, 6), (3, 15, 17), (4, 18, 16))
+y_groups = ((0, 5, 6), (1, 11, 13), (2, 14, 12))
+folded_x = tuple((first, slot) for first, *pair in x_groups for slot in pair)
+folded_y = tuple((first, slot) for first, *pair in y_groups for slot in pair)
+near_y = tuple(slots + tuple(slot for _, slot in folded_y) for slots in (plus_y, minus_y))
 y_units = tuple(
     tuple((slot, 1) for slot in near_y[k]) + tuple((slot, 2) for slot in (plus_y, minus_y)[k])
     + ((None, 1), (None, 2), (None, 3))
@@ -299,7 +300,7 @@
         ).start()
 
     def rows_of(r):
-        y_rows, strip, corners = {0: (48, 48, 16), 1: (16, 24, 0), 2: (64, 72, 16)}[r]
+        y_rows, strip, corners = {0: (48, 48, 16), 1: (16, 24, 0), 2: (48, 64, 16)}[r]
         return y_rows, strip, 2 * y_rows, strip + corners
 
     def side_start(kind, r, on_left_plane):
@@ -346,7 +347,7 @@
 
     def run_of(r):
         _, strip, first, size = rows_of(r)
-        return first + size, first + 2 * size, count_y * strip + (8, 0, 24)[r] * (count_y - 1)
+        return first + size, first + 2 * size, count_y * strip + (8, 0, 16)[r] * (count_y - 1)
 
     def wait_corners(r, sem):
         for is_kind, start, size in (
@@ -794,18 +795,23 @@
     receive(1, 1)
 
     advance(2)
-    lane_low = lane1 < 64
     y_cut = (slice(256, 384), slice(0, 128))
+    lines = [fx[group[0], edge:edge + 1, 0:WIDE] for edge in (11, 0) for group in x_groups]
+    halves = 0.5 * jnp.concatenate(lines + lines[:2], axis=0)
+    ahead, behind = moved_yz(halves, 0, -1, place[:8]), moved_yz(halves, 0, 1, place[:8])
     for kind in (0, 1):
         edge, second, low = ((11, 10, 9), (0, 1, 0))[kind]
         inward = (up_slots, down_slots)[kind]
         for b in range(3):
             cut = slice(b * 128, b * 128 + 128)
-            for i, slot in enumerate(near_x[kind]):
-                last_x[kind, 24 * b + i:24 * b + i + 1, :] = fx[slot, edge:edge + 1, cut]
             for i, slot in enumerate(inward):
-                last_x[kind, 24 * b + 14 + i:24 * b + 15 + i, :] = fx[slot, second:second + 1, cut]
-            last_x[kind, 24 * b + 19:24 * b + 22, :] = ext[low:low + 3, cut]
+                last_x[kind, 19 * b + i:19 * b + i + 1, :] = fx[slot, edge:edge + 1, cut]
+                last_x[kind, 19 * b + 11 + i:19 * b + 12 + i, :] = fx[slot, second:second + 1, cut]
+            for i, (first, slot) in enumerate(folded_x):
+                at = x_groups.index(next(g for g in x_groups if g[0] == first)) + 3 * kind
+                half = (ahead if lattice_vel[slot][2] == 1 else behind)[at:at + 1, cut]
+                last_x[kind, 19 * b + 5 + i:19 * b + 6 + i, :] = fx[slot, edge:edge + 1, cut] + half
+            last_x[kind, 19 * b + 16:19 * b + 19, :] = ext[low:low + 3, cut]
         for k in (0, 1):
             units = corner_units(kind, k)
             for i in range(0, len(units), 5):
@@ -821,21 +827,25 @@
         def _(edge=edge, slots=slots):
             for b in range(3):
                 for i, slot in enumerate(slots):
-                    last_a[8 * b + i:8 * b + i + 1, :] = fx[slot, edge:edge + 1, b * 128:b * 128 + 128]
+                    last_a[5 * b + i:5 * b + i + 1, :] = fx[slot, edge:edge + 1, b * 128:b * 128 + 128]
 
     send_x(2, lambda kind: last_x.at[kind], lambda k: last_corner.at[k])
 
     @pl.when(any_plane)
     def _():
-        start = run_of(2)[0] + count_y * 72
+        start = run_of(2)[0] + count_y * 64
         for j in range(1, count_y):
-            remote(last_a, land(last, start + 24 * (j - 1), 24), 2, plane_sem, gx, lax.rem(gy + j, count_y))
+            remote(last_a, land(last, start + 16 * (j - 1), 16), 2, plane_sem, gx, lax.rem(gy + j, count_y))
 
     for k in (0, 1):
+        spots = lax.rem(lane1 + (16 if k == 0 else 0), NZ)
         for i in range(0, len(y_units[k]), 5):
             line = None
             for j, (slot, deep) in enumerate(y_units[k][i:i + 5]):
                 part = ext[0:16, y_cut[k]] if slot is None else fx[slot, :, y_cut[k]]
+                for first, folded in folded_y:
+                    if folded == slot:
+                        part = part + moved_yz(0.5 * fx[first, :, y_cut[k]], 0, -lattice_vel[slot][2], spots)
                 part = rolled(part, NZ * j - lane_of(k, deep), 1)
                 line = part if j == 0 else jnp.where(lane1 >= NZ * j, part, line)
             last_y[k, 12 * (i // 5):12 * (i // 5) + 12, :] = line[:12]
@@ -847,13 +857,15 @@
 
     def unit_of_y(k, slot, deep):
         place = y_units[k].index((slot, deep))
-        row = 64 * k + 12 * (place // 5)
+        row = 48 * k + 12 * (place // 5)
         return rolled(last[row:row + 12], lane_of(k, deep) - NZ * (place % 5), 1)
 
     lane12 = lane1[:12]
     for slot in range(19):
         step_y = lattice_vel[slot][1]
-        if step_y == 0:
+        if any(slot == group[0] for group in y_groups):
+            rim = jnp.zeros((12, 128), jnp.float32)
+        elif step_y == 0:
             rim = jnp.where(lane12 < 64, unit_of_y(1, slot, 1), unit_of_y(0, slot, 1))
         elif step_y == 1:
             rim = jnp.where(lane12 >= 104, unit_of_y(0, slot, 1), unit_of_y(0, slot, 2))
@@ -875,17 +887,21 @@
             rows = ((15, 14), (12, 13))[kind]
             low = (21, 12)[kind]
             inward = (up_slots, down_slots)[kind]
+            whole = last[pl.ds(place, 64)]
+            for group in x_groups:
+                fx[group[0], rows[0]:rows[0] + 1, 0:WIDE] = jnp.zeros((1, WIDE), jnp.float32)
             for b in range(3):
                 cut = slice(b * 128, b * 128 + 128)
-                strip = last[pl.ds(place + 24 * b, 24)]
-                for i, slot in enumerate(near_x[kind]):
+                strip = whole[19 * b:19 * b + 19]
+                for i, slot in enumerate(inward):
                     fx[slot, rows[0]:rows[0] + 1, cut] = strip[i:i + 1]
-                for i, slot in enumerate(inward):
-                    fx[slot, rows[1]:rows[1] + 1, cut] = strip[14 + i:15 + i]
-                e_p[low:low + 3, cut] = strip[19:22]
+                    fx[slot, rows[1]:rows[1] + 1, cut] = strip[11 + i:12 + i]
+                for i, (_, slot) in enumerate(folded_x):
+                    fx[slot, rows[0]:rows[0] + 1, cut] = strip[5 + i:6 + i]
+                e_p[low:low + 3, cut] = strip[16:19]
             found = {}
             for k in (0, 1):
-                corner = last[pl.ds(place + 72 + 8 * k, 8)]
+                corner = last[pl.ds(place + 64 + 8 * k, 8)]
                 for i, (slot, deep_x, deep_y) in enumerate(corner_units(kind, k)):
                     part = corner[i // 5:i // 5 + 1]
                     part = rolled(part, lane_of(k, deep_y) - NZ * (i % 5), 1)
@@ -915,14 +931,14 @@
             wait_plane(2)
             start = run_of(2)[0]
             for b in range(blocks + 5):
-                row = start + 24 * (b % blocks)
-                ring_e[b] = last[row:row + 24]
-            start = start + 24 * blocks
+                row = start + 64 * (b % blocks // 3) + 19 * (b % 3)
+                ring_e[b, 0:19] = last[row:row + 19]
+            start = start + 64 * count_y
             for j in range(count_y):
                 source = lax.rem(gy + count_y - j, count_y)
                 for b in range(3):
-                    row = start + 24 * (j - 1) + 8 * b
-                    ring_o[source * 3 + b] = last_a[8 * b:8 * b + 8, :] if j == 0 else last[row:row + 8]
+                    row = start + 16 * (j - 1) + 5 * b
+                    ring_o[source * 3 + b, 0:5] = last_a[5 * b:5 * b + 5, :] if j == 0 else last[row:row + 5]
             for b in range(5):
                 ring_o[blocks + b] = ring_o[b]
             row = (15, 12)[kind]
@@ -935,7 +951,7 @@
                 )
             shift = shifts[3, place_of]
             phase = mixed(kind, window_of(ring_e, shift if kind == 0 else -shift - 1)[16:24])
-            row, at = ((22, 4), (12, 3))[kind]
+            row, at = ((22, 1), (12, 0))[kind]
             e_p[row:row + 2, 0:512] = phase[at:at + 2, 0:512]
             e_p[row:row + 2, 512:640] = phase[at:at + 2, 640:768]
 
@@ -980,9 +996,9 @@
         @pl.when(is_plane)
         def _(kind=kind, place_of=place_of):
             before, shift = shifts[2, place_of], shifts[3, place_of]
-            edge, top, a_row, own_row = ((3, -2, 4, 0), (0, -3, 6, 10))[kind]
+            edge, top, a_row, own_row = ((3, 1, 4, 0), (0, 0, 6, 10))[kind]
             far = window_of(ring_e, shift if kind == 0 else -shift - 1)
-            inner = strip_moved(strip_along_z(kind, far[14:22], place6))
+            inner = strip_moved(strip_along_z(kind, far[11:19], place6))
             turn = shift - before if kind == 0 else before - shift - 1
             outer = window_of(ring_o, turn)
             outer = 0.75 * outer + 0.25 * rolled(outer, -NZ if kind == 0 else NZ, 1)
@@ -994,7 +1010,7 @@
                 whole = r[0] + r[1] + r[2] + r[3] + r[4]
                 found = (whole, way * whole, r[3] - r[4], way * (r[1] - r[2]))
                 total = [b if a is None else a + b for a, b in zip(total, found)]
-            for i, slot in enumerate(zero_x):
+            for i, (_, slot) in enumerate(folded_x):
                 _, step_y, step_z = lattice_vel[slot]
                 line = moved_yz(far[5 + i:6 + i], step_y, step_z, place6[:1])
                 total[0] = total[0] + line
@@ -1072,11 +1088,11 @@
             pltpu.VMEM((8, 768), jnp.float32),
             pltpu.VMEM((blocks + 5, 24, 128), jnp.float32),
             pltpu.VMEM((blocks + 5, 8, 128), jnp.float32),
-            pltpu.VMEM((304 + 24 * blocks + 24 * (lax.axis_size("gy") - 1), 128), jnp.float32),
-            pltpu.VMEM((2, 72, 128), jnp.float32),
+            pltpu.VMEM((256 + 64 * lax.axis_size("gy") + 16 * (lax.axis_size("gy") - 1), 128), jnp.float32),
             pltpu.VMEM((2, 64, 128), jnp.float32),
+            pltpu.VMEM((2, 48, 128), jnp.float32),
             pltpu.VMEM((4, 8, 128), jnp.float32),
-            pltpu.VMEM((24, 128), jnp.float32),
+            pltpu.VMEM((16, 128), jnp.float32),
             pltpu.SemaphoreType.DMA((rounds,)),
             pltpu.SemaphoreType.DMA((rounds,)),
             pltpu.SemaphoreType.DMA((rounds,)),

time: 47.8 us -> 46.4 us (0.971)
  Pallas kernels: 44.4 us -> 43 us
    pallas_call x1, Pallas kernels: 44.4 us -> 43 us  [on_device(): pl.pallas_call(kernel, out_shape=(jax.ShapeDtypeStruct(populations.shape,...]
where the time goes in v5:
time: 46.4 us; the launch traced here: 46.2 us
  Pallas kernels  43 us (93%)
  local copies, waits for them, and re-layouts  2.6 us (6%)
  between operations  0.67 us (1%)
    pallas_call x1, Pallas kernels, on_device(): pl.pallas_call(kernel, out_shape=(jax.ShapeDtypeStruct(populations.shape,...  43 us
    unnamed x6, local copies, waits for them, and re-layouts  1.71 us

profile of v5, /device:TPU:89, one launch (start us, length us, event | category | flops | bytes accessed | tf_op | source)
XLA Modules:
  0.0 46.2 jit_solution(3243045396184731154)
XLA Ops:
  0.6 0.0 copy-start.1
  0.6 0.0 copy-start
  0.6 1.1 %copy.5.f_in = f32[19,12,384]{2,1,0:T(8,128)S(1)} copy(f32[19,12,384]{2,0,1:T(8,128)} %param.3) | data formatting | bytes 700416 | tf_op args[0]
  1.8 0.0 copy-done.1
  1.8 0.0 copy-done
  1.8 43.0 %shard_map.50 = (f32[19,12,384]{2,1,0:T(8,128)S(1)}, f32[12,384]{1,0:T(8,128)S(1)}) custom-call(s32[4,16]{1,0:T(4,128)S(1)} %copy-done.1, f32[19,12,384]{2,1,0:T(8,128)S(1)} %copy.5.f_in, f32[12,384]{1,0:T(8,128)S(1)} %copy-done), custom_call_target="tpu_custom_call" | custom-call | tf_op jit(solution)/shard_map/pallas_call | solution.py:1059
  44.8 0.9 %copy.6 = f32[19,12,384]{2,0,1:T(8,128)} copy(f32[19,12,384]{2,1,0:T(8,128)S(1)} %get-tuple-element.2) | data formatting | bytes 700416 | tf_op jit(solution)/shard_map/pallas_call | solution.py:1059
  45.6 0.6 %copy.8 = f32[12,384]{1,0:T(8,128)} copy(f32[12,384]{1,0:T(8,128)S(1)} %get-tuple-element.7) | data formatting | bytes 36864
Async XLA Ops:
  0.6 1.1 %copy-start.1 = (s32[4,16]{1,0:T(4,128)S(1)}, s32[4,16]{1,0:T(4,128)}, u32[]{:S(2)}) copy-start(s32[4,16]{1,0:T(4,128)} %shifts.1) | copy-start | bytes 772
  0.6 1.1 %copy-start = (f32[12,384]{1,0:T(8,128)S(1)}, f32[12,384]{1,0:T(8,128)}, u32[]{:S(2)}) copy-start(f32[12,384]{1,0:T(8,128)} %p_in.1) | copy-start | bytes 55300

commit v6 on v5

--- a/solution.py
+++ b/solution.py
@@ -70,6 +70,11 @@
     return tuple(units) + tuple((None, x, y) for x in (1, 2, 3) for y in range(1, 5 - x))
 
 
+first_units = tuple(("p", x, y) for x in (1, 2, 3) for y in range(1, 5 - x)) + tuple(
+    (what, 1, 1) for what in ("r", 0, 1, 2, "f")
+)
+
+
 def lane_of(k, depth):
     return 128 - NZ * depth if k == 0 else NZ * (depth - 1)
 
@@ -231,10 +236,10 @@
 
 def kernel(
     shifts, f_in, p_in, f_out, p_out,
-    f, ext, got, got_corner, to_x, to_y, to_corner, ring,
-    e_p, e_r, e_u, ring_b, ring_a, wide, out_x, out_y, out_corner, out_a,
-    fx, chem_x, tile_a, ring_e, ring_o, last, last_x, last_y, last_corner, last_a,
-    send_sem, near_sem, plane_sem, corner_sem, corner_send,
+    f, ext, to_x, to_y, to_corner, ring,
+    e_p, e_r, e_u, ring_b, ring_a, out_x, out_y, out_corner, out_a,
+    fx, chem_x, tile_a, ring_e, ring_o, last_x, last_y, last_corner, last_a,
+    *landings_and_semaphores,
 ):
     count_x, count_y = lax.axis_size("gx"), lax.axis_size("gy")
     gx, gy = lax.axis_index("gx"), lax.axis_index("gy")
@@ -290,106 +295,81 @@
     def pack_phase(r):
         for b in range(3):
             cut = slice(b * 128, b * 128 + 128)
-            to_x[0, 8 * b + 5:8 * b + 7, :] = ext[10:12, cut]
-            to_x[1, 8 * b + 5:8 * b + 7, :] = ext[0:2, cut]
-
-    def remote(src, dst, r, sem, x, y, sent=send_sem):
+            to_x[0, 7 * b + 5:7 * b + 7, :] = ext[10:12, cut]
+            to_x[1, 7 * b + 5:7 * b + 7, :] = ext[0:2, cut]
+
+    *landings, sent, arrived = landings_and_semaphores
+    brought = (
+        dict(zip(("y", "side", "corner", "plane", "around"), landings[0:5])),
+        dict(zip(("y", "side", "corner", "plane"), landings[5:9])),
+        dict(zip(("y", "side", "corner", "plane", "around"), landings[9:14])),
+    )
+    names = ("y", "side", "corner", "plane", "around")
+
+    def remote(src, r, name, index, x, y):
         pltpu.make_async_remote_copy(
-            src_ref=src, dst_ref=dst, send_sem=sent.at[r], recv_sem=sem.at[r],
+            src_ref=src, dst_ref=brought[r][name].at[index],
+            send_sem=sent.at[r, names.index(name)], recv_sem=arrived.at[r, names.index(name)],
             device_id=(x, y), device_id_type=MESH,
         ).start()
 
-    def rows_of(r):
-        y_rows, strip, corners = {0: (48, 48, 16), 1: (16, 24, 0), 2: (48, 64, 16)}[r]
-        return y_rows, strip, 2 * y_rows, strip + corners
-
-    def side_start(kind, r, on_left_plane):
-        _, _, first, size = rows_of(r)
-        return first if kind == 0 else jnp.where(on_left_plane, first, first + size)
-
-    def land(buffer, start, size):
-        return buffer.at[pl.ds(start, size)]
-
-    def landing(r):
-        return {0: wide, 1: got, 2: last}[r]
-
-    def send_x(r, strips, corners):
-        buffer = landing(r)
-        _, strip, first, size = rows_of(r)
-        n = r
+    def send_x(r, strips):
         for kind, is_plane, side in ((0, right_plane, above), (1, left_plane, below)):
             @pl.when(is_plane)
             def _(kind=kind, side=side):
-                place = pl.multiple_of(first + size + gy * strip, 8)
                 for y in far_first():
-                    remote(strips(kind), land(buffer, place, strip), n, plane_sem, side, y)
-
+                    remote(strips.at[kind], r, "plane", gy, side, y)
+
+    def send_sides(r, strips, corners):
+        for kind, is_plane, side in ((0, right_plane, above), (1, left_plane, below)):
             @pl.when(jnp.logical_not(is_plane))
             def _(kind=kind, side=side):
-                place = side_start(kind, r, lax.rem(side, SPAN) == 0)
                 for k, y in ((0, front), (1, back)):
-                    if r != 1:
-                        spot = land(buffer, pl.multiple_of(place + strip + 8 * k, 8), 8)
-                        remote(corners(2 * kind + k), spot, n, near_sem, side, y)
-                    else:
-                        spot = got_corner.at[2 * kind + k]
-                        remote(corners(2 * kind + k), spot, n, corner_sem, side, y, corner_send)
-                remote(strips(kind), land(buffer, pl.multiple_of(place, 8), strip), n, near_sem, side, gy)
-
-    def send_y(r, messages):
-        size = rows_of(r)[0]
-        n = r
-        for k, y in ((0, front), (1, back)):
-            remote(messages(k), land(landing(r), k * size, size), n, near_sem, gx, y)
-
-    def wait_for(ref, sem):
-        pltpu.make_async_copy(ref, ref, sem).wait()
-
-    def run_of(r):
-        _, strip, first, size = rows_of(r)
-        return first + size, first + 2 * size, count_y * strip + (8, 0, 16)[r] * (count_y - 1)
-
-    def wait_corners(r, sem):
-        for is_kind, start, size in (
-            (left_plane, 2, 2), (right_plane, 0, 2), (jnp.logical_not(any_plane), 0, 4)
-        ):
-            @pl.when(is_kind)
-            def _(start=start, size=size):
-                wait_for(got_corner.at[pl.ds(start, size)], sem.at[r])
-
-    def wait_sent(r):
-        buffer, n = landing(r), r
-        short, near, crossing = run_of(r)
-
+                    remote(corners.at[2 * kind + k], r, "corner", 2 * kind + k, side, y)
+                remote(strips.at[kind], r, "side", kind, side, gy)
+
+    def send_around(r, rows):
         @pl.when(any_plane)
         def _():
-            wait_for(land(buffer, 0, short + crossing), send_sem.at[n])
-
-        @pl.when(jnp.logical_not(any_plane))
-        def _():
-            wait_for(land(buffer, 0, near), send_sem.at[n])
-
-        if r == 1:
-            wait_corners(r, corner_send)
-
-    def wait_near(r):
-        buffer, n = landing(r), r
-        short, near, _ = run_of(r)
+            for j in range(1, count_y):
+                remote(rows, r, "around", j - 1, gx, lax.rem(gy + j, count_y))
+
+    def send_y(r, messages):
+        for k, y in ((0, front), (1, back)):
+            remote(messages.at[k], r, "y", k, gx, y)
+
+    def wait_for(r, name, sems):
+        ref, sem = brought[r][name], sems.at[r, names.index(name)]
+        if name in ("side", "corner"):
+            step = 1 if name == "side" else 2
+            for is_kind, start, size in (
+                (left_plane, 1, 1), (right_plane, 0, 1), (jnp.logical_not(any_plane), 0, 2)
+            ):
+                @pl.when(is_kind)
+                def _(start=start, size=size):
+                    part = ref.at[pl.ds(step * start, step * size)]
+                    pltpu.make_async_copy(part, part, sem).wait()
+        else:
+            pltpu.make_async_copy(ref, ref, sem).wait()
+
+    def wait_sent(r):
+        for name in ("y", "side", "corner"):
+            wait_for(r, name, sent)
 
         @pl.when(any_plane)
         def _():
-            wait_for(land(buffer, 0, short), near_sem.at[n])
-
-        @pl.when(jnp.logical_not(any_plane))
-        def _():
-            wait_for(land(buffer, 0, near), near_sem.at[n])
-
-        if r == 1:
-            wait_corners(r, corner_sem)
+            for name in ("plane", "around"):
+                if name in brought[r]:
+                    wait_for(r, name, sent)
+
+    def wait_near(r):
+        for name in ("side", "corner", "y"):
+            wait_for(r, name, arrived)
 
     def wait_plane(r):
-        short, _, crossing = run_of(r)
-        wait_for(land(landing(r), short, crossing), plane_sem.at[r])
+        for name in ("plane", "around"):
+            if name in brought[r]:
+                wait_for(r, name, arrived)
 
     def window_of(held, turn):
         start = ((gy * 16 - turn - 4) & (16 * count_y - 1)) * NZ
@@ -401,10 +381,9 @@
         return window_of(ring_b, shift if kind == 0 else -shift - 1)
 
     def close_ring(r):
-        first = run_of(r)[0]
         for b in range(blocks + 4):
-            row = first + 8 * (b % blocks)
-            ring[b] = got[row:row + 8]
+            row = 7 * (b % 3)
+            ring[b, 0:7] = brought[r]["plane"][b % blocks // 3, row:row + 7]
 
     def view(kind, shift):
         low = shift if kind == 0 else -shift - 1
@@ -430,9 +409,9 @@
     def receive(r, step):
         wait_near(r)
         for k in (0, 1):
-            patch_y(k, got[16 * k:16 * k + 16])
+            patch_y(k, brought[r]["y"][k])
         ext[0:12, 384:512] = jnp.where(
-            lane1 < 64, phase_part(1, got[16:32]), phase_part(0, got[0:16])
+            lane1 < 64, phase_part(1, brought[r]["y"][1]), phase_part(0, brought[r]["y"][0])
         )[:12]
         for kind, is_plane, _ in sides:
             @pl.when(jnp.logical_not(is_plane))
@@ -440,9 +419,9 @@
                 outer = 14 - 2 * kind
                 near_row = 15 - 3 * kind
                 e = (0, ROWS - 1)[kind]
-                place = pl.multiple_of(side_start(kind, 1, left_plane), 8)
-                strip = jnp.concatenate([got[pl.ds(place + 8 * b, 8)] for b in range(3)], axis=1)
-                first, last = got_corner[2 * kind], got_corner[2 * kind + 1]
+                side, corner = brought[r]["side"], brought[r]["corner"]
+                strip = jnp.concatenate([side[kind, 7 * b:7 * b + 7] for b in range(3)], axis=1)
+                first, last = corner[2 * kind], corner[2 * kind + 1]
                 plus = rolled(strip, NZ, 1)
                 minus = rolled(strip, -NZ, 1)
                 slots = up_slots if kind == 0 else down_slots
@@ -531,7 +510,7 @@
                 line = 12 if step_x == 1 else 15
                 shown = value if step_y != 0 else moved
                 for b in range(3):
-                    to_x[kind, 8 * b + i:8 * b + i + 1, :] = shown[line:line + 1, b * 128:b * 128 + 128]
+                    to_x[kind, 7 * b + i:7 * b + i + 1, :] = shown[line:line + 1, b * 128:b * 128 + 128]
                 if step_y != 0:
                     k = 2 * kind + (0 if step_y == 1 else 1)
                     cut = slice(0, 128) if step_y == 1 else slice(256, 384)
@@ -572,13 +551,14 @@
         for slot in (1, 7, 9, 11, 13):
             put_pair(slot)
         if r == 1:
-            send_x(r, lambda kind: to_x.at[kind], lambda k: to_corner.at[k])
+            send_x(r, to_x)
+            send_sides(r, to_x, to_corner)
         for slot in (3, 15, 17):
             put_pair(slot)
         if r == 1:
             for k in (0, 1):
                 to_y[k] = with_phase(k, packs[k], ext[0:16, 256:384] if k == 0 else ext[0:16, 0:128])
-            send_y(r, lambda k: to_y.at[k])
+            send_y(r, to_y)
         put_pair(5)
         put(0, keep * source(0) + 12.0 * weight * base)
 
@@ -606,15 +586,24 @@
                 out_x[kind, 16 * b + 13 + axis:16 * b + 14 + axis, :] = e_u[axis, second:second + 1, cut]
             for i, slot in enumerate(up_slots if kind == 0 else down_slots):
                 out_x[kind, 16 * b + 8 + i:16 * b + 9 + i, :] = f[slot, edge:edge + 1, cut]
-        third = (9, 0)[kind]
-        for k in (2 * kind, 2 * kind + 1):
-            cut = slice(256, 384) if k % 2 == 0 else slice(0, 128)
-            out_corner[k, 0:3, :] = e_p[third:third + 3, cut]
-            out_corner[k, 3:4, :] = e_r[edge:edge + 1, cut]
-            for axis in range(3):
-                out_corner[k, 4 + axis:5 + axis, :] = e_u[axis, edge:edge + 1, cut]
-            slot = (up_slots if kind == 0 else down_slots)[3 + k % 2]
-            out_corner[k, 7:8, :] = f[slot, edge:edge + 1, cut]
+        for k in (0, 1):
+            cut = slice(256, 384) if k == 0 else slice(0, 128)
+            slot = (up_slots if kind == 0 else down_slots)[3 + k]
+            for i in range(0, len(first_units), 5):
+                line = None
+                for j, (what, deep_x, deep_y) in enumerate(first_units[i:i + 5]):
+                    row = 12 - deep_x if kind == 0 else deep_x - 1
+                    if what == "p":
+                        part = e_p[row:row + 1, cut]
+                    elif what == "r":
+                        part = e_r[row:row + 1, cut]
+                    elif what == "f":
+                        part = f[slot, row:row + 1, cut]
+                    else:
+                        part = e_u[what, row:row + 1, cut]
+                    part = rolled(part, NZ * j - lane_of(k, deep_y), 1)
+                    line = part if j == 0 else jnp.where(lane1[:1] >= NZ * j, part, line)
+                out_corner[2 * kind + k, i // 5:i // 5 + 1, :] = line
     for k in (0, 1):
         cut = slice(256, 384) if k == 0 else slice(0, 128)
         low = lane1[:12] < 64
@@ -647,42 +636,47 @@
 
     pl.semaphore_wait(barrier, jnp.where(any_plane, 5 + count_y + max(count_y - 3, 0), 8))
 
-    send_x(0, lambda kind: out_x.at[kind], lambda k: out_corner.at[k])
-
-    @pl.when(any_plane)
-    def _():
-        start = run_of(0)[0] + count_y * 48
-        for j in range(1, count_y):
-            remote(out_a, land(wide, start + 8 * (j - 1), 8), 0, plane_sem, gx, lax.rem(gy + j, count_y))
-
-    send_y(0, lambda k: out_y.at[k])
+    send_around(0, out_a)
+    send_x(0, out_x)
+    send_sides(0, out_x, out_corner)
+    send_y(0, out_y)
 
     wait_near(0)
+    wide = brought[0]
     for k in (0, 1):
-        at = 48 * k
         cut = slice(512, 640) if k == 0 else slice(384, 512)
-        e_p[0:12, cut] = wide[at + 12:at + 24]
-        e_r[0:12, cut] = wide[at + 24:at + 36]
-        e_u[0, 0:12, cut] = pltpu.roll(wide[at + 24:at + 36], 64, 1)
-        e_u[1, 0:12, cut] = wide[at + 36:at + 48]
-        e_u[2, 0:12, cut] = pltpu.roll(wide[at + 36:at + 48], 64, 1)
+        e_p[0:12, cut] = wide["y"][k, 12:24]
+        e_r[0:12, cut] = wide["y"][k, 24:36]
+        e_u[0, 0:12, cut] = pltpu.roll(wide["y"][k, 24:36], 64, 1)
+        e_u[1, 0:12, cut] = wide["y"][k, 36:48]
+        e_u[2, 0:12, cut] = pltpu.roll(wide["y"][k, 36:48], 64, 1)
     for kind, is_plane, place_of in sides:
         low = (20, 12)[kind]
         edge, second, third = ((23, 22, 21), (12, 13, 12))[kind]
 
         @pl.when(jnp.logical_not(is_plane))
         def _(kind=kind, low=low, edge=edge, second=second, third=third):
-            place = pl.multiple_of(side_start(kind, 0, left_plane), 8)
             for k in (0, 1):
-                corner = wide[pl.ds(place + 48 + 8 * k, 8)]
                 cut = slice(512, 640) if k == 0 else slice(384, 512)
-                e_p[third:third + 3, cut] = corner[0:3]
-                e_r[edge:edge + 1, cut] = corner[3:4]
-                for axis in range(3):
-                    e_u[axis, edge:edge + 1, cut] = corner[4 + axis:5 + axis]
+                found = {}
+                for i, (what, deep_x, deep_y) in enumerate(first_units):
+                    start = lane_of(k, deep_y)
+                    part = wide["corner"][2 * kind + k, i // 5:i // 5 + 1]
+                    part = rolled(part, start - NZ * (i % 5), 1)
+                    here = (lane1[:1] >= start) & (lane1[:1] < start + NZ)
+                    key = (what, deep_x)
+                    found[key] = jnp.where(here, part, found[key]) if key in found else part
+                for (what, deep_x), line in found.items():
+                    row = 24 - deep_x if kind == 0 else 11 + deep_x
+                    if what == "p":
+                        e_p[row:row + 1, cut] = line
+                    elif what == "r":
+                        e_r[row:row + 1, cut] = line
+                    elif what != "f":
+                        e_u[what, row:row + 1, cut] = line
             for b in range(3):
                 cut = slice(b * 128, b * 128 + 128)
-                strip = wide[pl.ds(place + 16 * b, 16)]
+                strip = wide["side"][kind, 16 * b:16 * b + 16]
                 e_p[low:low + 4, cut] = strip[0:4]
                 e_r[edge:edge + 1, cut] = strip[4:5]
                 for axis in range(3):
@@ -693,17 +687,15 @@
         @pl.when(is_plane)
         def _(kind=kind, place_of=place_of):
             wait_plane(0)
-            start = run_of(0)[0]
             for b in range(blocks + 5):
-                row = start + 16 * (b % blocks)
-                ring_b[b] = wide[row:row + 16]
-            start = start + 16 * blocks
+                row = 16 * (b % 3)
+                ring_b[b] = wide["plane"][b % blocks // 3, row:row + 16]
             a_row = (4, 6)[kind]
             for j in range(count_y):
                 source = lax.rem(gy + count_y - j, count_y)
                 for b in range(3):
-                    row = start + 8 * (j - 1) + 2 * b
-                    piece = out_a[2 * b:2 * b + 2, :] if j == 0 else wide[row:row + 2]
+                    rows = slice(2 * b, 2 * b + 2)
+                    piece = out_a[rows] if j == 0 else wide["around"][j - 1, rows]
                     ring_a[source * 3 + b, a_row:a_row + 2, :] = piece
             for b in range(5):
                 ring_a[blocks + b] = ring_a[b]
@@ -735,7 +727,7 @@
     collide(e_r[0:16, 0:WIDE], [d[0:16, 0:WIDE] for d in drift], None, lambda slot: f[slot])
     for k in (0, 1):
         cut = slice(512, 640) if k == 0 else slice(384, 512)
-        patch_y(k, packed_post(k, wide[48 * k:48 * k + 16], e_r[0:16, cut], [d[0:16, cut] for d in drift], lane1))
+        patch_y(k, packed_post(k, wide["y"][k, 0:16], e_r[0:16, cut], [d[0:16, cut] for d in drift], lane1))
     for kind, is_plane, place_of in sides:
         @pl.when(is_plane)
         def _(kind=kind, place_of=place_of):
@@ -779,10 +771,14 @@
         @pl.when(jnp.logical_not(is_plane))
         def _(kind=kind):
             edge = (23, 12)[kind]
-            place = pl.multiple_of(side_start(kind, 0, left_plane), 8)
+            at = len(first_units) - 1
+            ends = [
+                rolled(wide["corner"][2 * kind + k, at // 5:at // 5 + 1], lane_of(k, 1) - NZ * (at % 5), 1)
+                for k in (1, 0)
+            ]
             strip = jnp.concatenate(
-                [wide[pl.ds(place + 16 * b + 8, 8)] for b in range(3)]
-                + [jnp.broadcast_to(wide[pl.ds(place + 48 + 8 * i, 8)][7:8], (8, 128)) for i in (1, 0)],
+                [wide["side"][kind, 16 * b + 8:16 * b + 16] for b in range(3)]
+                + [jnp.broadcast_to(line, (8, 128)) for line in ends],
                 axis=1,
             )
             strip = strip_post(
@@ -829,14 +825,9 @@
                 for i, slot in enumerate(slots):
                     last_a[5 * b + i:5 * b + i + 1, :] = fx[slot, edge:edge + 1, b * 128:b * 128 + 128]
 
-    send_x(2, lambda kind: last_x.at[kind], lambda k: last_corner.at[k])
-
-    @pl.when(any_plane)
-    def _():
-        start = run_of(2)[0] + count_y * 64
-        for j in range(1, count_y):
-            remote(last_a, land(last, start + 16 * (j - 1), 16), 2, plane_sem, gx, lax.rem(gy + j, count_y))
-
+    send_around(2, last_a)
+    send_x(2, last_x)
+    send_sides(2, last_x, last_corner)
     for k in (0, 1):
         spots = lax.rem(lane1 + (16 if k == 0 else 0), NZ)
         for i in range(0, len(y_units[k]), 5):
@@ -849,16 +840,17 @@
                 part = rolled(part, NZ * j - lane_of(k, deep), 1)
                 line = part if j == 0 else jnp.where(lane1 >= NZ * j, part, line)
             last_y[k, 12 * (i // 5):12 * (i // 5) + 12, :] = line[:12]
-    send_y(2, lambda k: last_y.at[k])
+    send_y(2, last_y)
     e_p[0:12, 0:WIDE] = ext[0:12, 0:WIDE]
     wait_sent(1)
 
     wait_near(2)
+    last = brought[2]
 
     def unit_of_y(k, slot, deep):
         place = y_units[k].index((slot, deep))
-        row = 48 * k + 12 * (place // 5)
-        return rolled(last[row:row + 12], lane_of(k, deep) - NZ * (place % 5), 1)
+        row = 12 * (place // 5)
+        return rolled(last["y"][k, row:row + 12], lane_of(k, deep) - NZ * (place % 5), 1)
 
     lane12 = lane1[:12]
     for slot in range(19):
@@ -883,11 +875,10 @@
     for kind, is_plane, place_of in sides:
         @pl.when(jnp.logical_not(is_plane))
         def _(kind=kind):
-            place = pl.multiple_of(side_start(kind, 2, left_plane), 8)
             rows = ((15, 14), (12, 13))[kind]
             low = (21, 12)[kind]
             inward = (up_slots, down_slots)[kind]
-            whole = last[pl.ds(place, 64)]
+            whole = last["side"][kind]
             for group in x_groups:
                 fx[group[0], rows[0]:rows[0] + 1, 0:WIDE] = jnp.zeros((1, WIDE), jnp.float32)
             for b in range(3):
@@ -901,7 +892,7 @@
                 e_p[low:low + 3, cut] = strip[16:19]
             found = {}
             for k in (0, 1):
-                corner = last[pl.ds(place + 64 + 8 * k, 8)]
+                corner = last["corner"][2 * kind + k]
                 for i, (slot, deep_x, deep_y) in enumerate(corner_units(kind, k)):
                     part = corner[i // 5:i // 5 + 1]
                     part = rolled(part, lane_of(k, deep_y) - NZ * (i % 5), 1)
@@ -929,16 +920,14 @@
         @pl.when(is_plane)
         def _(kind=kind, place_of=place_of):
             wait_plane(2)
-            start = run_of(2)[0]
             for b in range(blocks + 5):
-                row = start + 64 * (b % blocks // 3) + 19 * (b % 3)
-                ring_e[b, 0:19] = last[row:row + 19]
-            start = start + 64 * count_y
+                row = 19 * (b % 3)
+                ring_e[b, 0:19] = last["plane"][b % blocks // 3, row:row + 19]
             for j in range(count_y):
                 source = lax.rem(gy + count_y - j, count_y)
                 for b in range(3):
-                    row = start + 16 * (j - 1) + 5 * b
-                    ring_o[source * 3 + b, 0:5] = last_a[5 * b:5 * b + 5, :] if j == 0 else last[row:row + 5]
+                    rows = slice(5 * b, 5 * b + 5)
+                    ring_o[source * 3 + b, 0:5] = last_a[rows] if j == 0 else last["around"][j - 1, rows]
             for b in range(5):
                 ring_o[blocks + b] = ring_o[b]
             row = (15, 12)[kind]
@@ -1053,7 +1042,8 @@
 
 
 def on_device(populations, phase_field, plane_shifts):
-    blocks = 3 * lax.axis_size("gy")
+    parts = lax.axis_size("gy")
+    blocks = 3 * parts
     rounds = 3
     vmem = pl.BlockSpec(memory_space=pltpu.VMEM)
     return pl.pallas_call(
@@ -1067,9 +1057,7 @@
         scratch_shapes=[
             pltpu.VMEM((19, 16, WIDE), jnp.float32),
             pltpu.VMEM((16, 512), jnp.float32),
-            pltpu.VMEM((56 + 8 * blocks, 128), jnp.float32),
-            pltpu.VMEM((4, 1, 128), jnp.float32),
-            pltpu.VMEM((2, 24, 128), jnp.float32),
+            pltpu.VMEM((2, 21, 128), jnp.float32),
             pltpu.VMEM((2, 16, 128), jnp.float32),
             pltpu.VMEM((4, 1, 128), jnp.float32),
             pltpu.VMEM((blocks + 4, 8, 128), jnp.float32),
@@ -1078,26 +1066,29 @@
             pltpu.VMEM((3, 24, 640), jnp.float32),
             pltpu.VMEM((blocks + 5, 16, 128), jnp.float32),
             pltpu.VMEM((blocks + 5, 8, 128), jnp.float32),
-            pltpu.VMEM((160 + 16 * blocks + 8 * (lax.axis_size("gy") - 1), 128), jnp.float32),
             pltpu.VMEM((2, 48, 128), jnp.float32),
             pltpu.VMEM((2, 48, 128), jnp.float32),
-            pltpu.VMEM((4, 8, 128), jnp.float32),
-            pltpu.VMEM((8, 128), jnp.float32),
+            pltpu.VMEM((4, 3, 128), jnp.float32),
+            pltpu.VMEM((6, 128), jnp.float32),
             pltpu.VMEM((19, 16, 512), jnp.float32),
             pltpu.VMEM((16, 512), jnp.float32),
             pltpu.VMEM((8, 768), jnp.float32),
             pltpu.VMEM((blocks + 5, 24, 128), jnp.float32),
             pltpu.VMEM((blocks + 5, 8, 128), jnp.float32),
-            pltpu.VMEM((256 + 64 * lax.axis_size("gy") + 16 * (lax.axis_size("gy") - 1), 128), jnp.float32),
-            pltpu.VMEM((2, 64, 128), jnp.float32),
+            pltpu.VMEM((2, 57, 128), jnp.float32),
             pltpu.VMEM((2, 48, 128), jnp.float32),
-            pltpu.VMEM((4, 8, 128), jnp.float32),
-            pltpu.VMEM((16, 128), jnp.float32),
-            pltpu.SemaphoreType.DMA((rounds,)),
-            pltpu.SemaphoreType.DMA((rounds,)),
-            pltpu.SemaphoreType.DMA((rounds,)),
-            pltpu.SemaphoreType.DMA((rounds,)),
-            pltpu.SemaphoreType.DMA((rounds,)),
+            pltpu.VMEM((4, 5, 128), jnp.float32),
+            pltpu.VMEM((15, 128), jnp.float32),
+        ] + [
+            pltpu.VMEM((count, rows, 128), jnp.float32)
+            for count, rows in (
+                (2, 48), (2, 48), (4, 3), (parts, 48), (parts - 1, 6),
+                (2, 16), (2, 21), (4, 1), (parts, 21),
+                (2, 48), (2, 57), (4, 5), (parts, 57), (parts - 1, 15),
+            )
+        ] + [
+            pltpu.SemaphoreType.DMA((rounds, 5)),
+            pltpu.SemaphoreType.DMA((rounds, 5)),
         ],
         compiler_params=pltpu.CompilerParams(
             collective_id=0, has_side_effects=True, vmem_limit_bytes=32 * 1024 * 1024

time: 46.4 us -> 45.5 us (0.981)
  Pallas kernels: 43 us -> 42.1 us
    pallas_call x1, Pallas kernels: 43 us -> 42.1 us  [on_device(): pl.pallas_call(kernel, out_shape=(jax.ShapeDtypeStruct(populations.shape,...]
where the time goes in v6:
time: 45.5 us; the launch traced here: 45.4 us
  Pallas kernels  42.1 us (93%)
  local copies, waits for them, and re-layouts  2.6 us (6%)
  between operations  0.67 us (1%)
    pallas_call x1, Pallas kernels, on_device(): pl.pallas_call(kernel, out_shape=(jax.ShapeDtypeStruct(populations.shape,...  42.1 us
    unnamed x6, local copies, waits for them, and re-layouts  1.71 us

profile of v6, /device:TPU:89, one launch (start us, length us, event | category | flops | bytes accessed | tf_op | source)
XLA Modules:
  0.0 45.4 jit_solution(13948189977923928585)
XLA Ops:
  0.6 0.0 copy-start.1
  0.6 0.0 copy-start
  0.6 1.1 %copy.5.f_in = f32[19,12,384]{2,1,0:T(8,128)S(1)} copy(f32[19,12,384]{2,0,1:T(8,128)} %param.3) | data formatting | bytes 700416 | tf_op args[0]
  1.8 0.0 copy-done.1
  1.8 0.0 copy-done
  1.8 42.1 %shard_map.50 = (f32[19,12,384]{2,1,0:T(8,128)S(1)}, f32[12,384]{1,0:T(8,128)S(1)}) custom-call(s32[4,16]{1,0:T(4,128)S(1)} %copy-done.1, f32[19,12,384]{2,1,0:T(8,128)S(1)} %copy.5.f_in, f32[12,384]{1,0:T(8,128)S(1)} %copy-done), custom_call_target="tpu_custom_call" | custom-call | tf_op jit(solution)/shard_map/pallas_call | solution.py:1049
  43.9 0.9 %copy.6 = f32[19,12,384]{2,0,1:T(8,128)} copy(f32[19,12,384]{2,1,0:T(8,128)S(1)} %get-tuple-element.2) | data formatting | bytes 700416 | tf_op jit(solution)/shard_map/pallas_call | solution.py:1049
  44.8 0.6 %copy.8 = f32[12,384]{1,0:T(8,128)} copy(f32[12,384]{1,0:T(8,128)S(1)} %get-tuple-element.7) | data formatting | bytes 36864
Async XLA Ops:
  0.6 1.1 %copy-start.1 = (s32[4,16]{1,0:T(4,128)S(1)}, s32[4,16]{1,0:T(4,128)}, u32[]{:S(2)}) copy-start(s32[4,16]{1,0:T(4,128)} %shifts.1) | copy-start | bytes 772
  0.6 1.1 %copy-start = (f32[12,384]{1,0:T(8,128)S(1)}, f32[12,384]{1,0:T(8,128)}, u32[]{:S(2)}) copy-start(f32[12,384]{1,0:T(8,128)} %p_in.1) | copy-start | bytes 55300

commit v7 on v6

--- a/solution.py
+++ b/solution.py
@@ -793,7 +793,8 @@
     advance(2)
     y_cut = (slice(256, 384), slice(0, 128))
     lines = [fx[group[0], edge:edge + 1, 0:WIDE] for edge in (11, 0) for group in x_groups]
-    halves = 0.5 * jnp.concatenate(lines + lines[:2], axis=0)
+    lines += [fx[1, 11:12, 0:WIDE], fx[2, 0:1, 0:WIDE]]
+    halves = 0.5 * jnp.concatenate(lines, axis=0)
     ahead, behind = moved_yz(halves, 0, -1, place[:8]), moved_yz(halves, 0, 1, place[:8])
     for kind in (0, 1):
         edge, second, low = ((11, 10, 9), (0, 1, 0))[kind]
@@ -821,9 +822,14 @@
     for is_plane, edge, slots in ((left_plane, 0, down_slots), (right_plane, 11, up_slots)):
         @pl.when(is_plane)
         def _(edge=edge, slots=slots):
+            at = 6 if edge == 11 else 7
             for b in range(3):
-                for i, slot in enumerate(slots):
-                    last_a[5 * b + i:5 * b + i + 1, :] = fx[slot, edge:edge + 1, b * 128:b * 128 + 128]
+                cut = slice(b * 128, b * 128 + 128)
+                for i, slot in enumerate(slots[1:]):
+                    line = fx[slot, edge:edge + 1, cut]
+                    if lattice_vel[slot][2] != 0:
+                        line = line + (ahead if lattice_vel[slot][2] == 1 else behind)[at:at + 1, cut]
+                    last_a[4 * b + i:4 * b + i + 1, :] = line
 
     send_around(2, last_a)
     send_x(2, last_x)
@@ -912,6 +918,11 @@
                     row = rows[deep_x - 1]
                     fx[slot, row:row + 1, 384:512] = line[0]
 
+    for slot in range(19):
+        step_x, step_y, step_z = lattice_vel[slot]
+        if step_x == 0:
+            fx[slot] = moved_yz(fx[slot], step_y, step_z, place4)
+
     def mixed(kind, value):
         near, far = ((0.75, 0.25), (0.25, 0.75))[kind]
         return near * value + far * rolled(value, NZ, 1)
@@ -926,8 +937,8 @@
             for j in range(count_y):
                 source = lax.rem(gy + count_y - j, count_y)
                 for b in range(3):
-                    rows = slice(5 * b, 5 * b + 5)
-                    ring_o[source * 3 + b, 0:5] = last_a[rows] if j == 0 else last["around"][j - 1, rows]
+                    rows = slice(4 * b, 4 * b + 4)
+                    ring_o[source * 3 + b, 1:5] = last_a[rows] if j == 0 else last["around"][j - 1, rows]
             for b in range(5):
                 ring_o[blocks + b] = ring_o[b]
             row = (15, 12)[kind]
@@ -951,7 +962,7 @@
                 lane1[:size] < 64, value[at:at + size, 384:512], value[at:at + size, 512:640]
             )
 
-    for slot in range(19):
+    for slot in up_slots + down_slots:
         step_x, step_y, step_z = lattice_vel[slot]
         fx[slot] = moved_yz(rolled(fx[slot], step_x, 0), step_y, step_z, place4)
     p = e_p[...]
@@ -996,7 +1007,9 @@
             sign = 1.0 - 2.0 * kind
             for tile, way in ((inner, sign), (outer, -sign)):
                 r = [tile[i:i + 1] for i in range(5)]
-                whole = r[0] + r[1] + r[2] + r[3] + r[4]
+                whole = r[1] + r[2] + r[3] + r[4]
+                if tile is inner:
+                    whole = whole + r[0]
                 found = (whole, way * whole, r[3] - r[4], way * (r[1] - r[2]))
                 total = [b if a is None else a + b for a, b in zip(total, found)]
             for i, (_, slot) in enumerate(folded_x):
@@ -1078,13 +1091,13 @@
             pltpu.VMEM((2, 57, 128), jnp.float32),
             pltpu.VMEM((2, 48, 128), jnp.float32),
             pltpu.VMEM((4, 5, 128), jnp.float32),
-            pltpu.VMEM((15, 128), jnp.float32),
+            pltpu.VMEM((12, 128), jnp.float32),
         ] + [
             pltpu.VMEM((count, rows, 128), jnp.float32)
             for count, rows in (
                 (2, 48), (2, 48), (4, 3), (parts, 48), (parts - 1, 6),
                 (2, 16), (2, 21), (4, 1), (parts, 21),
-                (2, 48), (2, 57), (4, 5), (parts, 57), (parts - 1, 15),
+                (2, 48), (2, 57), (4, 5), (parts, 57), (parts - 1, 12),
             )
         ] + [
             pltpu.SemaphoreType.DMA((rounds, 5)),

time: 45.5 us -> 45.4 us (level)
  no operation moved by 1% of the time
where the time goes in v7:
time: 45.4 us; the launch traced here: 45.3 us
  Pallas kernels  42 us (93%)
  local copies, waits for them, and re-layouts  2.6 us (6%)
  between operations  0.67 us (1%)
    pallas_call x1, Pallas kernels, on_device(): pl.pallas_call(kernel, out_shape=(jax.ShapeDtypeStruct(populations.shape,...  42 us
    unnamed x6, local copies, waits for them, and re-layouts  1.71 us

profile of v7, /device:TPU:89, one launch (start us, length us, event | category | flops | bytes accessed | tf_op | source)
XLA Modules:
  0.0 45.3 jit_solution(6233217325682060677)
XLA Ops:
  0.6 0.0 copy-start.1
  0.6 0.0 copy-start
  0.6 1.1 %copy.5.f_in = f32[19,12,384]{2,1,0:T(8,128)S(1)} copy(f32[19,12,384]{2,0,1:T(8,128)} %param.3) | data formatting | bytes 700416 | tf_op args[0]
  1.8 0.0 copy-done.1
  1.8 0.0 copy-done
  1.8 42.0 %shard_map.50 = (f32[19,12,384]{2,1,0:T(8,128)S(1)}, f32[12,384]{1,0:T(8,128)S(1)}) custom-call(s32[4,16]{1,0:T(4,128)S(1)} %copy-done.1, f32[19,12,384]{2,1,0:T(8,128)S(1)} %copy.5.f_in, f32[12,384]{1,0:T(8,128)S(1)} %copy-done), custom_call_target="tpu_custom_call" | custom-call | tf_op jit(solution)/shard_map/pallas_call | solution.py:1062
  43.8 0.9 %copy.6 = f32[19,12,384]{2,0,1:T(8,128)} copy(f32[19,12,384]{2,1,0:T(8,128)S(1)} %get-tuple-element.2) | data formatting | bytes 700416 | tf_op jit(solution)/shard_map/pallas_call | solution.py:1062
  44.7 0.6 %copy.8 = f32[12,384]{1,0:T(8,128)} copy(f32[12,384]{1,0:T(8,128)S(1)} %get-tuple-element.7) | data formatting | bytes 36864
Async XLA Ops:
  0.6 1.1 %copy-start.1 = (s32[4,16]{1,0:T(4,128)S(1)}, s32[4,16]{1,0:T(4,128)}, u32[]{:S(2)}) copy-start(s32[4,16]{1,0:T(4,128)} %shifts.1) | copy-start | bytes 772
  0.6 1.1 %copy-start = (f32[12,384]{1,0:T(8,128)S(1)}, f32[12,384]{1,0:T(8,128)}, u32[]{:S(2)}) copy-start(f32[12,384]{1,0:T(8,128)} %p_in.1) | copy-start | bytes 55300

commit v8 on v7

--- a/solution.py
+++ b/solution.py
@@ -606,11 +606,6 @@
                 out_corner[2 * kind + k, i // 5:i // 5 + 1, :] = line
     for k in (0, 1):
         cut = slice(256, 384) if k == 0 else slice(0, 128)
-        low = lane1[:12] < 64
-        if k == 0:
-            pair = lambda a, b: jnp.where(low, pltpu.roll(b, 64, 1), a)
-        else:
-            pair = lambda a, b: jnp.where(low, a, pltpu.roll(b, 64, 1))
         packed = None
         for i, slot in enumerate(plus_y if k == 0 else minus_y):
             block = f[slot, :, cut]
@@ -620,9 +615,20 @@
             else:
                 packed = jnp.where(lane1 >= i * NZ if k == 0 else lane1 < 128 - i * NZ, part, packed)
         out_y[k, 0:12, :] = packed[:12]
-        out_y[k, 12:24, :] = e_p[0:12, cut]
-        out_y[k, 24:36, :] = pair(e_r[0:12, cut], e_u[0, 0:12, cut])
-        out_y[k, 36:48, :] = pair(e_u[1, 0:12, cut], e_u[2, 0:12, cut])
+        lane12 = lane1[:12]
+        free = lane12 < 32 if k == 0 else lane12 >= 96
+        second = (lane12 >= 32) & (lane12 < 80) if k == 0 else (lane12 >= 48) & (lane12 < 96)
+        density_at, flow_at, deep_at = ((NZ, 32, 80), (96, 96, NZ))[k]
+        out_y[k, 12:24, :] = jnp.where(free, rolled(e_r[0:12, cut], density_at, 1), e_p[0:12, cut])
+        u_z = e_u[2, 0:12, cut]
+        out_y[k, 24:36, :] = jnp.where(
+            free, rolled(u_z, flow_at, 1),
+            jnp.where(second, rolled(e_u[1, 0:12, cut], -48 if k == 0 else 48, 1), e_u[0, 0:12, cut]),
+        )
+        deep = [rolled(u_z[4 * g:4 * g + 4], NZ * g - deep_at, 1) for g in range(3)]
+        out_y[k, 36:40, :] = jnp.where(
+            lane1[:4] < NZ, deep[0], jnp.where(lane1[:4] < 2 * NZ, deep[1], deep[2])
+        )
 
     @pl.when(left_plane)
     def _():
@@ -646,10 +652,17 @@
     for k in (0, 1):
         cut = slice(512, 640) if k == 0 else slice(384, 512)
         e_p[0:12, cut] = wide["y"][k, 12:24]
-        e_r[0:12, cut] = wide["y"][k, 24:36]
-        e_u[0, 0:12, cut] = pltpu.roll(wide["y"][k, 24:36], 64, 1)
-        e_u[1, 0:12, cut] = wide["y"][k, 36:48]
-        e_u[2, 0:12, cut] = pltpu.roll(wide["y"][k, 36:48], 64, 1)
+        density_at, flow_at, deep_at = ((NZ, 32, 80), (96, 96, NZ))[k]
+        flow = wide["y"][k, 24:36]
+        e_r[0:12, cut] = rolled(wide["y"][k, 12:24], -density_at, 1)
+        e_u[0, 0:12, cut] = flow
+        e_u[1, 0:12, cut] = rolled(flow, 48 if k == 0 else -48, 1)
+        e_u[2, 0:12, cut] = rolled(flow, -flow_at, 1)
+        here = (lane1[:4] >= deep_at) & (lane1[:4] < deep_at + NZ)
+        for g in range(3):
+            rows = slice(4 * g, 4 * g + 4)
+            deep = rolled(wide["y"][k, 36:40], deep_at - NZ * g, 1)
+            e_u[2, rows, cut] = jnp.where(here, deep, e_u[2, rows, cut])
     for kind, is_plane, place_of in sides:
         low = (20, 12)[kind]
         edge, second, third = ((23, 22, 21), (12, 13, 12))[kind]
@@ -1080,7 +1093,7 @@
             pltpu.VMEM((blocks + 5, 16, 128), jnp.float32),
             pltpu.VMEM((blocks + 5, 8, 128), jnp.float32),
             pltpu.VMEM((2, 48, 128), jnp.float32),
-            pltpu.VMEM((2, 48, 128), jnp.float32),
+            pltpu.VMEM((2, 40, 128), jnp.float32),
             pltpu.VMEM((4, 3, 128), jnp.float32),
             pltpu.VMEM((6, 128), jnp.float32),
             pltpu.VMEM((19, 16, 512), jnp.float32),
@@ -1095,7 +1108,7 @@
         ] + [
             pltpu.VMEM((count, rows, 128), jnp.float32)
             for count, rows in (
-                (2, 48), (2, 48), (4, 3), (parts, 48), (parts - 1, 6),
+                (2, 40), (2, 48), (4, 3), (parts, 48), (parts - 1, 6),
                 (2, 16), (2, 21), (4, 1), (parts, 21),
                 (2, 48), (2, 57), (4, 5), (parts, 57), (parts - 1, 12),
             )

time: 45.4 us -> 45.3 us (level)
  no operation moved by 1% of the time
where the time goes in v8:
time: 45.3 us; the launch traced here: 45.1 us
  Pallas kernels  41.9 us (92%)
  local copies, waits for them, and re-layouts  2.6 us (6%)
  between operations  0.67 us (1%)
    pallas_call x1, Pallas kernels, on_device(): pl.pallas_call(kernel, out_shape=(jax.ShapeDtypeStruct(populations.shape,...  41.9 us
    unnamed x6, local copies, waits for them, and re-layouts  1.71 us

profile of v8, /device:TPU:89, one launch (start us, length us, event | category | flops | bytes accessed | tf_op | source)
XLA Modules:
  0.0 45.1 jit_solution(11573426662910461935)
XLA Ops:
  0.6 0.0 copy-start.1
  0.6 0.0 copy-start
  0.6 1.1 %copy.5.f_in = f32[19,12,384]{2,1,0:T(8,128)S(1)} copy(f32[19,12,384]{2,0,1:T(8,128)} %param.3) | data formatting | bytes 700416 | tf_op args[0]
  1.8 0.0 copy-done.1
  1.8 0.0 copy-done
  1.8 41.9 %shard_map.50 = (f32[19,12,384]{2,1,0:T(8,128)S(1)}, f32[12,384]{1,0:T(8,128)S(1)}) custom-call(s32[4,16]{1,0:T(4,128)S(1)} %copy-done.1, f32[19,12,384]{2,1,0:T(8,128)S(1)} %copy.5.f_in, f32[12,384]{1,0:T(8,128)S(1)} %copy-done), custom_call_target="tpu_custom_call" | custom-call | tf_op jit(solution)/shard_map/pallas_call | solution.py:1075
  43.6 0.9 %copy.6 = f32[19,12,384]{2,0,1:T(8,128)} copy(f32[19,12,384]{2,1,0:T(8,128)S(1)} %get-tuple-element.2) | data formatting | bytes 700416 | tf_op jit(solution)/shard_map/pallas_call | solution.py:1075
  44.5 0.6 %copy.8 = f32[12,384]{1,0:T(8,128)} copy(f32[12,384]{1,0:T(8,128)S(1)} %get-tuple-element.7) | data formatting | bytes 36864
Async XLA Ops:
  0.6 1.1 %copy-start.1 = (s32[4,16]{1,0:T(4,128)S(1)}, s32[4,16]{1,0:T(4,128)}, u32[]{:S(2)}) copy-start(s32[4,16]{1,0:T(4,128)} %shifts.1) | copy-start | bytes 772
  0.6 1.1 %copy-start = (f32[12,384]{1,0:T(8,128)S(1)}, f32[12,384]{1,0:T(8,128)}, u32[]{:S(2)}) copy-start(f32[12,384]{1,0:T(8,128)} %p_in.1) | copy-start | bytes 55300

commit v9 on v8

--- a/solution.py
+++ b/solution.py
@@ -264,7 +264,9 @@
         order = [(half // 2, 1), (half // 2, 0)]
         for dx in range(half // 2 - 1, -1, -1):
             order += [(d, z) for z in (1, 0) for d in sorted({dx, (half - dx) % half})]
-        return [2 * lax.rem(gy // 2 + dx, half) + lax.rem(gy + dz, 2) for dx, dz in dict.fromkeys(order)]
+        place = lax.rem(gx, 2 * SPAN)
+        turn = jnp.where((place == 0) | (place == 2 * SPAN - 1), 1, 0)
+        return [2 * lax.rem(gy // 2 + dx, half) + lax.rem(gy + dz + turn, 2) for dx, dz in dict.fromkeys(order)]
 
     for is_plane, side in ((left_plane, below), (right_plane, above)):
         @pl.when(is_plane)

time: 45.3 us -> 45.6 us (level)
  no operation moved by 1% of the time
where the time goes in v9:
time: 45.6 us; the launch traced here: 45.5 us
  Pallas kernels  42.2 us (93%)
  local copies, waits for them, and re-layouts  2.6 us (6%)
  between operations  0.67 us (1%)
    pallas_call x1, Pallas kernels, on_device(): pl.pallas_call(kernel, out_shape=(jax.ShapeDtypeStruct(populations.shape,...  42.2 us
    unnamed x6, local copies, waits for them, and re-layouts  1.71 us

profile of v9, /device:TPU:89, one launch (start us, length us, event | category | flops | bytes accessed | tf_op | source)
XLA Modules:
  0.0 45.5 jit_solution(10844676291160603813)
XLA Ops:
  0.6 0.0 copy-start.1
  0.6 0.0 copy-start
  0.6 1.1 %copy.5.f_in = f32[19,12,384]{2,1,0:T(8,128)S(1)} copy(f32[19,12,384]{2,0,1:T(8,128)} %param.3) | data formatting | bytes 700416 | tf_op args[0]
  1.8 0.0 copy-done.1
  1.8 0.0 copy-done
  1.8 42.2 %shard_map.50 = (f32[19,12,384]{2,1,0:T(8,128)S(1)}, f32[12,384]{1,0:T(8,128)S(1)}) custom-call(s32[4,16]{1,0:T(4,128)S(1)} %copy-done.1, f32[19,12,384]{2,1,0:T(8,128)S(1)} %copy.5.f_in, f32[12,384]{1,0:T(8,128)S(1)} %copy-done), custom_call_target="tpu_custom_call" | custom-call | tf_op jit(solution)/shard_map/pallas_call | solution.py:1077
  44.0 0.9 %copy.6 = f32[19,12,384]{2,0,1:T(8,128)} copy(f32[19,12,384]{2,1,0:T(8,128)S(1)} %get-tuple-element.2) | data formatting | bytes 700416 | tf_op jit(solution)/shard_map/pallas_call | solution.py:1077
  44.8 0.6 %copy.8 = f32[12,384]{1,0:T(8,128)} copy(f32[12,384]{1,0:T(8,128)S(1)} %get-tuple-element.7) | data formatting | bytes 36864
Async XLA Ops:
  0.6 1.1 %copy-start.1 = (s32[4,16]{1,0:T(4,128)S(1)}, s32[4,16]{1,0:T(4,128)}, u32[]{:S(2)}) copy-start(s32[4,16]{1,0:T(4,128)} %shifts.1) | copy-start | bytes 772
  0.6 1.1 %copy-start = (f32[12,384]{1,0:T(8,128)S(1)}, f32[12,384]{1,0:T(8,128)}, u32[]{:S(2)}) copy-start(f32[12,384]{1,0:T(8,128)} %p_in.1) | copy-start | bytes 55300
